TPU v7x, 512 devices: a whole 4x8x8 slice. The times are simulated.
512 devices in a mesh: slab: 512 (over x, z, y, core).
Axes of the slice: x: 4, y: 8, z: 8, core: 2. Of those that a mesh axis runs over, the one named last changes fastest.
Arguments:
- skull_state: float32 [6, 4096, 4096], P(None, 'slab'), may hold values from -6 to 6
- stiffness: float32 [4096, 4096], P('slab'), may hold values from 0.15 to 0.45
- intersection_src: int32 [131072, 4], P('slab'), may hold values from 0 to 12287
- intersection_weight: float32 [131072, 4], P('slab'), may hold values from 0.05 to 1
- brain_vel: float32 [3, 1048576], P(None, 'slab'), may hold values from -6 to 6
- connectivity: int32 [8, 1048576], P(None, 'slab'), may hold values from 0 to 2303
- region: int32 [1048576], P('slab'), may hold values from 0 to 4
- shear_table: float32 [4], replicated, may hold values from 1 to 10
- bulk_table: float32 [4], replicated, may hold values from 2 to 20
- prony_weight: float32 [12, 4], replicated, may hold values from 0.05 to 0.5
- prony_tau: float32 [12], replicated, may hold values from 0.05 to 20
- prony_state: float32 [12, 6, 1048576], P(None, None, 'slab'), may hold values from -6 to 6
- node_mass: float32 [1048576], P('slab'), may hold values from 0.5 to 2
Outputs:
- skull_out: float32 [6, 4096, 4096], P(None, 'slab')
- brain_out: float32 [3, 1048576], P(None, 'slab')
- prony_out: float32 [12, 6, 1048576], P(None, None, 'slab')
Inputs may be any that keep to these rules, and one draw needn't show every extreme that they name: `intersection_src`: values are slot*4096+lane. `region`: 4 marks an empty slot.
All inputs are finite; a program needn't handle non-finite values.
Results may differ from a plain program's by a relative error of at most 0.0003.
Values sent between devices are 32-bit elements; how exact they have to be, the bound alone decides.
No kernel may reach another device: no remote copies, remote signals or barrier semaphores. Data moves between devices by JAX's collectives and lax.ppermute only.
A program may use at most 64 MiB of HBM per device.

v0:
```python
import jax
import jax.numpy as jnp
import numpy as np
from jax import lax
from jax.sharding import PartitionSpec as P

SUBSTEPS = 8
SHARED = 256


STEP_SKULL = 1.0
DAMPING = 0.05
STEP_BRAIN = 0.2
COUPLING = 0.5


def padded_2(block, sides, width):
    for axis, dim in sides:
        count = lax.axis_size(axis)
        forward = [(i, i + 1) for i in range(count - 1)]
        backward = [(target, source) for source, target in forward]
        low = lax.ppermute(
            lax.slice_in_dim(block, block.shape[dim] - width, None, axis=dim), axis, forward
        )
        high = lax.ppermute(lax.slice_in_dim(block, 0, width, axis=dim), axis, backward)
        block = jnp.concatenate([low, block, high], axis=dim)
    return block


def passed_along(block, axis, distance):
    devices = range(lax.axis_size(axis))
    route = [(i - distance, i) for i in devices if i - distance in devices]
    return lax.ppermute(block, axis, route)


def strain_table():
    table = np.zeros((6, 24), np.float32)
    for corner in range(8):
        slopes = [0.25 * ((corner >> direction & 1) * 2 - 1) for direction in range(3)]
        table[0, corner] = slopes[0]
        table[1, 8 + corner] = slopes[1]
        table[2, 16 + corner] = slopes[2]
        table[3, corner] = slopes[1]
        table[3, 8 + corner] = slopes[0]
        table[4, 8 + corner] = slopes[2]
        table[4, 16 + corner] = slopes[1]
        table[5, corner] = slopes[2]
        table[5, 16 + corner] = slopes[0]
    return jnp.asarray(table)


def advance(padded, velocity, stiffs):
    displace = padded[:, 1:-1]
    laplace = (
        padded[:, 2:]
        + padded[:, :-2]
        + jnp.roll(displace, 1, 2)
        + jnp.roll(displace, -1, 2)
        - 4.0 * displace
    )
    velocity = velocity + STEP_SKULL * (stiffs * laplace - DAMPING * velocity)
    return (displace + STEP_SKULL * velocity, velocity)


def element_forces(corners, region, shear_table, bulk_table, prony_weight, prony_tau, prony_state):
    table = strain_table()
    high = lax.Precision.HIGHEST
    rate = jnp.dot(table, corners.reshape(24, -1), precision=high)
    strain = STEP_BRAIN * rate
    trace = strain[0] + strain[1] + strain[2]
    deviator = jnp.concatenate([strain[:3] - trace[None] / 3.0, 0.5 * strain[3:]], 0)
    labels = jnp.arange(shear_table.shape[0], dtype=jnp.int32)
    onehot = (region[None, :] == labels[:, None]).astype(strain.dtype)
    shear = jnp.dot(shear_table[None], onehot, precision=high)[0]
    bulk = jnp.dot(bulk_table[None], onehot, precision=high)[0]
    weights = jnp.dot(prony_weight, onehot, precision=high)
    live = jnp.sum(onehot, 0)
    decay = jnp.exp(-STEP_BRAIN / prony_tau)
    factor = (1.0 - decay) * prony_tau / STEP_BRAIN
    memory = (
        decay[:, None, None] * prony_state
        + (2.0 * shear[None] * weights * factor[:, None])[:, None, :] * deviator[None]
    )
    stress = jnp.sum(memory, 0) + 2.0 * shear[None] * deviator
    stress = stress.at[:3].add((bulk * trace)[None])
    stress = stress * live[None]
    forces = -jnp.dot(table.T, stress, precision=high)
    return (forces.reshape(3, 8, -1), memory)


def record(layer, kept):
    kept.append(padded_2(layer[None], (("slab", 0),), 1))


def on_device(
    skull_state,
    stiffness,
    intersection_src,
    intersection_weight,
    brain_vel,
    connectivity,
    region,
    shear_table,
    bulk_table,
    prony_weight,
    prony_tau,
    prony_state,
    node_mass,
):
    layers = skull_state.shape[1]
    lanes = skull_state.shape[2]
    displace, velocity = (skull_state[:3], skull_state[3:])
    kept = []
    for substep in range(SUBSTEPS):
        padded = padded_2(displace, (("slab", 1),), 1)
        displace, velocity = advance(padded, velocity, stiffness)
        record(velocity[:, layers - 1], kept)
    history = jnp.stack(kept).transpose(0, 2, 1, 3).reshape(3 * SUBSTEPS, 3 * lanes)
    iface = intersection_src.shape[0]
    taken = history[:, intersection_src]
    normed = intersection_weight / jnp.sum(intersection_weight, 1, keepdims=True)
    moved = jnp.sum(taken * normed[None], -1).reshape(SUBSTEPS, 3, iface)
    coeffs = (jnp.arange(SUBSTEPS, dtype=jnp.float32) + 1.0) / 36.0
    target = jnp.sum(moved * coeffs[:, None, None], 0)
    nodes = brain_vel.shape[1]
    ghost = passed_along(brain_vel[:, :SHARED], "slab", -1)
    all_vel = jnp.concatenate([brain_vel, ghost], 1)
    corners = all_vel[:, connectivity]
    forces, memory = element_forces(
        corners, region, shear_table, bulk_table, prony_weight, prony_tau, prony_state
    )
    summed = (
        jnp.zeros((3, nodes + SHARED), brain_vel.dtype)
        .at[:, connectivity.reshape(-1)]
        .add(forces.reshape(3, -1))
    )
    incoming = passed_along(summed[:, nodes:], "slab", 1)
    owned = summed[:, :nodes].at[:, :SHARED].add(incoming)
    updated = brain_vel + STEP_BRAIN * owned / node_mass[None]
    updated = updated.at[:, nodes - iface :].add(
        COUPLING * (target - brain_vel[:, nodes - iface :])
    )
    skull_out = jnp.concatenate([displace, velocity], 0)
    return (skull_out, updated, memory)


def solution(mesh):
    placed = (
        P(None, "slab", None),
        P("slab", None),
        P("slab", None),
        P("slab", None),
        P(None, "slab"),
        P(None, "slab"),
        P("slab"),
        P(),
        P(),
        P(),
        P(),
        P(None, None, "slab"),
        P("slab"),
    )
    return jax.shard_map(
        on_device,
        mesh=mesh,
        in_specs=placed,
        out_specs=(P(None, "slab", None), P(None, "slab"), P(None, None, "slab")),
        check_vma=False,
    )
```

profile of v0, /device:TPU:7, one launch (start us, length us, event | category | flops | bytes accessed | tf_op | source)
XLA Modules:
  0.0 357.9 jit_solution(16869671016733139001)
XLA Ops:
  0.7 1.9 fusion.100
  2.6 2.6 collective-permute-start
  5.2 3.1 collective-permute-start.1
  9.0 12.4 %collective-permute-start.16 = (f32[3,256]{1,0:T(4,128)S(1)}, f32[3,256]{1,0:T(4,128)S(1)}, u32[]{:S(2)}, u32[]{:S(2)}) collective-permute-start(f32[3,256]{1,0:T(4,128)S(1)} %slice.399), channel_id=1, source_target_pairs={{1,0},{2,1},{3,2},{4,3},{5,4},{6,5},{7,6},{8,7},{9,8},{10,9},{11,1... | collective-permute-start | bytes 9224 | tf_op jit(solution)/shard_map/ppermute | solution.py:33
  21.4 2.1 fusion.102
  26.2 54.4 %gather_fusion = f32[16384,3]{1,0:T(8,128)} fusion(f32[3,2304]{0,1:T(8,128)S(1)} %copy.75, s32[16384]{0:T(1024)S(1)} %broadcast_clamp_fusion), kind=kCustom, calls=%fused_computation | custom fusion | bytes 458752 | tf_op jit(solution)/shard_map/gather | solution.py:128
  80.6 5.3 %copy.76 = f32[8,2048,3]{1,0,2:T(8,128)S(1)} copy(f32[8,2048,3]{2,1,0:T(8,128)} %bitcast.91) | data formatting | bytes 393216 | tf_op jit(solution)/shard_map/gather | solution.py:128
  86.3 1.1 fusion.83
  88.4 5.1 %copy.77 = f32[3,16384]{0,1:T(8,128)} copy(f32[3,16384]{1,0:T(4,128)S(1)} %reshape.163) | data formatting | bytes 393216 | tf_op jit(solution)/shard_map/reshape;reshape | solution.py:135
  93.5 80.0 %scatter_custom_fusion = f32[3,2304]{0,1:T(8,128)S(1)} fusion(s32[16384]{0:T(1024)} %bitcast.98, f32[3,16384]{0,1:T(8,128)} %copy.77, f32[]{:T(128)} %constant.107.clone.1), kind=kCustom, calls=%fused_computation.3 | custom fusion | flops 49152 | bytes 8416768 | tf_op jit(solution)/shard_map/scatter-add | solution.py:135
  173.6 1.9 collective-permute-start.17
  177.0 1.1 slice.471
  178.2 1.6 copy.85
  179.8 2.3 collective-permute-done.17
  183.5 1.2 slice_add_fusion.4
  184.9 8.5 %collective-permute-start.2 = (f32[3,1,4096]{2,1,0:T(1,128)S(1)}, f32[3,1,4096]{2,1,0:T(1,128)S(1)}, u32[]{:S(2)}, u32[]{:S(2)}) collective-permute-start(f32[3,1,4096]{2,1,0:T(1,128)S(1)} %get-tuple-element.117), channel_id=1, source_target_pairs={{1,0},{2,1},{3,2},{4,3},{5,4},{6,5},{7,6},{8,7},{9,8},{10,9},{11,1... | collective-permute-start | bytes 147464 | tf_op jit(solution)/shard_map/ppermute | solution.py:25
  193.4 1.9 collective-permute-start.3
  195.4 1.9 collective-permute-start.18
  197.3 4.9 %collective-permute-start.19 = (f32[1,3,4096]{2,0,1:T(1,128)S(1)}, f32[1,3,4096]{2,0,1:T(1,128)S(1)}, u32[]{:S(2)}, u32[]{:S(2)}) collective-permute-start(f32[1,3,4096]{2,0,1:T(1,128)S(1)} %slice_bitcast_fusion.7), channel_id=1, source_target_pairs={{1,0},{2,1},{3,2},{4,3},{5,4},{6,5},{7,6},{8,7},{9,8},{10,9},{11,1... | collective-permute-start | bytes 147464 | tf_op jit(solution)/shard_map/ppermute | solution.py:25
  202.7 1.9 collective-permute-start.20
  204.6 7.9 %collective-permute-start.21 = (f32[1,3,4096]{2,0,1:T(1,128)S(1)}, f32[1,3,4096]{2,0,1:T(1,128)S(1)}, u32[]{:S(2)}, u32[]{:S(2)}) collective-permute-start(f32[1,3,4096]{2,0,1:T(1,128)S(1)} %slice_bitcast_fusion.6), channel_id=1, source_target_pairs={{1,0},{2,1},{3,2},{4,3},{5,4},{6,5},{7,6},{8,7},{9,8},{10,9},{11,1... | collective-permute-start | bytes 147464 | tf_op jit(solution)/shard_map/ppermute | solution.py:25
  212.7 7.9 %collective-permute-start.4 = (f32[3,1,4096]{2,1,0:T(1,128)S(1)}, f32[3,1,4096]{2,1,0:T(1,128)S(1)}, u32[]{:S(2)}, u32[]{:S(2)}) collective-permute-start(f32[3,1,4096]{2,1,0:T(1,128)S(1)} %get-tuple-element.111), channel_id=1, source_target_pairs={{1,0},{2,1},{3,2},{4,3},{5,4},{6,5},{7,6},{8,7},{9,8},{10,9},{11,1... | collective-permute-start | bytes 147464 | tf_op jit(solution)/shard_map/ppermute | solution.py:25
  220.6 1.9 collective-permute-start.5
  224.1 4.2 %collective-permute-start.22 = (f32[1,3,4096]{2,0,1:T(1,128)S(1)}, f32[1,3,4096]{2,0,1:T(1,128)S(1)}, u32[]{:S(2)}, u32[]{:S(2)}) collective-permute-start(f32[1,3,4096]{2,0,1:T(1,128)S(1)} %slice_bitcast_fusion.5), channel_id=1, source_target_pairs={{0,1},{1,2},{2,3},{3,4},{4,5},{5,6},{6,7},{7,8},{8,9},{9,10},{10,1... | collective-permute-start | bytes 147464 | tf_op jit(solution)/shard_map/ppermute | solution.py:22
  228.3 6.1 %collective-permute-start.23 = (f32[1,3,4096]{2,0,1:T(1,128)S(1)}, f32[1,3,4096]{2,0,1:T(1,128)S(1)}, u32[]{:S(2)}, u32[]{:S(2)}) collective-permute-start(f32[1,3,4096]{2,0,1:T(1,128)S(1)} %slice_bitcast_fusion.5), channel_id=1, source_target_pairs={{1,0},{2,1},{3,2},{4,3},{5,4},{6,5},{7,6},{8,7},{9,8},{10,9},{11,1... | collective-permute-start | bytes 147464 | tf_op jit(solution)/shard_map/ppermute | solution.py:25
  234.7 7.9 %collective-permute-start.6 = (f32[3,1,4096]{2,1,0:T(1,128)S(1)}, f32[3,1,4096]{2,1,0:T(1,128)S(1)}, u32[]{:S(2)}, u32[]{:S(2)}) collective-permute-start(f32[3,1,4096]{2,1,0:T(1,128)S(1)} %get-tuple-element.105), channel_id=1, source_target_pairs={{1,0},{2,1},{3,2},{4,3},{5,4},{6,5},{7,6},{8,7},{9,8},{10,9},{11,1... | collective-permute-start | bytes 147464 | tf_op jit(solution)/shard_map/ppermute | solution.py:25
  242.6 1.9 collective-permute-start.7
  246.1 4.2 %collective-permute-start.24 = (f32[1,3,4096]{2,0,1:T(1,128)S(1)}, f32[1,3,4096]{2,0,1:T(1,128)S(1)}, u32[]{:S(2)}, u32[]{:S(2)}) collective-permute-start(f32[1,3,4096]{2,0,1:T(1,128)S(1)} %slice_bitcast_fusion.4), channel_id=1, source_target_pairs={{0,1},{1,2},{2,3},{3,4},{4,5},{5,6},{6,7},{7,8},{8,9},{9,10},{10,1... | collective-permute-start | bytes 147464 | tf_op jit(solution)/shard_map/ppermute | solution.py:22
  250.3 6.1 %collective-permute-start.25 = (f32[1,3,4096]{2,0,1:T(1,128)S(1)}, f32[1,3,4096]{2,0,1:T(1,128)S(1)}, u32[]{:S(2)}, u32[]{:S(2)}) collective-permute-start(f32[1,3,4096]{2,0,1:T(1,128)S(1)} %slice_bitcast_fusion.4), channel_id=1, source_target_pairs={{1,0},{2,1},{3,2},{4,3},{5,4},{6,5},{7,6},{8,7},{9,8},{10,9},{11,1... | collective-permute-start | bytes 147464 | tf_op jit(solution)/shard_map/ppermute | solution.py:25
  256.7 7.9 %collective-permute-start.8 = (f32[3,1,4096]{2,1,0:T(1,128)S(1)}, f32[3,1,4096]{2,1,0:T(1,128)S(1)}, u32[]{:S(2)}, u32[]{:S(2)}) collective-permute-start(f32[3,1,4096]{2,1,0:T(1,128)S(1)} %get-tuple-element.99), channel_id=1, source_target_pairs={{1,0},{2,1},{3,2},{4,3},{5,4},{6,5},{7,6},{8,7},{9,8},{10,9},{11,1... | collective-permute-start | bytes 147464 | tf_op jit(solution)/shard_map/ppermute | solution.py:25
  264.6 1.9 collective-permute-start.9
  268.1 4.2 %collective-permute-start.26 = (f32[1,3,4096]{2,0,1:T(1,128)S(1)}, f32[1,3,4096]{2,0,1:T(1,128)S(1)}, u32[]{:S(2)}, u32[]{:S(2)}) collective-permute-start(f32[1,3,4096]{2,0,1:T(1,128)S(1)} %slice_bitcast_fusion.3), channel_id=1, source_target_pairs={{0,1},{1,2},{2,3},{3,4},{4,5},{5,6},{6,7},{7,8},{8,9},{9,10},{10,1... | collective-permute-start | bytes 147464 | tf_op jit(solution)/shard_map/ppermute | solution.py:22
  272.3 6.1 %collective-permute-start.27 = (f32[1,3,4096]{2,0,1:T(1,128)S(1)}, f32[1,3,4096]{2,0,1:T(1,128)S(1)}, u32[]{:S(2)}, u32[]{:S(2)}) collective-permute-start(f32[1,3,4096]{2,0,1:T(1,128)S(1)} %slice_bitcast_fusion.3), channel_id=1, source_target_pairs={{1,0},{2,1},{3,2},{4,3},{5,4},{6,5},{7,6},{8,7},{9,8},{10,9},{11,1... | collective-permute-start | bytes 147464 | tf_op jit(solution)/shard_map/ppermute | solution.py:25
  278.7 7.9 %collective-permute-start.10 = (f32[3,1,4096]{2,1,0:T(1,128)S(1)}, f32[3,1,4096]{2,1,0:T(1,128)S(1)}, u32[]{:S(2)}, u32[]{:S(2)}) collective-permute-start(f32[3,1,4096]{2,1,0:T(1,128)S(1)} %get-tuple-element.93), channel_id=1, source_target_pairs={{1,0},{2,1},{3,2},{4,3},{5,4},{6,5},{7,6},{8,7},{9,8},{10,9},{11,1... | collective-permute-start | bytes 147464 | tf_op jit(solution)/shard_map/ppermute | solution.py:25
  286.5 1.9 collective-permute-start.11
  290.0 4.2 %collective-permute-start.28 = (f32[1,3,4096]{2,0,1:T(1,128)S(1)}, f32[1,3,4096]{2,0,1:T(1,128)S(1)}, u32[]{:S(2)}, u32[]{:S(2)}) collective-permute-start(f32[1,3,4096]{2,0,1:T(1,128)S(1)} %slice_bitcast_fusion.2), channel_id=1, source_target_pairs={{0,1},{1,2},{2,3},{3,4},{4,5},{5,6},{6,7},{7,8},{8,9},{9,10},{10,1... | collective-permute-start | bytes 147464 | tf_op jit(solution)/shard_map/ppermute | solution.py:22
  294.2 6.1 %collective-permute-start.29 = (f32[1,3,4096]{2,0,1:T(1,128)S(1)}, f32[1,3,4096]{2,0,1:T(1,128)S(1)}, u32[]{:S(2)}, u32[]{:S(2)}) collective-permute-start(f32[1,3,4096]{2,0,1:T(1,128)S(1)} %slice_bitcast_fusion.2), channel_id=1, source_target_pairs={{1,0},{2,1},{3,2},{4,3},{5,4},{6,5},{7,6},{8,7},{9,8},{10,9},{11,1... | collective-permute-start | bytes 147464 | tf_op jit(solution)/shard_map/ppermute | solution.py:25
  300.6 7.9 %collective-permute-start.12 = (f32[3,1,4096]{2,1,0:T(1,128)S(1)}, f32[3,1,4096]{2,1,0:T(1,128)S(1)}, u32[]{:S(2)}, u32[]{:S(2)}) collective-permute-start(f32[3,1,4096]{2,1,0:T(1,128)S(1)} %get-tuple-element.87), channel_id=1, source_target_pairs={{1,0},{2,1},{3,2},{4,3},{5,4},{6,5},{7,6},{8,7},{9,8},{10,9},{11,1... | collective-permute-start | bytes 147464 | tf_op jit(solution)/shard_map/ppermute | solution.py:25
  308.5 2.1 collective-permute-start.13
  312.0 4.2 %collective-permute-start.30 = (f32[1,3,4096]{2,0,1:T(1,128)S(1)}, f32[1,3,4096]{2,0,1:T(1,128)S(1)}, u32[]{:S(2)}, u32[]{:S(2)}) collective-permute-start(f32[1,3,4096]{2,0,1:T(1,128)S(1)} %slice_bitcast_fusion.1), channel_id=1, source_target_pairs={{0,1},{1,2},{2,3},{3,4},{4,5},{5,6},{6,7},{7,8},{8,9},{9,10},{10,1... | collective-permute-start | bytes 147464 | tf_op jit(solution)/shard_map/ppermute | solution.py:22
  316.2 6.1 %collective-permute-start.31 = (f32[1,3,4096]{2,0,1:T(1,128)S(1)}, f32[1,3,4096]{2,0,1:T(1,128)S(1)}, u32[]{:S(2)}, u32[]{:S(2)}) collective-permute-start(f32[1,3,4096]{2,0,1:T(1,128)S(1)} %slice_bitcast_fusion.1), channel_id=1, source_target_pairs={{1,0},{2,1},{3,2},{4,3},{5,4},{6,5},{7,6},{8,7},{9,8},{10,9},{11,1... | collective-permute-start | bytes 147464 | tf_op jit(solution)/shard_map/ppermute | solution.py:25
  322.6 7.9 %collective-permute-start.14 = (f32[3,1,4096]{2,1,0:T(1,128)S(1)}, f32[3,1,4096]{2,1,0:T(1,128)S(1)}, u32[]{:S(2)}, u32[]{:S(2)}) collective-permute-start(f32[3,1,4096]{2,1,0:T(1,128)S(1)} %get-tuple-element.81), channel_id=1, source_target_pairs={{1,0},{2,1},{3,2},{4,3},{5,4},{6,5},{7,6},{8,7},{9,8},{10,9},{11,1... | collective-permute-start | bytes 147464 | tf_op jit(solution)/shard_map/ppermute | solution.py:25
  330.5 1.9 collective-permute-start.15
  334.0 4.2 %collective-permute-start.32 = (f32[1,3,4096]{2,0,1:T(1,128)S(1)}, f32[1,3,4096]{2,0,1:T(1,128)S(1)}, u32[]{:S(2)}, u32[]{:S(2)}) collective-permute-start(f32[1,3,4096]{2,0,1:T(1,128)S(1)} %slice_bitcast_fusion), channel_id=1, source_target_pairs={{0,1},{1,2},{2,3},{3,4},{4,5},{5,6},{6,7},{7,8},{8,9},{9,10},{10,1... | collective-permute-start | bytes 147464 | tf_op jit(solution)/shard_map/ppermute | solution.py:22
  338.2 6.1 %collective-permute-start.33 = (f32[1,3,4096]{2,0,1:T(1,128)S(1)}, f32[1,3,4096]{2,0,1:T(1,128)S(1)}, u32[]{:S(2)}, u32[]{:S(2)}) collective-permute-start(f32[1,3,4096]{2,0,1:T(1,128)S(1)} %slice_bitcast_fusion), channel_id=1, source_target_pairs={{1,0},{2,1},{3,2},{4,3},{5,4},{6,5},{7,6},{8,7},{9,8},{10,9},{11,1... | collective-permute-start | bytes 147464 | tf_op jit(solution)/shard_map/ppermute | solution.py:25
  346.3 4.0 %copy.82 = f32[24,12288]{0,1:T(8,128)} copy(f32[24,12288]{1,0:T(8,128)S(1)} %bitcast.92) | data formatting | bytes 2359296 | tf_op jit(solution)/shard_map/reshape | solution.py:118
  350.3 5.6 %gather_fusion.1 = f32[1024,24]{1,0:T(8,128)S(1)} fusion(f32[24,12288]{0,1:T(8,128)} %copy.82, s32[1024]{0:T(1024)S(1)} %broadcast_clamp_fusion.1), kind=kCustom, calls=%fused_computation.1 | custom fusion | bytes 200704 | tf_op jit(solution)/shard_map/gather | solution.py:120
  356.6 1.3 fusion.80
  (161 shorter events, 21.4 us)
Async XLA Ops:
  0.6 24.9 %copy-start = (f32[12,4]{0,1:T(4,128)S(1)}, f32[12,4]{0,1:T(4,128)}, u32[]{:S(2)}) copy-start(f32[12,4]{0,1:T(4,128)} %param.29) | copy-start | bytes 580
  0.6 22.8 %copy-start.2 = (f32[6,8,4096]{2,1,0:T(8,128)S(1)}, f32[6,8,4096]{2,1,0:T(8,128)}, u32[]{:S(2)}) copy-start(f32[6,8,4096]{2,1,0:T(8,128)} %param.20) | copy-start | bytes 2359300
  0.7 25.2 %copy-start.7 = (f32[3,2048]{1,0:T(4,128)S(1)}, f32[3,2048]{1,0:T(4,128)}, u32[]{:S(2)}) copy-start(f32[3,2048]{1,0:T(4,128)} %param.24) | copy-start | bytes 73732
  0.7 23.4 %copy-start.15 = (s32[256,4]{0,1:T(4,128)S(1)}, s32[256,4]{0,1:T(4,128)}, u32[]{:S(2)}) copy-start(s32[256,4]{0,1:T(4,128)} %param.22) | copy-start | bytes 12292
  0.7 23.7 %copy-start.13 = (f32[256,4]{0,1:T(4,128)S(1)}, f32[256,4]{0,1:T(4,128)}, u32[]{:S(2)}) copy-start(f32[256,4]{0,1:T(4,128)} %param.23) | copy-start | bytes 12292
  0.7 23.8 %copy-start.6 = (s32[8,2048]{1,0:T(8,128)S(1)}, s32[8,2048]{1,0:T(8,128)}, u32[]{:S(2)}) copy-start(s32[8,2048]{1,0:T(8,128)} %param.25) | copy-start | bytes 196612
  0.7 23.8 %copy-start.11 = (s32[2048]{0:T(1024)S(1)}, s32[2048]{0:T(1024)}, u32[]{:S(2)}) copy-start(s32[2048]{0:T(1024)} %param.26) | copy-start | bytes 24580
  0.7 23.8 %copy-start.16 = (f32[4]{0:T(128)S(1)}, f32[4]{0:T(128)}, u32[]{:S(2)}) copy-start(f32[4]{0:T(128)} %param.27) | copy-start | bytes 52
  0.7 24.0 %copy-start.17 = (f32[12]{0:T(128)S(1)}, f32[12]{0:T(128)}, u32[]{:S(2)}) copy-start(f32[12]{0:T(128)} %param.30) | copy-start | bytes 148
  2.6 180.8 %collective-permute-start = (f32[3,1,4096]{2,1,0:T(1,128)}, f32[3,1,4096]{2,1,0:T(1,128)}, u32[]{:S(2)}, u32[]{:S(2)}) collective-permute-start(f32[3,1,4096]{2,1,0:T(1,128)} %get-tuple-element.75), channel_id=1, source_target_pairs={{1,0},{2,1},{3,2},{4,3},{5,4},{6,5},{7,6},{8,7},{9,8},{10,9},{11,1... | collective-permute-start | bytes 147464 | tf_op jit(solution)/shard_map/ppermute | solution.py:25
  5.2 178.2 %collective-permute-start.1 = (f32[3,1,4096]{2,1,0:T(1,128)}, f32[3,1,4096]{2,1,0:T(1,128)}, u32[]{:S(2)}, u32[]{:S(2)}) collective-permute-start(f32[3,1,4096]{2,1,0:T(1,128)} %get-tuple-element.76), channel_id=1, source_target_pairs={{0,1},{1,2},{2,3},{3,4},{4,5},{5,6},{6,7},{7,8},{8,9},{9,10},{10,1... | collective-permute-start | bytes 147464 | tf_op jit(solution)/shard_map/ppermute | solution.py:22
  9.0 16.8 %collective-permute-start.16 = (f32[3,256]{1,0:T(4,128)S(1)}, f32[3,256]{1,0:T(4,128)S(1)}, u32[]{:S(2)}, u32[]{:S(2)}) collective-permute-start(f32[3,256]{1,0:T(4,128)S(1)} %slice.399), channel_id=1, source_target_pairs={{1,0},{2,1},{3,2},{4,3},{5,4},{6,5},{7,6},{8,7},{9,8},{10,9},{11,1... | collective-permute-start | bytes 9224 | tf_op jit(solution)/shard_map/ppermute | solution.py:33
  173.6 8.5 %collective-permute-start.17 = (f32[3,256]{1,0:T(4,128)S(1)}, f32[3,256]{1,0:T(4,128)S(1)}, u32[]{:S(2)}, u32[]{:S(2)}) collective-permute-start(f32[3,256]{1,0:T(4,128)S(1)} %copy.87), channel_id=1, source_target_pairs={{0,1},{1,2},{2,3},{3,4},{4,5},{5,6},{6,7},{7,8},{8,9},{9,10},{10,1... | collective-permute-start | bytes 9224 | tf_op jit(solution)/shard_map/ppermute | solution.py:33
  177.0 5.8 %copy-start.14 = (f32[2048]{0:T(1024)S(1)}, f32[2048]{0:T(1024)}, u32[]{:S(2)}) copy-start(f32[2048]{0:T(1024)} %param.32) | copy-start | bytes 24580
  177.0 6.5 %copy-start.1 = (f32[8,4096]{1,0:T(8,128)S(1)}, f32[8,4096]{1,0:T(8,128)}, u32[]{:S(2)}) copy-start(f32[8,4096]{1,0:T(8,128)} %param.21) | copy-start | bytes 393220
  177.0 6.5 %slice-start = ((f32[6,8,4096]{2,1,0:T(8,128)}), f32[3,8,4096]{2,1,0:T(8,128)S(1)}, s32[]{:S(2)}) async-start(f32[6,8,4096]{2,1,0:T(8,128)} %param.20), calls=%async_computation | async-start | bytes 786432 | tf_op jit(solution)/shard_map/slice | solution.py:112
  177.0 6.5 %copy-start.9 = (f32[3,8,1]{2,1,0:T(8,128)S(1)}, f32[3,8,1]{2,1,0:T(8,128)}, u32[]{:S(2)}) copy-start(f32[3,8,1]{2,1,0:T(8,128)} %get-tuple-element.77) | copy-start | bytes 292
  177.0 6.5 %copy-start.10 = (f32[3,8,1]{2,1,0:T(8,128)S(1)}, f32[3,8,1]{2,1,0:T(8,128)}, u32[]{:S(2)}) copy-start(f32[3,8,1]{2,1,0:T(8,128)} %get-tuple-element.78) | copy-start | bytes 292
  184.9 17.4 %collective-permute-start.2 = (f32[3,1,4096]{2,1,0:T(1,128)S(1)}, f32[3,1,4096]{2,1,0:T(1,128)S(1)}, u32[]{:S(2)}, u32[]{:S(2)}) collective-permute-start(f32[3,1,4096]{2,1,0:T(1,128)S(1)} %get-tuple-element.117), channel_id=1, source_target_pairs={{1,0},{2,1},{3,2},{4,3},{5,4},{6,5},{7,6},{8,7},{9,8},{10,9},{11,1... | collective-permute-start | bytes 147464 | tf_op jit(solution)/shard_map/ppermute | solution.py:25
  193.4 8.9 %collective-permute-start.3 = (f32[3,1,4096]{2,1,0:T(1,128)S(1)}, f32[3,1,4096]{2,1,0:T(1,128)S(1)}, u32[]{:S(2)}, u32[]{:S(2)}) collective-permute-start(f32[3,1,4096]{2,1,0:T(1,128)S(1)} %get-tuple-element.118), channel_id=1, source_target_pairs={{0,1},{1,2},{2,3},{3,4},{4,5},{5,6},{6,7},{7,8},{8,9},{9,10},{10,1... | collective-permute-start | bytes 147464 | tf_op jit(solution)/shard_map/ppermute | solution.py:22
  195.4 25.2 %collective-permute-start.18 = (f32[1,3,4096]{2,0,1:T(1,128)S(1)}, f32[1,3,4096]{2,0,1:T(1,128)S(1)}, u32[]{:S(2)}, u32[]{:S(2)}) collective-permute-start(f32[1,3,4096]{2,0,1:T(1,128)S(1)} %slice_bitcast_fusion.7), channel_id=1, source_target_pairs={{0,1},{1,2},{2,3},{3,4},{4,5},{5,6},{6,7},{7,8},{8,9},{9,10},{10,1... | collective-permute-start | bytes 147464 | tf_op jit(solution)/shard_map/ppermute | solution.py:22
  197.3 25.2 %collective-permute-start.19 = (f32[1,3,4096]{2,0,1:T(1,128)S(1)}, f32[1,3,4096]{2,0,1:T(1,128)S(1)}, u32[]{:S(2)}, u32[]{:S(2)}) collective-permute-start(f32[1,3,4096]{2,0,1:T(1,128)S(1)} %slice_bitcast_fusion.7), channel_id=1, source_target_pairs={{1,0},{2,1},{3,2},{4,3},{5,4},{6,5},{7,6},{8,7},{9,8},{10,9},{11,1... | collective-permute-start | bytes 147464 | tf_op jit(solution)/shard_map/ppermute | solution.py:25
  202.7 39.9 %collective-permute-start.20 = (f32[1,3,4096]{2,0,1:T(1,128)S(1)}, f32[1,3,4096]{2,0,1:T(1,128)S(1)}, u32[]{:S(2)}, u32[]{:S(2)}) collective-permute-start(f32[1,3,4096]{2,0,1:T(1,128)S(1)} %slice_bitcast_fusion.6), channel_id=1, source_target_pairs={{0,1},{1,2},{2,3},{3,4},{4,5},{5,6},{6,7},{7,8},{8,9},{9,10},{10,1... | collective-permute-start | bytes 147464 | tf_op jit(solution)/shard_map/ppermute | solution.py:22
  204.6 39.9 %collective-permute-start.21 = (f32[1,3,4096]{2,0,1:T(1,128)S(1)}, f32[1,3,4096]{2,0,1:T(1,128)S(1)}, u32[]{:S(2)}, u32[]{:S(2)}) collective-permute-start(f32[1,3,4096]{2,0,1:T(1,128)S(1)} %slice_bitcast_fusion.6), channel_id=1, source_target_pairs={{1,0},{2,1},{3,2},{4,3},{5,4},{6,5},{7,6},{8,7},{9,8},{10,9},{11,1... | collective-permute-start | bytes 147464 | tf_op jit(solution)/shard_map/ppermute | solution.py:25
  212.7 10.0 %collective-permute-start.4 = (f32[3,1,4096]{2,1,0:T(1,128)S(1)}, f32[3,1,4096]{2,1,0:T(1,128)S(1)}, u32[]{:S(2)}, u32[]{:S(2)}) collective-permute-start(f32[3,1,4096]{2,1,0:T(1,128)S(1)} %get-tuple-element.111), channel_id=1, source_target_pairs={{1,0},{2,1},{3,2},{4,3},{5,4},{6,5},{7,6},{8,7},{9,8},{10,9},{11,1... | collective-permute-start | bytes 147464 | tf_op jit(solution)/shard_map/ppermute | solution.py:25
  220.6 3.1 collective-permute-start.5
  224.1 40.5 %collective-permute-start.22 = (f32[1,3,4096]{2,0,1:T(1,128)S(1)}, f32[1,3,4096]{2,0,1:T(1,128)S(1)}, u32[]{:S(2)}, u32[]{:S(2)}) collective-permute-start(f32[1,3,4096]{2,0,1:T(1,128)S(1)} %slice_bitcast_fusion.5), channel_id=1, source_target_pairs={{0,1},{1,2},{2,3},{3,4},{4,5},{5,6},{6,7},{7,8},{8,9},{9,10},{10,1... | collective-permute-start | bytes 147464 | tf_op jit(solution)/shard_map/ppermute | solution.py:22
  228.3 38.2 %collective-permute-start.23 = (f32[1,3,4096]{2,0,1:T(1,128)S(1)}, f32[1,3,4096]{2,0,1:T(1,128)S(1)}, u32[]{:S(2)}, u32[]{:S(2)}) collective-permute-start(f32[1,3,4096]{2,0,1:T(1,128)S(1)} %slice_bitcast_fusion.5), channel_id=1, source_target_pairs={{1,0},{2,1},{3,2},{4,3},{5,4},{6,5},{7,6},{8,7},{9,8},{10,9},{11,1... | collective-permute-start | bytes 147464 | tf_op jit(solution)/shard_map/ppermute | solution.py:25
  234.7 10.0 %collective-permute-start.6 = (f32[3,1,4096]{2,1,0:T(1,128)S(1)}, f32[3,1,4096]{2,1,0:T(1,128)S(1)}, u32[]{:S(2)}, u32[]{:S(2)}) collective-permute-start(f32[3,1,4096]{2,1,0:T(1,128)S(1)} %get-tuple-element.105), channel_id=1, source_target_pairs={{1,0},{2,1},{3,2},{4,3},{5,4},{6,5},{7,6},{8,7},{9,8},{10,9},{11,1... | collective-permute-start | bytes 147464 | tf_op jit(solution)/shard_map/ppermute | solution.py:25
  242.6 3.1 collective-permute-start.7
  246.1 40.5 %collective-permute-start.24 = (f32[1,3,4096]{2,0,1:T(1,128)S(1)}, f32[1,3,4096]{2,0,1:T(1,128)S(1)}, u32[]{:S(2)}, u32[]{:S(2)}) collective-permute-start(f32[1,3,4096]{2,0,1:T(1,128)S(1)} %slice_bitcast_fusion.4), channel_id=1, source_target_pairs={{0,1},{1,2},{2,3},{3,4},{4,5},{5,6},{6,7},{7,8},{8,9},{9,10},{10,1... | collective-permute-start | bytes 147464 | tf_op jit(solution)/shard_map/ppermute | solution.py:22
  250.3 38.2 %collective-permute-start.25 = (f32[1,3,4096]{2,0,1:T(1,128)S(1)}, f32[1,3,4096]{2,0,1:T(1,128)S(1)}, u32[]{:S(2)}, u32[]{:S(2)}) collective-permute-start(f32[1,3,4096]{2,0,1:T(1,128)S(1)} %slice_bitcast_fusion.4), channel_id=1, source_target_pairs={{1,0},{2,1},{3,2},{4,3},{5,4},{6,5},{7,6},{8,7},{9,8},{10,9},{11,1... | collective-permute-start | bytes 147464 | tf_op jit(solution)/shard_map/ppermute | solution.py:25
  256.7 10.0 %collective-permute-start.8 = (f32[3,1,4096]{2,1,0:T(1,128)S(1)}, f32[3,1,4096]{2,1,0:T(1,128)S(1)}, u32[]{:S(2)}, u32[]{:S(2)}) collective-permute-start(f32[3,1,4096]{2,1,0:T(1,128)S(1)} %get-tuple-element.99), channel_id=1, source_target_pairs={{1,0},{2,1},{3,2},{4,3},{5,4},{6,5},{7,6},{8,7},{9,8},{10,9},{11,1... | collective-permute-start | bytes 147464 | tf_op jit(solution)/shard_map/ppermute | solution.py:25
  264.6 3.1 collective-permute-start.9
  268.1 40.5 %collective-permute-start.26 = (f32[1,3,4096]{2,0,1:T(1,128)S(1)}, f32[1,3,4096]{2,0,1:T(1,128)S(1)}, u32[]{:S(2)}, u32[]{:S(2)}) collective-permute-start(f32[1,3,4096]{2,0,1:T(1,128)S(1)} %slice_bitcast_fusion.3), channel_id=1, source_target_pairs={{0,1},{1,2},{2,3},{3,4},{4,5},{5,6},{6,7},{7,8},{8,9},{9,10},{10,1... | collective-permute-start | bytes 147464 | tf_op jit(solution)/shard_map/ppermute | solution.py:22
  272.3 38.4 %collective-permute-start.27 = (f32[1,3,4096]{2,0,1:T(1,128)S(1)}, f32[1,3,4096]{2,0,1:T(1,128)S(1)}, u32[]{:S(2)}, u32[]{:S(2)}) collective-permute-start(f32[1,3,4096]{2,0,1:T(1,128)S(1)} %slice_bitcast_fusion.3), channel_id=1, source_target_pairs={{1,0},{2,1},{3,2},{4,3},{5,4},{6,5},{7,6},{8,7},{9,8},{10,9},{11,1... | collective-permute-start | bytes 147464 | tf_op jit(solution)/shard_map/ppermute | solution.py:25
  278.7 10.0 %collective-permute-start.10 = (f32[3,1,4096]{2,1,0:T(1,128)S(1)}, f32[3,1,4096]{2,1,0:T(1,128)S(1)}, u32[]{:S(2)}, u32[]{:S(2)}) collective-permute-start(f32[3,1,4096]{2,1,0:T(1,128)S(1)} %get-tuple-element.93), channel_id=1, source_target_pairs={{1,0},{2,1},{3,2},{4,3},{5,4},{6,5},{7,6},{8,7},{9,8},{10,9},{11,1... | collective-permute-start | bytes 147464 | tf_op jit(solution)/shard_map/ppermute | solution.py:25
  286.5 3.1 collective-permute-start.11
  290.0 40.5 %collective-permute-start.28 = (f32[1,3,4096]{2,0,1:T(1,128)S(1)}, f32[1,3,4096]{2,0,1:T(1,128)S(1)}, u32[]{:S(2)}, u32[]{:S(2)}) collective-permute-start(f32[1,3,4096]{2,0,1:T(1,128)S(1)} %slice_bitcast_fusion.2), channel_id=1, source_target_pairs={{0,1},{1,2},{2,3},{3,4},{4,5},{5,6},{6,7},{7,8},{8,9},{9,10},{10,1... | collective-permute-start | bytes 147464 | tf_op jit(solution)/shard_map/ppermute | solution.py:22
  294.2 38.2 %collective-permute-start.29 = (f32[1,3,4096]{2,0,1:T(1,128)S(1)}, f32[1,3,4096]{2,0,1:T(1,128)S(1)}, u32[]{:S(2)}, u32[]{:S(2)}) collective-permute-start(f32[1,3,4096]{2,0,1:T(1,128)S(1)} %slice_bitcast_fusion.2), channel_id=1, source_target_pairs={{1,0},{2,1},{3,2},{4,3},{5,4},{6,5},{7,6},{8,7},{9,8},{10,9},{11,1... | collective-permute-start | bytes 147464 | tf_op jit(solution)/shard_map/ppermute | solution.py:25
  300.6 10.2 %collective-permute-start.12 = (f32[3,1,4096]{2,1,0:T(1,128)S(1)}, f32[3,1,4096]{2,1,0:T(1,128)S(1)}, u32[]{:S(2)}, u32[]{:S(2)}) collective-permute-start(f32[3,1,4096]{2,1,0:T(1,128)S(1)} %get-tuple-element.87), channel_id=1, source_target_pairs={{1,0},{2,1},{3,2},{4,3},{5,4},{6,5},{7,6},{8,7},{9,8},{10,9},{11,1... | collective-permute-start | bytes 147464 | tf_op jit(solution)/shard_map/ppermute | solution.py:25
  308.5 3.1 collective-permute-start.13
  312.0 33.3 %collective-permute-start.30 = (f32[1,3,4096]{2,0,1:T(1,128)S(1)}, f32[1,3,4096]{2,0,1:T(1,128)S(1)}, u32[]{:S(2)}, u32[]{:S(2)}) collective-permute-start(f32[1,3,4096]{2,0,1:T(1,128)S(1)} %slice_bitcast_fusion.1), channel_id=1, source_target_pairs={{0,1},{1,2},{2,3},{3,4},{4,5},{5,6},{6,7},{7,8},{8,9},{9,10},{10,1... | collective-permute-start | bytes 147464 | tf_op jit(solution)/shard_map/ppermute | solution.py:22
  316.2 29.1 %collective-permute-start.31 = (f32[1,3,4096]{2,0,1:T(1,128)S(1)}, f32[1,3,4096]{2,0,1:T(1,128)S(1)}, u32[]{:S(2)}, u32[]{:S(2)}) collective-permute-start(f32[1,3,4096]{2,0,1:T(1,128)S(1)} %slice_bitcast_fusion.1), channel_id=1, source_target_pairs={{1,0},{2,1},{3,2},{4,3},{5,4},{6,5},{7,6},{8,7},{9,8},{10,9},{11,1... | collective-permute-start | bytes 147464 | tf_op jit(solution)/shard_map/ppermute | solution.py:25
  322.6 10.0 %collective-permute-start.14 = (f32[3,1,4096]{2,1,0:T(1,128)S(1)}, f32[3,1,4096]{2,1,0:T(1,128)S(1)}, u32[]{:S(2)}, u32[]{:S(2)}) collective-permute-start(f32[3,1,4096]{2,1,0:T(1,128)S(1)} %get-tuple-element.81), channel_id=1, source_target_pairs={{1,0},{2,1},{3,2},{4,3},{5,4},{6,5},{7,6},{8,7},{9,8},{10,9},{11,1... | collective-permute-start | bytes 147464 | tf_op jit(solution)/shard_map/ppermute | solution.py:25
  330.5 3.1 collective-permute-start.15
  334.0 11.5 %collective-permute-start.32 = (f32[1,3,4096]{2,0,1:T(1,128)S(1)}, f32[1,3,4096]{2,0,1:T(1,128)S(1)}, u32[]{:S(2)}, u32[]{:S(2)}) collective-permute-start(f32[1,3,4096]{2,0,1:T(1,128)S(1)} %slice_bitcast_fusion), channel_id=1, source_target_pairs={{0,1},{1,2},{2,3},{3,4},{4,5},{5,6},{6,7},{7,8},{8,9},{9,10},{10,1... | collective-permute-start | bytes 147464 | tf_op jit(solution)/shard_map/ppermute | solution.py:22
  338.2 7.3 %collective-permute-start.33 = (f32[1,3,4096]{2,0,1:T(1,128)S(1)}, f32[1,3,4096]{2,0,1:T(1,128)S(1)}, u32[]{:S(2)}, u32[]{:S(2)}) collective-permute-start(f32[1,3,4096]{2,0,1:T(1,128)S(1)} %slice_bitcast_fusion), channel_id=1, source_target_pairs={{1,0},{2,1},{3,2},{4,3},{5,4},{6,5},{7,6},{8,7},{9,8},{10,9},{11,1... | collective-permute-start | bytes 147464 | tf_op jit(solution)/shard_map/ppermute | solution.py:25
  (6 other events, 29.2 us)
where the time goes:
time: 365 us; the launch traced here: 358 us
  starting transfers between devices  168 us (46%)
  other arithmetic  91.2 us (25%)
  local copies, waits for them, and re-layouts  88 us (24%)
  waiting for transfers between devices  7.98 us (2%)
    ppermute x16, starting transfers between devices, padded_2(): lax.ppermute(lax.slice_in_dim(block, 0, width, axis=dim), axis, backward)  108 us
    scatter-add x1, other arithmetic, on_device(): summed = jnp.zeros((3, nodes + SHARED), brain_vel.dtype).at[:, connectivi...  80 us
    gather x2, local copies, waits for them, and re-layouts, on_device(): corners = all_vel[:, connectivity]  59.7 us
    ppermute x16, starting transfers between devices, padded_2(): lax.ppermute(lax.slice_in_dim(block, block.shape[dim] - width, None, axis...  45.8 us
    ppermute x2, starting transfers between devices, passed_along(): return lax.ppermute(block, axis, route)  14.3 us
  transfers between devices with their start and end apart: 34, of which 7 were waited for; matrix products, arithmetic and copies ran while one was open for 46% of the time, Pallas kernels for 0%

commit v1 on v0

v1 whole, which is shorter than its diff:
```python
import jax
import jax.numpy as jnp
import numpy as np
from jax import lax
from jax.experimental import pallas as pl
from jax.experimental.pallas import tpu as pltpu
from jax.sharding import PartitionSpec as P

SUBSTEPS = 8
SHARED = 256
STEP_BRAIN = 0.2
DAMPING = 0.05
COUPLING = 0.5
EDGE = 128
DEEP = 24
GROUP = 8
LO = 256
HI = 16


def strain_rows():
    table = np.zeros((16, 32), np.float32)
    for corner in range(8):
        slopes = [0.25 * ((corner >> direction & 1) * 2 - 1) for direction in range(3)]
        table[0, corner] = slopes[0]
        table[1, 8 + corner] = slopes[1]
        table[2, 16 + corner] = slopes[2]
        table[3, corner] = slopes[1]
        table[3, 8 + corner] = slopes[0]
        table[4, 8 + corner] = slopes[2]
        table[4, 16 + corner] = slopes[1]
        table[5, corner] = slopes[2]
        table[5, 16 + corner] = slopes[0]
    return table


def lookup(row, lane):
    return jnp.take_along_axis(
        jnp.broadcast_to(row, lane.shape), lane, axis=1, mode="promise_in_bounds"
    )


def pack_kernel(state, stiff, vel, out, nodes, shared, sems):
    lanes = state.shape[2]
    fetch = pltpu.make_async_copy(vel.at[:, 0:SHARED], nodes, sems.at[0])
    copies = [
        pltpu.make_async_copy(state, out.at[0:6, :, 0:lanes], sems.at[1]),
        pltpu.make_async_copy(stiff, out.at[6, :, 0:lanes], sems.at[2]),
    ]
    fetch.start()
    for copy in copies:
        copy.start()
    shared[...] = jnp.zeros((7, 8, EDGE), jnp.float32)
    fetch.wait()
    for c in range(3):
        for half in range(2):
            shared[c, half : half + 1, :] = nodes[c : c + 1, half * 128 : half * 128 + 128]
    copies.append(pltpu.make_async_copy(shared, out.at[:, :, lanes:], sems.at[3]))
    copies[-1].start()
    for copy in copies:
        copy.wait()


def is_odd():
    return lax.rem(lax.axis_index("slab"), 2) == 1


def fill(d, v, k, state, stiff, got_b, got_a, slabs):
    columns = state.shape[2] // 128
    odd = is_odd()

    def column(j, carry):
        here = pl.ds(pl.multiple_of(j * 128, 128), 128)
        for c in range(7):
            if slabs != [1]:
                a, b = got_a[c, :, here], got_b[c, :, here]
            for slab in slabs:
                if slab == 1:
                    value = state[c, :, here] if c < 6 else stiff[:, here]
                else:
                    value = jnp.where(odd, a, b) if slab == 0 else jnp.where(odd, b, a)
                at = slab * 8
                if c < 3:
                    d[pl.ds(pl.multiple_of((c * (columns + 2) + 1 + j) * DEEP + at, 8), 8), :] = value
                elif c < 6:
                    v[pl.ds(pl.multiple_of(((c - 3) * columns + j) * DEEP + at, 8), 8), :] = value
                else:
                    k[pl.ds(pl.multiple_of(j * DEEP + at, 8), 8), :] = value
        return carry

    lax.fori_loop(0, columns, column, 0, unroll=2)
    wrap(d, columns)


def wrap(d, columns):
    for c in range(3):
        base = c * (columns + 2) * DEEP
        d[base : base + DEEP, :] = d[base + columns * DEEP : base + (columns + 1) * DEEP, :]
        end = base + (columns + 1) * DEEP
        d[end : end + DEEP, :] = d[base + DEEP : base + 2 * DEEP, :]


def advance(d, v, k, windows, columns, emit):
    lane = lax.broadcasted_iota(jnp.int32, (8, 128), 1)
    first, last = lane == 0, lane == 127

    def group(g, carry):
        def at(ref, column, row):
            start = pl.multiple_of(g * (GROUP * DEEP), 8) + (column * DEEP + row)
            return ref[pl.ds(start, 8), :]

        for w in windows:
            stiffs = [at(k, i, w) for i in range(GROUP)]
            ready = []
            for c in range(3):
                base = c * (columns + 2)
                middles = [at(d, base + i, w) for i in range(GROUP + 2)]
                ahead = [pltpu.roll(m, 1, 1) for m in middles[:-1]]
                behind = [pltpu.roll(m, 127, 1) for m in middles[1:]]
                for i in range(GROUP):
                    left = jnp.where(first, ahead[i], ahead[i + 1])
                    right = jnp.where(last, behind[i + 1], behind[i])
                    middle = middles[i + 1]
                    above = at(d, base + i + 1, w - 1)
                    below = at(d, base + i + 1, w + 1)
                    laplace = (below + above) + (left + right) - 4.0 * middle
                    old = at(v, c * columns + i, w)
                    new = old + (stiffs[i] * laplace - DAMPING * old)
                    ready.append((w, c, g, i, middle + new, new))
            for item in ready:
                emit(*item)
        return carry

    lax.fori_loop(0, columns // GROUP, group, 0)


def keep(d, v, columns):
    def emit(w, c, g, i, new_d, new_v):
        base = pl.multiple_of(g * (GROUP * DEEP), 8)
        d[pl.ds(base + ((c * (columns + 2) + 1 + i) * DEEP + w), 8), :] = new_d
        v[pl.ds(base + ((c * columns + i) * DEEP + w), 8), :] = new_v

    return emit


WHOLE = [[1, 9, 15], [2, 10, 14], [3, 11, 13], [4, 12], [5, 11], [6, 10], [7, 9], [8]]
CONE = [[8, 15], [9, 14], [10, 13], [11, 12], [12], [12], [12], [12]]


def skull_kernel(state, stiff, got_b, got_a, out, d0, v0, d1, v1, k):
    columns = state.shape[2] // 128
    fill(d0, v0, k, state, stiff, got_b, got_a, [0, 1, 2])
    now, later = (d0, v0), (d1, v1)

    def last(w, c, g, i, new_d, new_v):
        here = pl.ds(pl.multiple_of(g * (GROUP * 128), 128) + i * 128, 128)
        out[c, :, here] = new_d
        out[3 + c, :, here] = new_v

    for step in range(SUBSTEPS):
        ends = step == SUBSTEPS - 1
        advance(*now, k, WHOLE[step], columns, last if ends else keep(*later, columns))
        if not ends:
            wrap(later[0], columns)
        now, later = later, now


def cone_kernel(state, stiff, got_b, got_a, shared, send, d0, v0, d1, v1, k):
    columns = state.shape[2] // 128
    fill(d0, v0, k, state, stiff, got_b, got_a, [0, 1, 2])
    now, later = (d0, v0), (d1, v1)
    for c in range(3):
        for half in range(2):
            send[c, columns + half : columns + half + 1, :] = shared[c : c + 1, half * 128 : half * 128 + 128]
    for step in range(SUBSTEPS):
        advance(*now, k, CONE[step], columns, keep(*later, columns))
        if step < SUBSTEPS - 1:
            wrap(later[0], columns)
        now, later = later, now
        for c in range(3):
            row = now[1][pl.ds(c * columns * DEEP + 15, columns, stride=DEEP), :]
            part = ((step + 1.0) / 36.0) * row
            send[c, 0:columns, :] = part if step == 0 else send[c, 0:columns, :] + part


def corners_kernel(vel, conn, out):
    blocks = conn.shape[1] // 128
    tables = vel.shape[1] // 128

    def block(b, carry):
        here = pl.ds(pl.multiple_of(b * 128, 128), 128)
        node = conn[:, here]
        lane, row = node & 127, node >> 7
        found = [jnp.zeros((8, 128), jnp.float32) for _ in range(3)]
        for r in range(tables):
            mine = row == r
            for c in range(3):
                value = lookup(vel[c : c + 1, r * 128 : r * 128 + 128], lane)
                found[c] = jnp.where(mine, value, found[c])
        for c in range(3):
            out[c * 8 : c * 8 + 8, here] = found[c]
        out[24:32, here] = jnp.zeros((8, 128), jnp.float32)
        return carry

    lax.fori_loop(0, blocks, block, 0)


def in_parts(value, count):
    parts = []
    for _ in range(count):
        part = value.astype(jnp.bfloat16)
        value = value - part.astype(jnp.float32)
        parts.append(part)
    return parts


def hexes_kernel(
    got_b, got_a, corners, conn, region, strain, spread, shear, bulk, weight, tau, memory_in,
    memory, owned, shared,
    work, rate, gains,
):
    lanes = got_a.shape[2] - EDGE
    elems = conn.shape[1]
    terms = memory_in.shape[0]
    regions = shear.shape[0]
    odd = is_odd()
    blocks = elems // 128
    first = owned.shape[1] // 128

    def add_shared(b, carry):
        here = pl.ds(pl.multiple_of(b * 128, 128), 128)
        node = conn[:, here]
        lane, row = node & 127, node >> 7
        for c in range(3):
            found = corners[c * 8 : c * 8 + 8, here]
            for half in range(2):
                a = got_a[c, half : half + 1, lanes:]
                b_ = got_b[c, half : half + 1, lanes:]
                found = jnp.where(row == first + half, lookup(jnp.where(odd, b_, a), lane), found)
            work[c * 8 : c * 8 + 8, here] = found
        work[24:32, here] = jnp.zeros((8, 128), jnp.float32)
        return carry

    lax.fori_loop(0, blocks, add_shared, 0, unroll=2)
    table = strain[...].astype(jnp.bfloat16)
    rate[...] = STEP_BRAIN * sum(
        jnp.dot(table, part, preferred_element_type=jnp.float32) for part in in_parts(work[...], 3)
    )

    def put(index, value):
        gains[index * 8 : index * 8 + 8, :] = jnp.broadcast_to(value, (8, 128))

    for r in range(regions):
        put(terms * regions + r, 2.0 * shear[r])
        put((terms + 1) * regions + r, bulk[r])
    for t in range(terms):
        span = jnp.full((8, 128), tau[t], jnp.float32)
        decay = jnp.exp(-STEP_BRAIN / span)
        put((terms + 2) * regions + t, decay)
        factor = (1.0 - decay) * span / STEP_BRAIN
        for r in range(regions):
            put(t * regions + r, (2.0 * shear[r] * weight[r, t]) * factor)

    def gain(index):
        return gains[index * 8 : index * 8 + 6, :]

    normal = lax.broadcasted_iota(jnp.int32, (6, 128), 0) < 3

    def block(b, carry):
        here = pl.ds(pl.multiple_of(b * 128, 128), 128)
        strains = rate[0:6, here]
        trace = rate[0:1, here] + rate[1:2, here] + rate[2:3, here]
        dev = jnp.where(normal, strains - trace / 3.0, 0.5 * strains)
        label = jnp.broadcast_to(region[:, here], (6, 128))
        masks = [label == r for r in range(regions)]

        def pick(t):
            chosen = jnp.zeros((6, 128), jnp.float32)
            for r, mask in enumerate(masks):
                chosen = jnp.where(mask, gain(t * regions + r), chosen)
            return chosen

        stress = pick(terms) * dev + jnp.where(normal, pick(terms + 1) * trace, 0.0)
        for t in range(terms):
            new = gain((terms + 2) * regions + t) * memory_in[t, :, here] + pick(t) * dev
            memory[t, :, here] = new
            stress = stress + new
        rate[0:6, here] = jnp.where(label < regions, stress, 0.0)
        return carry

    lax.fori_loop(0, blocks, block, 0, unroll=2)
    rate[6:16, :] = jnp.zeros((10, elems), jnp.float32)
    table = spread[...].astype(jnp.bfloat16)
    work[...] = sum(jnp.dot(table, part, preferred_element_type=jnp.float32) for part in in_parts(rate[...], 2))

    low_rows = lax.broadcasted_iota(jnp.int32, (LO, elems), 0)
    high_rows = lax.broadcasted_iota(jnp.int32, (HI, elems), 0)

    def corner(q, sums):
        node = conn[pl.ds(q, 1), :]
        low = (low_rows == (node & (LO - 1))).astype(jnp.float32).astype(jnp.bfloat16)
        mine = high_rows == (node >> 8)
        parts = []
        for c in range(3):
            parts += in_parts(jnp.where(mine, work[pl.ds(c * 8 + q, 1), :], 0.0), 2)
        return sums + lax.dot_general(
            jnp.concatenate(parts, 0), low, (((1,), (1,)), ((), ())), preferred_element_type=jnp.float32
        )

    sums = lax.fori_loop(0, 8, corner, jnp.zeros((6 * HI, LO), jnp.float32))
    for c in range(3):
        at = c * 2 * HI
        whole = sums[at : at + HI] + sums[at + HI : at + 2 * HI]
        for h in range(8):
            owned[c : c + 1, h * LO : h * LO + LO] = whole[h : h + 1]
        shared[c : c + 1, :] = whole[8:9]


def finish_kernel(sent, got_b, got_a, owned, vel, mass, src, weight, out):
    nodes = vel.shape[1]
    tables = sent.shape[1] - 2
    odd = is_odd()
    place = jnp.concatenate([src[:, 0:128], src[:, 128:256]], 0)
    share = weight[...] / jnp.sum(weight[...], 0, keepdims=True)
    share = jnp.concatenate([share[:, 0:128], share[:, 128:256]], 0)
    lane, row = place & 127, place >> 7
    for c in range(3):
        before = jnp.where(odd, got_a[c], got_b[c])
        after = jnp.where(odd, got_b[c], got_a[c])
        found = jnp.zeros((8, 128), jnp.float32)
        for slot, values in enumerate((before, sent[c], after)):
            for r in range(tables):
                found = jnp.where(row == slot * tables + r, lookup(values[r : r + 1], lane), found)
        found = found * share
        target = jnp.concatenate(
            [jnp.sum(found[0:4], 0, keepdims=True), jnp.sum(found[4:8], 0, keepdims=True)], 1
        )
        incoming = jnp.concatenate([before[tables : tables + 1], before[tables + 1 : tables + 2]], 1)
        old = vel[c : c + 1, :]
        total = owned[c : c + 1, :]
        total = jnp.concatenate([total[:, 0:SHARED] + incoming, total[:, SHARED:]], 1)
        new = old + STEP_BRAIN * total / mass[...]
        split = nodes - SHARED
        out[c : c + 1, 0:split] = new[:, 0:split]
        out[c : c + 1, split:] = new[:, split:] + COUPLING * (target - old[:, split:])


def on_device(
    skull_state, stiffness, intersection_src, intersection_weight, brain_vel, connectivity, region,
    shear_table, bulk_table, prony_weight, prony_tau, prony_state, node_mass,
):
    lanes = skull_state.shape[2]
    columns = lanes // 128
    nodes = brain_vel.shape[1]
    elems = connectivity.shape[1]
    terms, regions = prony_weight.shape
    count = lax.axis_size("slab")
    vmem = pl.BlockSpec(memory_space=pltpu.VMEM)
    smem = pl.BlockSpec(memory_space=pltpu.SMEM)
    hbm = pl.BlockSpec(memory_space=pltpu.HBM)
    shape = lambda *dims: jax.ShapeDtypeStruct(dims, jnp.float32)
    scratch = lambda *dims: pltpu.VMEM(dims, jnp.float32)

    def kernel(body, out, operands, results, scratch_shapes=(), flops=1_000_000, vmem_mib=32):
        return pl.pallas_call(
            body,
            out_shape=out,
            in_specs=operands,
            out_specs=results,
            scratch_shapes=list(scratch_shapes),
            compiler_params=pltpu.CompilerParams(vmem_limit_bytes=vmem_mib << 20),
            cost_estimate=pl.CostEstimate(flops=flops, bytes_accessed=4_000_000, transcendentals=0),
            name=body.__name__.removesuffix("_kernel"),
        )

    swap_a = [(i, i ^ 1) for i in range(count)]
    swap_b = [(i, ((i + 1) ^ 1) - 1) for i in range(1, count - 1)]
    field = [scratch(3 * (columns + 2) * DEEP, 128), scratch(3 * columns * DEEP, 128)]
    slabs = field + field + [scratch(columns * DEEP, 128)]
    table = strain_rows()

    package = kernel(
        pack_kernel, shape(7, 8, lanes + EDGE), [hbm, hbm, hbm], hbm,
        [scratch(3, SHARED), scratch(7, 8, EDGE), pltpu.SemaphoreType.DMA((4,))], vmem_mib=60,
    )(skull_state, stiffness, brain_vel)
    got_b = lax.ppermute(package, "slab", swap_b)
    got_a = lax.ppermute(package, "slab", swap_a)
    corners = kernel(corners_kernel, shape(32, elems), [vmem] * 2, vmem)(brain_vel, connectivity)
    memory, owned, shared = kernel(
        hexes_kernel,
        (shape(*prony_state.shape), shape(3, nodes), shape(3, SHARED)),
        [vmem] * 7 + [smem] * 4 + [vmem],
        [vmem] * 3,
        [scratch(32, elems), scratch(16, elems), scratch(((terms + 2) * regions + terms) * 8, 128)],
    )(
        got_b, got_a, corners, connectivity, region.reshape(1, elems), jnp.asarray(table), jnp.asarray(-table.T),
        shear_table, bulk_table, prony_weight.T, prony_tau, prony_state,
    )
    sent = kernel(cone_kernel, shape(3, columns + 2, 128), [vmem] * 5, vmem, slabs)(
        skull_state, stiffness, got_b, got_a, shared
    )
    back_b = lax.ppermute(sent, "slab", swap_b)
    back_a = lax.ppermute(sent, "slab", swap_a)
    skull_out = kernel(skull_kernel, shape(*skull_state.shape), [vmem] * 4, vmem, slabs, 50_000_000)(
        skull_state, stiffness, got_b, got_a
    )
    brain_out = kernel(finish_kernel, shape(3, nodes), [vmem] * 8, vmem)(
        sent, back_b, back_a, owned, brain_vel, node_mass.reshape(1, nodes), intersection_src.T, intersection_weight.T
    )
    return skull_out, brain_out, memory


def solution(mesh):
    placed = (
        P(None, "slab", None),
        P("slab", None),
        P("slab", None),
        P("slab", None),
        P(None, "slab"),
        P(None, "slab"),
        P("slab"),
        P(),
        P(),
        P(),
        P(),
        P(None, None, "slab"),
        P("slab"),
    )
    return jax.shard_map(
        on_device,
        mesh=mesh,
        in_specs=placed,
        out_specs=(P(None, "slab", None), P(None, "slab"), P(None, None, "slab")),
        check_vma=False,
    )
```

time: 365 us -> 88.3 us (0.24); the launches traced: 358 us -> 88 us
  starting transfers between devices: 168 us -> 33.3 us
  other arithmetic: 91.2 us -> 0 us
  local copies, waits for them, and re-layouts: 88 us -> 1.36 us
  Pallas kernels: 0 us -> 52.2 us
  waiting for transfers between devices: 7.98 us -> 0.28 us
    ppermute x34 -> x4, starting transfers between devices: 168 us -> 33.3 us  [the longest x1 15.2 us: on_device(): back_a = lax.ppermute(sent, 'slab', swap_a)]
    scatter-add x3 -> x0, other arithmetic: 81.9 us -> none  [the longest x1 80 us: on_device(): summed = jnp.zeros((3, nodes + SHARED), brain_vel.dtype).at[:, connectivi...]
    gather x3 -> x0, local copies, waits for them, and re-layouts: 65.3 us -> none  [the longest x2 59.7 us: on_device(): corners = all_vel[:, connectivity]]
    pallas_call x0 -> x6, Pallas kernels: none -> 52.2 us  [the longest x1 28.9 us: on_device(): kernel(pack_kernel, shape(7, 8, lanes + EDGE), [hbm, hbm, hbm], hbm, [scr...]
    slice x29 -> x0, local copies, waits for them, and re-layouts: 8.63 us -> none  [the longest x16 4.5 us: advance(): jnp.roll(displace, 1, 2)]
    ppermute x34 -> x4, waiting for transfers between devices: 7.98 us -> 0.28 us  [the longest x1 0.27 us: on_device(): got_a = lax.ppermute(package, 'slab', swap_a)]
    another operation x10 -> x0, local copies, waits for them, and re-layouts: 5.56 us -> none  [the longest x2 5.21 us: on_device(): forces.reshape(3, -1)]
    add x11 -> x0, other arithmetic: 4.06 us -> none  [the longest x8 3.39 us: advance(): return (displace + STEP_SKULL * velocity, velocity)]
  transfers between devices with their start and end apart: 34 -> 4, of which waited for: 7 -> 1; matrix products, arithmetic and copies ran while one was open for 46% -> 0% of each run, Pallas kernels for 0% -> 11%
where the time goes in v1:
time: 88.3 us; the launch traced here: 88 us
  Pallas kernels  52.2 us (59%)
  starting transfers between devices  33.3 us (38%)
  local copies, waits for them, and re-layouts  1.36 us (2%)
    pallas_call x1, Pallas kernels, on_device(): kernel(pack_kernel, shape(7, 8, lanes + EDGE), [hbm, hbm, hbm], hbm, [scr...  28.9 us
    ppermute x1, starting transfers between devices, on_device(): back_a = lax.ppermute(sent, 'slab', swap_a)  15.2 us
    ppermute x1, starting transfers between devices, on_device(): got_a = lax.ppermute(package, 'slab', swap_a)  12.4 us
    pallas_call x1, Pallas kernels, on_device(): kernel(skull_kernel, shape(*skull_state.shape), [vmem] * 4, vmem, slabs,...  8.08 us
    pallas_call x1, Pallas kernels, on_device(): kernel(hexes_kernel, (shape(*prony_state.shape), shape(3, nodes), shape(3...  6.44 us
    pallas_call x1, Pallas kernels, on_device(): kernel(cone_kernel, shape(3, columns + 2, 128), [vmem] * 5, vmem, slabs)  5.78 us
    ppermute x1, starting transfers between devices, on_device(): got_b = lax.ppermute(package, 'slab', swap_b)  3.76 us
    pallas_call x1, Pallas kernels, on_device(): kernel(corners_kernel, shape(32, elems), [vmem] * 2, vmem)  1.98 us
  transfers between devices with their start and end apart: 4, of which 1 were waited for; matrix products, arithmetic and copies ran while one was open for 0% of the time, Pallas kernels for 11%

profile of v1, /device:TPU:7, one launch (start us, length us, event | category | flops | bytes accessed | tf_op | source)
XLA Modules:
  0.0 88.0 jit_solution(18392623220626125713)
XLA Ops:
  0.6 0.0 copy-start.3
  0.6 0.0 copy-start.4
  0.7 0.0 copy-start.2
  0.7 28.9 %pack.1 = f32[7,8,4224]{2,1,0:T(8,128)} custom-call(f32[6,8,4096]{2,1,0:T(8,128)} %state.5, f32[8,4096]{1,0:T(8,128)} %stiff.5, f32[3,2048]{1,0:T(4,128)} %vel.5), custom_call_target="tpu_custom_call" | custom-call | flops 1000000 | bytes 4000000 | tf_op jit(solution)/shard_map/pack/pallas_call | solution.py:382
  29.6 0.0 copy-start.5
  29.6 3.8 %collective-permute-start = (f32[7,8,4224]{2,1,0:T(8,128)}, f32[7,8,4224]{2,1,0:T(8,128)S(1)}, u32[]{:S(2)}, u32[]{:S(2)}) collective-permute-start(f32[7,8,4224]{2,1,0:T(8,128)} %pack.1), channel_id=1, source_target_pairs={{1,2},{2,1},{3,4},{4,3},{5,6},{6,5},{7,8},{8,7},{9,10},{10,9},{11,... | collective-permute-start | bytes 2838536 | tf_op jit(solution)/shard_map/ppermute | solution.py:386
  33.4 12.4 %collective-permute-start.1 = (f32[7,8,4224]{2,1,0:T(8,128)}, f32[7,8,4224]{2,1,0:T(8,128)S(1)}, u32[]{:S(2)}, u32[]{:S(2)}) collective-permute-start(f32[7,8,4224]{2,1,0:T(8,128)} %pack.1), channel_id=1, source_target_pairs={{0,1},{1,0},{2,3},{3,2},{4,5},{5,4},{6,7},{7,6},{8,9},{9,8},{10,11... | collective-permute-start | bytes 2838536 | tf_op jit(solution)/shard_map/ppermute | solution.py:387
  45.8 0.0 copy-done.3
  45.8 0.0 copy-done.4
  45.8 0.0 copy-start.6
  45.8 0.0 copy-start.7
  45.8 2.0 %corners.1 = f32[32,2048]{1,0:T(8,128)S(1)} custom-call(f32[3,2048]{1,0:T(4,128)S(1)} %copy-done.3, s32[8,2048]{1,0:T(8,128)S(1)} %copy-done.4), custom_call_target="tpu_custom_call" | custom-call | flops 1000000 | bytes 4000000 | tf_op jit(solution)/shard_map/corners/pallas_call | solution.py:388
  47.8 0.0 copy-start.11
  47.8 0.0 collective-permute-done.got_b
  47.8 0.3 collective-permute-done.1.got_a
  48.1 0.0 copy-start.12
  48.1 0.0 copy-start.13
  48.1 0.0 copy-start.14
  48.1 0.0 copy-done.2
  48.1 0.0 copy-done.5
  48.1 0.0 copy-done.6
  48.1 0.0 copy-done.7
  48.1 0.3 copy-done.11
  48.5 0.3 copy-done.12
  48.8 0.0 copy-done.13
  48.8 0.0 copy-done.14
  48.8 0.0 copy-start
  48.8 0.0 copy-start.1
  48.8 6.4 %hexes.1 = (f32[12,6,2048]{2,1,0:T(8,128)}, f32[3,2048]{1,0:T(4,128)S(1)}, f32[3,256]{1,0:T(4,128)S(1)}) custom-call(f32[7,8,4224]{2,1,0:T(8,128)S(1)} %collective-permute-done.got_b, f32[7,8,4224]{2,1,0:T(8,128)S(1)} %collective-permute-done.1.got_a, f32[32,2048]{1,0:T(8,128)S(1)} %corners.1, s32[8,2048]{1,0:T(8,128)S(1)} %copy-done.4, ...), custom_call_target="tpu_custom_call" | custom-call | flops 1000000 | bytes 4000000 | tf_op jit(solution)/shard_map/hexes/pallas_call | solution.py:389
  55.2 0.0 copy-done
  55.2 0.0 copy-done.1
  55.2 5.8 %cone.1.sent = f32[3,34,128]{2,1,0:T(8,128)S(1)} custom-call(f32[6,8,4096]{2,1,0:T(8,128)S(1)} %copy-done, f32[8,4096]{1,0:T(8,128)S(1)} %copy-done.1, f32[7,8,4224]{2,1,0:T(8,128)S(1)} %collective-permute-done.got_b, f32[7,8,4224]{2,1,0:T(8,128)S(1)} %collective-permute-done.1.got_a, f32[3,256]{1,0:T(4,128)S(1)} %get-tuple-element.6.shared), custom_call_target="tpu_custom_call" | custom-call | flops 1000000 | bytes 4000000 | tf_op jit(solution)/shard_map/cone/pallas_call | solution.py:399
  61.0 1.9 %collective-permute-start.2 = (f32[3,34,128]{2,1,0:T(8,128)S(1)}, f32[3,34,128]{2,1,0:T(8,128)S(1)}, u32[]{:S(2)}, u32[]{:S(2)}) collective-permute-start(f32[3,34,128]{2,1,0:T(8,128)S(1)} %cone.1.sent), channel_id=1, source_target_pairs={{1,2},{2,1},{3,4},{4,3},{5,6},{6,5},{7,8},{8,7},{9,10},{10,9},{11,... | collective-permute-start | bytes 156680 | tf_op jit(solution)/shard_map/ppermute | solution.py:402
  63.0 15.2 %collective-permute-start.3 = (f32[3,34,128]{2,1,0:T(8,128)S(1)}, f32[3,34,128]{2,1,0:T(8,128)S(1)}, u32[]{:S(2)}, u32[]{:S(2)}) collective-permute-start(f32[3,34,128]{2,1,0:T(8,128)S(1)} %cone.1.sent), channel_id=1, source_target_pairs={{0,1},{1,0},{2,3},{3,2},{4,5},{5,4},{6,7},{7,6},{8,9},{9,8},{10,11... | collective-permute-start | bytes 156680 | tf_op jit(solution)/shard_map/ppermute | solution.py:403
  78.2 0.0 copy-start.8
  78.2 0.0 copy-start.10
  78.2 8.1 %skull.1 = f32[6,8,4096]{2,1,0:T(8,128)} custom-call(f32[6,8,4096]{2,1,0:T(8,128)S(1)} %copy-done, f32[8,4096]{1,0:T(8,128)S(1)} %copy-done.1, f32[7,8,4224]{2,1,0:T(8,128)S(1)} %collective-permute-done.got_b, f32[7,8,4224]{2,1,0:T(8,128)S(1)} %collective-permute-done.1.got_a), custom_call_target="tpu_custom_call" | custom-call | flops 50000000 | bytes 4000000 | tf_op jit(solution)/shard_map/skull/pallas_call | solution.py:404
  86.3 0.0 copy-start.9
  86.3 0.0 collective-permute-done.2.got_b
  86.3 0.0 collective-permute-done.3.got_a
  86.3 0.0 copy-done.8
  86.3 0.0 copy-done.10
  86.3 0.7 copy-done.9
  86.9 1.0 %finish.1 = f32[3,2048]{1,0:T(4,128)} custom-call(f32[3,34,128]{2,1,0:T(8,128)S(1)} %cone.1.sent, f32[3,34,128]{2,1,0:T(8,128)S(1)} %collective-permute-done.2.got_b, f32[3,34,128]{2,1,0:T(8,128)S(1)} %collective-permute-done.3.got_a, f32[3,2048]{1,0:T(4,128)S(1)} %get-tuple-element.7.owned, f32[3,2048]{1,0:T(4,128)S(1)} %copy-done.3, ...), custom_call_target="tpu_custom_call" | custom-call | flops 1000000 | bytes 4000000 | tf_op jit(solution)/shard_map/finish/pallas_call | solution.py:407
Async XLA Ops:
  0.6 45.1 %copy-start.3 = (f32[3,2048]{1,0:T(4,128)S(1)}, f32[3,2048]{1,0:T(4,128)}, u32[]{:S(2)}) copy-start(f32[3,2048]{1,0:T(4,128)} %vel.5) | copy-start | bytes 73732
  0.6 45.1 %copy-start.4 = (s32[8,2048]{1,0:T(8,128)S(1)}, s32[8,2048]{1,0:T(8,128)}, u32[]{:S(2)}) copy-start(s32[8,2048]{1,0:T(8,128)} %conn.3) | copy-start | bytes 196612
  0.7 47.5 %copy-start.2 = (f32[12,6,2048]{2,1,0:T(8,128)S(1)}, f32[12,6,2048]{2,1,0:T(8,128)}, u32[]{:S(2)}) copy-start(f32[12,6,2048]{2,1,0:T(8,128)} %memory_in.1) | copy-start | bytes 1769476
  29.6 18.5 %copy-start.5 = (f32[32,16]{1,0:T(8,128)S(1)}, f32[32,16]{1,0:T(8,128)}, u32[]{:S(2)}) copy-start(f32[32,16]{1,0:T(8,128)} %constant.5.clone.spread) | copy-start | bytes 6148
  29.6 18.2 %collective-permute-start = (f32[7,8,4224]{2,1,0:T(8,128)}, f32[7,8,4224]{2,1,0:T(8,128)S(1)}, u32[]{:S(2)}, u32[]{:S(2)}) collective-permute-start(f32[7,8,4224]{2,1,0:T(8,128)} %pack.1), channel_id=1, source_target_pairs={{1,2},{2,1},{3,4},{4,3},{5,6},{6,5},{7,8},{8,7},{9,10},{10,9},{11,... | collective-permute-start | bytes 2838536 | tf_op jit(solution)/shard_map/ppermute | solution.py:386
  33.4 14.7 %collective-permute-start.1 = (f32[7,8,4224]{2,1,0:T(8,128)}, f32[7,8,4224]{2,1,0:T(8,128)S(1)}, u32[]{:S(2)}, u32[]{:S(2)}) collective-permute-start(f32[7,8,4224]{2,1,0:T(8,128)} %pack.1), channel_id=1, source_target_pairs={{0,1},{1,0},{2,3},{3,2},{4,5},{5,4},{6,7},{7,6},{8,9},{9,8},{10,11... | collective-permute-start | bytes 2838536 | tf_op jit(solution)/shard_map/ppermute | solution.py:387
  45.8 2.3 %copy-start.6 = (s32[2048]{0:T(1024)S(1)}, s32[2048]{0:T(1024)}, u32[]{:S(2)}) copy-start(s32[2048]{0:T(1024)} %param.21) | copy-start | bytes 24580
  45.8 2.3 %copy-start.7 = (f32[16,32]{1,0:T(8,128)S(1)}, f32[16,32]{1,0:T(8,128)}, u32[]{:S(2)}) copy-start(f32[16,32]{1,0:T(8,128)} %constant.4.clone.strain) | copy-start | bytes 6148
  47.8 0.7 copy-start.11
  48.1 0.7 copy-start.12
  48.1 0.7 copy-start.13
  48.1 0.7 copy-start.14
  48.8 6.4 %copy-start = (f32[6,8,4096]{2,1,0:T(8,128)S(1)}, f32[6,8,4096]{2,1,0:T(8,128)}, u32[]{:S(2)}) copy-start(f32[6,8,4096]{2,1,0:T(8,128)} %state.5) | copy-start | bytes 2359300
  48.8 6.4 %copy-start.1 = (f32[8,4096]{1,0:T(8,128)S(1)}, f32[8,4096]{1,0:T(8,128)}, u32[]{:S(2)}) copy-start(f32[8,4096]{1,0:T(8,128)} %stiff.5) | copy-start | bytes 393220
  61.0 25.2 %collective-permute-start.2 = (f32[3,34,128]{2,1,0:T(8,128)S(1)}, f32[3,34,128]{2,1,0:T(8,128)S(1)}, u32[]{:S(2)}, u32[]{:S(2)}) collective-permute-start(f32[3,34,128]{2,1,0:T(8,128)S(1)} %cone.1.sent), channel_id=1, source_target_pairs={{1,2},{2,1},{3,4},{4,3},{5,6},{6,5},{7,8},{8,7},{9,10},{10,9},{11,... | collective-permute-start | bytes 156680 | tf_op jit(solution)/shard_map/ppermute | solution.py:402
  63.0 23.3 %collective-permute-start.3 = (f32[3,34,128]{2,1,0:T(8,128)S(1)}, f32[3,34,128]{2,1,0:T(8,128)S(1)}, u32[]{:S(2)}, u32[]{:S(2)}) collective-permute-start(f32[3,34,128]{2,1,0:T(8,128)S(1)} %cone.1.sent), channel_id=1, source_target_pairs={{0,1},{1,0},{2,3},{3,2},{4,5},{5,4},{6,7},{7,6},{8,9},{9,8},{10,11... | collective-permute-start | bytes 156680 | tf_op jit(solution)/shard_map/ppermute | solution.py:403
  78.2 8.1 %copy-start.8 = (f32[2048]{0:T(1024)S(1)}, f32[2048]{0:T(1024)}, u32[]{:S(2)}) copy-start(f32[2048]{0:T(1024)} %param.27) | copy-start | bytes 24580
  78.2 8.1 %copy-start.10 = (f32[256,4]{0,1:T(4,128)S(1)}, f32[256,4]{0,1:T(4,128)}, u32[]{:S(2)}) copy-start(f32[256,4]{0,1:T(4,128)} %param.18) | copy-start | bytes 12292
  86.3 0.7 copy-start.9

commit v2 on v1

--- a/solution.py
+++ b/solution.py
@@ -40,24 +40,25 @@
     )
 
 
-def pack_kernel(state, stiff, vel, out, nodes, shared, sems):
+def pack_kernel(state, stiff, vel, out, nodes, package, sems):
     lanes = state.shape[2]
-    fetch = pltpu.make_async_copy(vel.at[:, 0:SHARED], nodes, sems.at[0])
-    copies = [
-        pltpu.make_async_copy(state, out.at[0:6, :, 0:lanes], sems.at[1]),
-        pltpu.make_async_copy(stiff, out.at[6, :, 0:lanes], sems.at[2]),
+    first = pltpu.make_async_copy(vel.at[:, 0:SHARED], nodes, sems.at[14])
+    arrive = [
+        pltpu.make_async_copy(state.at[c] if c < 6 else stiff, package.at[c, :, 0:lanes], sems.at[c]) for c in range(7)
     ]
-    fetch.start()
-    for copy in copies:
+    leave = [pltpu.make_async_copy(package.at[c], out.at[c], sems.at[7 + c]) for c in range(7)]
+    first.start()
+    for copy in arrive:
         copy.start()
-    shared[...] = jnp.zeros((7, 8, EDGE), jnp.float32)
-    fetch.wait()
+    package[:, :, lanes:] = jnp.zeros((7, 8, EDGE), jnp.float32)
+    first.wait()
     for c in range(3):
         for half in range(2):
-            shared[c, half : half + 1, :] = nodes[c : c + 1, half * 128 : half * 128 + 128]
-    copies.append(pltpu.make_async_copy(shared, out.at[:, :, lanes:], sems.at[3]))
-    copies[-1].start()
-    for copy in copies:
+            package[c, half : half + 1, lanes:] = nodes[c : c + 1, half * 128 : half * 128 + 128]
+    for c in range(7):
+        arrive[c].wait()
+        leave[c].start()
+    for copy in leave:
         copy.wait()
 
 
@@ -65,20 +66,23 @@
     return lax.rem(lax.axis_index("slab"), 2) == 1
 
 
-def fill(d, v, k, state, stiff, got_b, got_a, slabs):
+def from_previous(by_b, by_a):
+    return jnp.where(is_odd(), by_a, by_b)
+
+
+def from_next(by_b, by_a):
+    return jnp.where(is_odd(), by_b, by_a)
+
+
+def fill(d, v, k, state, stiff, got_a, got_b):
     columns = state.shape[2] // 128
-    odd = is_odd()
 
     def column(j, carry):
         here = pl.ds(pl.multiple_of(j * 128, 128), 128)
         for c in range(7):
-            if slabs != [1]:
-                a, b = got_a[c, :, here], got_b[c, :, here]
-            for slab in slabs:
-                if slab == 1:
-                    value = state[c, :, here] if c < 6 else stiff[:, here]
-                else:
-                    value = jnp.where(odd, a, b) if slab == 0 else jnp.where(odd, b, a)
+            own = state[c, :, here] if c < 6 else stiff[:, here]
+            b, a = got_b[c, :, here], got_a[c, :, here]
+            for slab, value in enumerate((from_previous(b, a), own, from_next(b, a))):
                 at = slab * 8
                 if c < 3:
                     d[pl.ds(pl.multiple_of((c * (columns + 2) + 1 + j) * DEEP + at, 8), 8), :] = value
@@ -144,18 +148,22 @@
 
 
 WHOLE = [[1, 9, 15], [2, 10, 14], [3, 11, 13], [4, 12], [5, 11], [6, 10], [7, 9], [8]]
-CONE = [[8, 15], [9, 14], [10, 13], [11, 12], [12], [12], [12], [12]]
-
-
-def skull_kernel(state, stiff, got_b, got_a, out, d0, v0, d1, v1, k):
+
+
+def skull_kernel(state, stiff, got_a, got_b, shared, out, send, d0, v0, d1, v1, k):
     columns = state.shape[2] // 128
-    fill(d0, v0, k, state, stiff, got_b, got_a, [0, 1, 2])
+    fill(d0, v0, k, state, stiff, got_a, got_b)
     now, later = (d0, v0), (d1, v1)
+    for c in range(3):
+        for half in range(2):
+            send[c, columns + half : columns + half + 1, :] = shared[c : c + 1, half * 128 : half * 128 + 128]
 
     def last(w, c, g, i, new_d, new_v):
         here = pl.ds(pl.multiple_of(g * (GROUP * 128), 128) + i * 128, 128)
         out[c, :, here] = new_d
         out[3 + c, :, here] = new_v
+        base = pl.multiple_of(g * (GROUP * DEEP), 8)
+        v0[pl.ds(base + ((c * columns + i) * DEEP + w), 8), :] = new_v
 
     for step in range(SUBSTEPS):
         ends = step == SUBSTEPS - 1
@@ -163,27 +171,42 @@
         if not ends:
             wrap(later[0], columns)
         now, later = later, now
-
-
-def cone_kernel(state, stiff, got_b, got_a, shared, send, d0, v0, d1, v1, k):
-    columns = state.shape[2] // 128
-    fill(d0, v0, k, state, stiff, got_b, got_a, [0, 1, 2])
-    now, later = (d0, v0), (d1, v1)
-    for c in range(3):
-        for half in range(2):
-            send[c, columns + half : columns + half + 1, :] = shared[c : c + 1, half * 128 : half * 128 + 128]
-    for step in range(SUBSTEPS):
-        advance(*now, k, CONE[step], columns, keep(*later, columns))
-        if step < SUBSTEPS - 1:
-            wrap(later[0], columns)
-        now, later = later, now
         for c in range(3):
             row = now[1][pl.ds(c * columns * DEEP + 15, columns, stride=DEEP), :]
             part = ((step + 1.0) / 36.0) * row
             send[c, 0:columns, :] = part if step == 0 else send[c, 0:columns, :] + part
 
 
-def corners_kernel(vel, conn, out):
+def prepare_kernel(vel, conn, src, weight, shear, bulk, prony, tau, out, place, share, gains, lows):
+    elems = conn.shape[1]
+    regions, terms = prony.shape
+    normed = weight[...] / jnp.sum(weight[...], 0, keepdims=True)
+    for half in range(2):
+        place[half * 4 : half * 4 + 4, :] = src[:, half * 128 : half * 128 + 128]
+        share[half * 4 : half * 4 + 4, :] = normed[:, half * 128 : half * 128 + 128]
+
+    def put(index, value):
+        gains[index * 8 : index * 8 + 8, :] = jnp.broadcast_to(value, (8, 128))
+
+    for r in range(regions):
+        put(terms * regions + r, 2.0 * shear[r])
+        put((terms + 1) * regions + r, bulk[r])
+    for t in range(terms):
+        span = jnp.full((8, 128), tau[t], jnp.float32)
+        decay = jnp.exp(-STEP_BRAIN / span)
+        put((terms + 2) * regions + t, decay)
+        factor = (1.0 - decay) * span / STEP_BRAIN
+        for r in range(regions):
+            put(t * regions + r, (2.0 * shear[r] * prony[r, t]) * factor)
+
+    low_rows = lax.broadcasted_iota(jnp.int32, (LO, elems), 0)
+
+    def corner(q, carry):
+        node = conn[pl.ds(q, 1), :]
+        lows[q] = (low_rows == (node & (LO - 1))).astype(jnp.float32).astype(jnp.bfloat16)
+        return carry
+
+    lax.fori_loop(0, 8, corner, 0)
     blocks = conn.shape[1] // 128
     tables = vel.shape[1] // 128
 
@@ -215,17 +238,17 @@
 
 
 def hexes_kernel(
-    got_b, got_a, corners, conn, region, strain, spread, shear, bulk, weight, tau, memory_in,
-    memory, owned, shared,
-    work, rate, gains,
+    got_a, got_b, corners, conn, region, strain, spread, vel, mass, memory_in, gains, lows,
+    memory, base, shared, scale,
+    work, rate,
 ):
-    lanes = got_a.shape[2] - EDGE
     elems = conn.shape[1]
     terms = memory_in.shape[0]
-    regions = shear.shape[0]
-    odd = is_odd()
+    regions = (gains.shape[0] // 8 - terms) // (terms + 2)
     blocks = elems // 128
-    first = owned.shape[1] // 128
+    lanes = got_b.shape[2] - EDGE
+    ghost = from_next(got_b[0:3, :, lanes:], got_a[0:3, :, lanes:])
+    first = base.shape[1] // 128
 
     def add_shared(b, carry):
         here = pl.ds(pl.multiple_of(b * 128, 128), 128)
@@ -234,9 +257,8 @@
         for c in range(3):
             found = corners[c * 8 : c * 8 + 8, here]
             for half in range(2):
-                a = got_a[c, half : half + 1, lanes:]
-                b_ = got_b[c, half : half + 1, lanes:]
-                found = jnp.where(row == first + half, lookup(jnp.where(odd, b_, a), lane), found)
+                value = lookup(ghost[c, half : half + 1], lane)
+                found = jnp.where(row == first + half, value, found)
             work[c * 8 : c * 8 + 8, here] = found
         work[24:32, here] = jnp.zeros((8, 128), jnp.float32)
         return carry
@@ -246,20 +268,6 @@
     rate[...] = STEP_BRAIN * sum(
         jnp.dot(table, part, preferred_element_type=jnp.float32) for part in in_parts(work[...], 3)
     )
-
-    def put(index, value):
-        gains[index * 8 : index * 8 + 8, :] = jnp.broadcast_to(value, (8, 128))
-
-    for r in range(regions):
-        put(terms * regions + r, 2.0 * shear[r])
-        put((terms + 1) * regions + r, bulk[r])
-    for t in range(terms):
-        span = jnp.full((8, 128), tau[t], jnp.float32)
-        decay = jnp.exp(-STEP_BRAIN / span)
-        put((terms + 2) * regions + t, decay)
-        factor = (1.0 - decay) * span / STEP_BRAIN
-        for r in range(regions):
-            put(t * regions + r, (2.0 * shear[r] * weight[r, t]) * factor)
 
     def gain(index):
         return gains[index * 8 : index * 8 + 6, :]
@@ -293,18 +301,16 @@
     table = spread[...].astype(jnp.bfloat16)
     work[...] = sum(jnp.dot(table, part, preferred_element_type=jnp.float32) for part in in_parts(rate[...], 2))
 
-    low_rows = lax.broadcasted_iota(jnp.int32, (LO, elems), 0)
     high_rows = lax.broadcasted_iota(jnp.int32, (HI, elems), 0)
 
     def corner(q, sums):
         node = conn[pl.ds(q, 1), :]
-        low = (low_rows == (node & (LO - 1))).astype(jnp.float32).astype(jnp.bfloat16)
         mine = high_rows == (node >> 8)
         parts = []
         for c in range(3):
             parts += in_parts(jnp.where(mine, work[pl.ds(c * 8 + q, 1), :], 0.0), 2)
         return sums + lax.dot_general(
-            jnp.concatenate(parts, 0), low, (((1,), (1,)), ((), ())), preferred_element_type=jnp.float32
+            jnp.concatenate(parts, 0), lows[q], (((1,), (1,)), ((), ())), preferred_element_type=jnp.float32
         )
 
     sums = lax.fori_loop(0, 8, corner, jnp.zeros((6 * HI, LO), jnp.float32))
@@ -312,37 +318,33 @@
         at = c * 2 * HI
         whole = sums[at : at + HI] + sums[at + HI : at + 2 * HI]
         for h in range(8):
-            owned[c : c + 1, h * LO : h * LO + LO] = whole[h : h + 1]
+            here = slice(h * LO, h * LO + LO)
+            old = vel[c : c + 1, here]
+            base[c : c + 1, here] = old * (1.0 - COUPLING if h == 7 else 1.0) + STEP_BRAIN * whole[h : h + 1] / mass[:, here]
         shared[c : c + 1, :] = whole[8:9]
-
-
-def finish_kernel(sent, got_b, got_a, owned, vel, mass, src, weight, out):
-    nodes = vel.shape[1]
+    scale[...] = STEP_BRAIN / mass[:, 0:SHARED]
+
+
+def finish_kernel(sent, got_a, got_b, base, scale, place, share, out):
+    nodes = base.shape[1]
     tables = sent.shape[1] - 2
-    odd = is_odd()
-    place = jnp.concatenate([src[:, 0:128], src[:, 128:256]], 0)
-    share = weight[...] / jnp.sum(weight[...], 0, keepdims=True)
-    share = jnp.concatenate([share[:, 0:128], share[:, 128:256]], 0)
-    lane, row = place & 127, place >> 7
+    lane, row = place[...] & 127, place[...] >> 7
     for c in range(3):
-        before = jnp.where(odd, got_a[c], got_b[c])
-        after = jnp.where(odd, got_b[c], got_a[c])
+        before = from_previous(got_b[c], got_a[c])
+        after = from_next(got_b[c], got_a[c])
         found = jnp.zeros((8, 128), jnp.float32)
         for slot, values in enumerate((before, sent[c], after)):
             for r in range(tables):
                 found = jnp.where(row == slot * tables + r, lookup(values[r : r + 1], lane), found)
-        found = found * share
+        found = found * share[...]
         target = jnp.concatenate(
             [jnp.sum(found[0:4], 0, keepdims=True), jnp.sum(found[4:8], 0, keepdims=True)], 1
         )
         incoming = jnp.concatenate([before[tables : tables + 1], before[tables + 1 : tables + 2]], 1)
-        old = vel[c : c + 1, :]
-        total = owned[c : c + 1, :]
-        total = jnp.concatenate([total[:, 0:SHARED] + incoming, total[:, SHARED:]], 1)
-        new = old + STEP_BRAIN * total / mass[...]
         split = nodes - SHARED
-        out[c : c + 1, 0:split] = new[:, 0:split]
-        out[c : c + 1, split:] = new[:, split:] + COUPLING * (target - old[:, split:])
+        out[c : c + 1, 0:SHARED] = base[c : c + 1, 0:SHARED] + incoming * scale[...]
+        out[c : c + 1, SHARED:split] = base[c : c + 1, SHARED:split]
+        out[c : c + 1, split:] = base[c : c + 1, split:] + COUPLING * target
 
 
 def on_device(
@@ -375,37 +377,55 @@
 
     swap_a = [(i, i ^ 1) for i in range(count)]
     swap_b = [(i, ((i + 1) ^ 1) - 1) for i in range(1, count - 1)]
+
+    def swap(value):
+        return lax.ppermute(value, "slab", swap_b), lax.ppermute(value, "slab", swap_a)
+
     field = [scratch(3 * (columns + 2) * DEEP, 128), scratch(3 * columns * DEEP, 128)]
     slabs = field + field + [scratch(columns * DEEP, 128)]
     table = strain_rows()
 
     package = kernel(
         pack_kernel, shape(7, 8, lanes + EDGE), [hbm, hbm, hbm], hbm,
-        [scratch(3, SHARED), scratch(7, 8, EDGE), pltpu.SemaphoreType.DMA((4,))], vmem_mib=60,
+        [scratch(3, SHARED), scratch(7, 8, lanes + EDGE), pltpu.SemaphoreType.DMA((15,))], vmem_mib=60,
     )(skull_state, stiffness, brain_vel)
-    got_b = lax.ppermute(package, "slab", swap_b)
-    got_a = lax.ppermute(package, "slab", swap_a)
-    corners = kernel(corners_kernel, shape(32, elems), [vmem] * 2, vmem)(brain_vel, connectivity)
-    memory, owned, shared = kernel(
+    got_b, got_a = swap(package)
+    gain_rows = ((terms + 2) * regions + terms) * 8
+    corners, place, share, gains, lows = kernel(
+        prepare_kernel,
+        (
+            shape(32, elems),
+            jax.ShapeDtypeStruct((8, 128), jnp.int32),
+            shape(8, 128),
+            shape(gain_rows, 128),
+            jax.ShapeDtypeStruct((8, LO, elems), jnp.bfloat16),
+        ),
+        [vmem] * 4 + [smem] * 4,
+        [vmem] * 5,
+    )(
+        brain_vel, connectivity, intersection_src.T, intersection_weight.T,
+        shear_table, bulk_table, prony_weight.T, prony_tau,
+    )
+    memory, base, shared, scale = kernel(
         hexes_kernel,
-        (shape(*prony_state.shape), shape(3, nodes), shape(3, SHARED)),
-        [vmem] * 7 + [smem] * 4 + [vmem],
-        [vmem] * 3,
-        [scratch(32, elems), scratch(16, elems), scratch(((terms + 2) * regions + terms) * 8, 128)],
+        (shape(*prony_state.shape), shape(3, nodes), shape(3, SHARED), shape(1, SHARED)),
+        [vmem] * 12,
+        [vmem] * 4,
+        [scratch(32, elems), scratch(16, elems)],
     )(
-        got_b, got_a, corners, connectivity, region.reshape(1, elems), jnp.asarray(table), jnp.asarray(-table.T),
-        shear_table, bulk_table, prony_weight.T, prony_tau, prony_state,
-    )
-    sent = kernel(cone_kernel, shape(3, columns + 2, 128), [vmem] * 5, vmem, slabs)(
-        skull_state, stiffness, got_b, got_a, shared
-    )
-    back_b = lax.ppermute(sent, "slab", swap_b)
-    back_a = lax.ppermute(sent, "slab", swap_a)
-    skull_out = kernel(skull_kernel, shape(*skull_state.shape), [vmem] * 4, vmem, slabs, 50_000_000)(
-        skull_state, stiffness, got_b, got_a
-    )
-    brain_out = kernel(finish_kernel, shape(3, nodes), [vmem] * 8, vmem)(
-        sent, back_b, back_a, owned, brain_vel, node_mass.reshape(1, nodes), intersection_src.T, intersection_weight.T
+        got_a, got_b, corners, connectivity, region.reshape(1, elems), jnp.asarray(table), jnp.asarray(-table.T),
+        brain_vel, node_mass.reshape(1, nodes), prony_state, gains, lows,
+    )
+    skull_out, sent = kernel(
+        skull_kernel,
+        (shape(*skull_state.shape), shape(3, columns + 2, 128)),
+        [vmem] * 5,
+        [vmem] * 2,
+        slabs,
+    )(skull_state, stiffness, got_a, got_b, shared)
+    back_b, back_a = swap(sent)
+    brain_out = kernel(finish_kernel, shape(3, nodes), [vmem] * 7, vmem)(
+        sent, back_a, back_b, base, scale, place, share
     )
     return skull_out, brain_out, memory
 

time: 88.3 us -> 59.3 us (0.67)
  Pallas kernels: 52.2 us -> 21.6 us
  local copies, waits for them, and re-layouts: 1.36 us -> 9.55 us
  starting transfers between devices: 33.3 us -> 25.9 us
    pallas_call x1, Pallas kernels: 28.9 us -> 2.15 us  [on_device(): kernel(pack_kernel, shape(7, 8, lanes + EDGE), [hbm, hbm, hbm], hbm, [scr...]
    unnamed x30, local copies, waits for them, and re-layouts: 1.36 us -> 9.55 us
    ppermute x4, starting transfers between devices: 33.3 us -> 25.9 us  [the longest x2 20.2 us: swap(): lax.ppermute(value, 'slab', swap_a)]
    pallas_call x4 -> x3, Pallas kernels: 16.8 us -> 13.3 us  [the longest x1 8.25 us: on_device(): kernel(skull_kernel, (shape(*skull_state.shape), shape(3, columns + 2, 12...]
  transfers between devices with their start and end apart: 4 -> 4, of which waited for: 1 -> 1; matrix products, arithmetic and copies ran while one was open for 0% -> 0% of each run, Pallas kernels for 11% -> 7%
where the time goes in v2:
time: 59.3 us; the launch traced here: 58.7 us
  starting transfers between devices  25.9 us (44%)
  Pallas kernels  21.6 us (36%)
  local copies, waits for them, and re-layouts  9.55 us (16%)
  waiting for transfers between devices  0.87 us (1%)
  between operations  0.75 us (1%)
    ppermute x2, starting transfers between devices, swap(): lax.ppermute(value, 'slab', swap_a)  20.2 us
    unnamed x30, local copies, waits for them, and re-layouts  9.55 us
    pallas_call x1, Pallas kernels, on_device(): kernel(skull_kernel, (shape(*skull_state.shape), shape(3, columns + 2, 12...  8.25 us
    pallas_call x1, Pallas kernels, on_device(): kernel(hexes_kernel, (shape(*prony_state.shape), shape(3, nodes), shape(3...  6.19 us
    ppermute x2, starting transfers between devices, swap(): lax.ppermute(value, 'slab', swap_b)  5.67 us
    pallas_call x1, Pallas kernels, on_device(): kernel(prepare_kernel, (shape(32, elems), jax.ShapeDtypeStruct((8, 128),...  4.03 us
    pallas_call x1, Pallas kernels, on_device(): kernel(pack_kernel, shape(7, 8, lanes + EDGE), [hbm, hbm, hbm], hbm, [scr...  2.15 us
  transfers between devices with their start and end apart: 4, of which 1 were waited for; matrix products, arithmetic and copies ran while one was open for 0% of the time, Pallas kernels for 7%

profile of v2, /device:TPU:7, one launch (start us, length us, event | category | flops | bytes accessed | tf_op | source)
XLA Modules:
  0.0 58.7 jit_solution(12222004705831695979)
XLA Ops:
  0.6 0.0 copy-start.2
  0.6 0.0 copy-start
  0.6 2.1 %pack.1 = f32[7,8,4224]{2,1,0:T(8,128)} custom-call(f32[6,8,4096]{2,1,0:T(8,128)} %state.3, f32[8,4096]{1,0:T(8,128)} %stiff.3, f32[3,2048]{1,0:T(4,128)} %vel.5), custom_call_target="tpu_custom_call" | custom-call | flops 1000000 | bytes 4000000 | tf_op jit(solution)/shard_map/pack/pallas_call | solution.py:388
  2.8 3.8 %collective-permute-start.1 = (f32[7,8,4224]{2,1,0:T(8,128)}, f32[7,8,4224]{2,1,0:T(8,128)S(1)}, u32[]{:S(2)}, u32[]{:S(2)}) collective-permute-start(f32[7,8,4224]{2,1,0:T(8,128)} %pack.1), channel_id=1, source_target_pairs={{1,2},{2,1},{3,4},{4,3},{5,6},{6,5},{7,8},{8,7},{9,10},{10,9},{11,... | collective-permute-start | bytes 2838536 | tf_op jit(solution)/shard_map/ppermute | solution.py:382
  6.6 12.4 %collective-permute-start = (f32[7,8,4224]{2,1,0:T(8,128)}, f32[7,8,4224]{2,1,0:T(8,128)S(1)}, u32[]{:S(2)}, u32[]{:S(2)}) collective-permute-start(f32[7,8,4224]{2,1,0:T(8,128)} %pack.1), channel_id=1, source_target_pairs={{0,1},{1,0},{2,3},{3,2},{4,5},{5,4},{6,7},{7,6},{8,9},{9,8},{10,11... | collective-permute-start | bytes 2838536 | tf_op jit(solution)/shard_map/ppermute | solution.py:382
  19.0 0.0 copy-start.3
  19.0 0.7 %copy-done.3 = f32[3,2048]{1,0:T(4,128)S(1)} copy-done((f32[3,2048]{1,0:T(4,128)S(1)}, f32[3,2048]{1,0:T(4,128)}, u32[]{:S(2)}) %copy-start.3) | copy-done | bytes 24600
  19.7 0.0 copy-start.4
  19.7 0.8 %copy-done.4 = s32[8,2048]{1,0:T(8,128)S(1)} copy-done((s32[8,2048]{1,0:T(8,128)S(1)}, s32[8,2048]{1,0:T(8,128)}, u32[]{:S(2)}) %copy-start.4) | copy-done | bytes 65560
  20.6 0.0 copy-start.9
  20.6 0.7 %copy-done.9 = s32[256,4]{0,1:T(4,128)S(1)} copy-done((s32[256,4]{0,1:T(4,128)S(1)}, s32[256,4]{0,1:T(4,128)}, u32[]{:S(2)}) %copy-start.9) | copy-done | bytes 4120
  21.3 0.0 copy-start.10
  21.3 0.7 %copy-done.10 = f32[256,4]{0,1:T(4,128)S(1)} copy-done((f32[256,4]{0,1:T(4,128)S(1)}, f32[256,4]{0,1:T(4,128)}, u32[]{:S(2)}) %copy-start.10) | copy-done | bytes 4120
  21.9 0.0 copy-start.11
  21.9 0.7 %copy-done.11 = f32[12,4]{0,1:T(4,128)S(1)} copy-done((f32[12,4]{0,1:T(4,128)S(1)}, f32[12,4]{0,1:T(4,128)}, u32[]{:S(2)}) %copy-start.11) | copy-done | bytes 216
  22.6 0.0 copy-start.12
  22.6 0.7 %copy-done.12 = f32[4]{0:T(128)S(1)} copy-done((f32[4]{0:T(128)S(1)}, f32[4]{0:T(128)}, u32[]{:S(2)}) %copy-start.12) | copy-done | bytes 40
  23.3 0.0 copy-start.13
  23.3 0.7 %copy-done.13 = f32[4]{0:T(128)S(1)} copy-done((f32[4]{0:T(128)S(1)}, f32[4]{0:T(128)}, u32[]{:S(2)}) %copy-start.13) | copy-done | bytes 40
  23.9 0.0 copy-start.14
  23.9 0.7 %copy-done.14 = f32[12]{0:T(128)S(1)} copy-done((f32[12]{0:T(128)S(1)}, f32[12]{0:T(128)}, u32[]{:S(2)}) %copy-start.14) | copy-done | bytes 72
  24.6 4.0 %prepare.1 = (f32[32,2048]{1,0:T(8,128)S(1)}, s32[8,128]{1,0:T(8,128)S(1)}, f32[8,128]{1,0:T(8,128)S(1)}, f32[544,128]{1,0:T(8,128)S(1)}, bf16[8,256,2048]{2,1,0:T(8,128)(2,1)S(1)}) custom-call(f32[3,2048]{1,0:T(4,128)S(1)} %copy-done.3, s32[8,2048]{1,0:T(8,128)S(1)} %copy-done.4, s32[4,256]{1,0:T(4,128)S(1)} %bitcast.7, f32[4,256]{1,0:T(4,128)S(1)} %bitcast.8, ...), custom_call_target="tpu_custom_call" | custom-call | flops 1000000 | bytes 4000000 | tf_op jit(solution)/shard_map/prepare/pallas_call | solution.py:394
  28.6 0.0 collective-permute-done.1.got_b
  28.6 0.0 collective-permute-done.got_a
  28.6 0.0 copy-start.1
  28.7 1.1 %copy-done.1 = f32[12,6,2048]{2,1,0:T(8,128)S(1)} copy-done((f32[12,6,2048]{2,1,0:T(8,128)S(1)}, f32[12,6,2048]{2,1,0:T(8,128)}, u32[]{:S(2)}) %copy-start.1) | copy-done | bytes 589848
  29.8 0.0 copy-start.5
  29.8 0.7 %copy-done.5 = f32[32,16]{1,0:T(8,128)S(1)} copy-done((f32[32,16]{1,0:T(8,128)S(1)}, f32[32,16]{1,0:T(8,128)}, u32[]{:S(2)}) %copy-start.5) | copy-done | bytes 2072
  30.5 0.0 copy-start.6
  30.5 0.7 %copy-done.6 = s32[2048]{0:T(1024)S(1)} copy-done((s32[2048]{0:T(1024)S(1)}, s32[2048]{0:T(1024)}, u32[]{:S(2)}) %copy-start.6) | copy-done | bytes 8216
  31.2 0.0 copy-start.7
  31.2 0.7 %copy-done.7 = f32[2048]{0:T(1024)S(1)} copy-done((f32[2048]{0:T(1024)S(1)}, f32[2048]{0:T(1024)}, u32[]{:S(2)}) %copy-start.7) | copy-done | bytes 8216
  31.9 0.0 copy-start.8
  31.9 0.7 %copy-done.8 = f32[16,32]{1,0:T(8,128)S(1)} copy-done((f32[16,32]{1,0:T(8,128)S(1)}, f32[16,32]{1,0:T(8,128)}, u32[]{:S(2)}) %copy-start.8) | copy-done | bytes 2072
  32.6 6.2 %hexes.1 = (f32[12,6,2048]{2,1,0:T(8,128)}, f32[3,2048]{1,0:T(4,128)S(1)}, f32[3,256]{1,0:T(4,128)S(1)}, f32[1,256]{1,0:T(1,128)S(1)}) custom-call(f32[7,8,4224]{2,1,0:T(8,128)S(1)} %collective-permute-done.got_a, f32[7,8,4224]{2,1,0:T(8,128)S(1)} %collective-permute-done.1.got_b, f32[32,2048]{1,0:T(8,128)S(1)} %get-tuple-element.14.corners, ...), custom_call_target="tpu_custom_call" | custom-call | flops 1000000 | bytes 4000000 | tf_op jit(solution)/shard_map/hexes/pallas_call | solution.py:409
  38.8 0.0 copy-done.2
  38.8 0.0 copy-done
  38.8 8.2 %skull.1 = (f32[6,8,4096]{2,1,0:T(8,128)}, f32[3,34,128]{2,1,0:T(8,128)S(1)}) custom-call(f32[6,8,4096]{2,1,0:T(8,128)S(1)} %copy-done, f32[8,4096]{1,0:T(8,128)S(1)} %copy-done.2, f32[7,8,4224]{2,1,0:T(8,128)S(1)} %collective-permute-done.got_a, f32[7,8,4224]{2,1,0:T(8,128)S(1)} %collective-permute-done.1.got_b, f32[3,256]{1,0:T(4,128)S(1)} %get-tuple-element.17.shared), custom_call_target="tpu_custom_call" | custom-call | flops 1000000 | bytes 4000000 | tf_op jit(solution)/shard_map/skull/pallas_call | solution.py:419
  47.0 1.9 %collective-permute-start.3 = (f32[3,34,128]{2,1,0:T(8,128)S(1)}, f32[3,34,128]{2,1,0:T(8,128)S(1)}, u32[]{:S(2)}, u32[]{:S(2)}) collective-permute-start(f32[3,34,128]{2,1,0:T(8,128)S(1)} %get-tuple-element.19.sent), channel_id=1, source_target_pairs={{1,2},{2,1},{3,4},{4,3},{5,6},{6,5},{7,8},{8,7},{9,10},{10,9},{11,... | collective-permute-start | bytes 156680 | tf_op jit(solution)/shard_map/ppermute | solution.py:382
  48.9 7.8 %collective-permute-start.2 = (f32[3,34,128]{2,1,0:T(8,128)S(1)}, f32[3,34,128]{2,1,0:T(8,128)S(1)}, u32[]{:S(2)}, u32[]{:S(2)}) collective-permute-start(f32[3,34,128]{2,1,0:T(8,128)S(1)} %get-tuple-element.19.sent), channel_id=1, source_target_pairs={{0,1},{1,0},{2,3},{3,2},{4,5},{5,4},{6,7},{7,6},{8,9},{9,8},{10,11... | collective-permute-start | bytes 156680 | tf_op jit(solution)/shard_map/ppermute | solution.py:382
  56.8 0.0 collective-permute-done.3.got_b
  56.8 0.9 %collective-permute-done.2.got_a = f32[3,34,128]{2,1,0:T(8,128)S(1)} collective-permute-done((f32[3,34,128]{2,1,0:T(8,128)S(1)}, f32[3,34,128]{2,1,0:T(8,128)S(1)}, u32[]{:S(2)}, u32[]{:S(2)}) %collective-permute-start.2) | collective-permute-done | bytes 52256 | tf_op jit(solution)/shard_map/ppermute | solution.py:382
  57.7 1.0 %finish.1 = f32[3,2048]{1,0:T(4,128)} custom-call(f32[3,34,128]{2,1,0:T(8,128)S(1)} %get-tuple-element.19.sent, f32[3,34,128]{2,1,0:T(8,128)S(1)} %collective-permute-done.2.got_a, f32[3,34,128]{2,1,0:T(8,128)S(1)} %collective-permute-done.3.got_b, f32[3,2048]{1,0:T(4,128)S(1)} %get-tuple-element.20.base, f32[1,256]{1,0:T(1,128)S(1)} %get-tuple-element.21.scale, ...), custom_call_target="tpu_custom_call" | custom-call | flops 1000000 | bytes 4000000 | tf_op jit(solution)/shard_map/finish/pallas_call | solution.py:427
Async XLA Ops:
  0.6 38.2 %copy-start.2 = (f32[8,4096]{1,0:T(8,128)S(1)}, f32[8,4096]{1,0:T(8,128)}, u32[]{:S(2)}) copy-start(f32[8,4096]{1,0:T(8,128)} %stiff.3) | copy-start | bytes 393220
  0.6 38.1 %copy-start = (f32[6,8,4096]{2,1,0:T(8,128)S(1)}, f32[6,8,4096]{2,1,0:T(8,128)}, u32[]{:S(2)}) copy-start(f32[6,8,4096]{2,1,0:T(8,128)} %state.3) | copy-start | bytes 2359300
  2.8 25.8 %collective-permute-start.1 = (f32[7,8,4224]{2,1,0:T(8,128)}, f32[7,8,4224]{2,1,0:T(8,128)S(1)}, u32[]{:S(2)}, u32[]{:S(2)}) collective-permute-start(f32[7,8,4224]{2,1,0:T(8,128)} %pack.1), channel_id=1, source_target_pairs={{1,2},{2,1},{3,4},{4,3},{5,6},{6,5},{7,8},{8,7},{9,10},{10,9},{11,... | collective-permute-start | bytes 2838536 | tf_op jit(solution)/shard_map/ppermute | solution.py:382
  6.6 22.1 %collective-permute-start = (f32[7,8,4224]{2,1,0:T(8,128)}, f32[7,8,4224]{2,1,0:T(8,128)S(1)}, u32[]{:S(2)}, u32[]{:S(2)}) collective-permute-start(f32[7,8,4224]{2,1,0:T(8,128)} %pack.1), channel_id=1, source_target_pairs={{0,1},{1,0},{2,3},{3,2},{4,5},{5,4},{6,7},{7,6},{8,9},{9,8},{10,11... | collective-permute-start | bytes 2838536 | tf_op jit(solution)/shard_map/ppermute | solution.py:382
  19.0 0.8 %copy-start.3 = (f32[3,2048]{1,0:T(4,128)S(1)}, f32[3,2048]{1,0:T(4,128)}, u32[]{:S(2)}) copy-start(f32[3,2048]{1,0:T(4,128)} %vel.5) | copy-start | bytes 73732
  19.7 0.8 %copy-start.4 = (s32[8,2048]{1,0:T(8,128)S(1)}, s32[8,2048]{1,0:T(8,128)}, u32[]{:S(2)}) copy-start(s32[8,2048]{1,0:T(8,128)} %conn.3) | copy-start | bytes 196612
  20.6 0.7 %copy-start.9 = (s32[256,4]{0,1:T(4,128)S(1)}, s32[256,4]{0,1:T(4,128)}, u32[]{:S(2)}) copy-start(s32[256,4]{0,1:T(4,128)} %param.17) | copy-start | bytes 12292
  21.3 0.7 %copy-start.10 = (f32[256,4]{0,1:T(4,128)S(1)}, f32[256,4]{0,1:T(4,128)}, u32[]{:S(2)}) copy-start(f32[256,4]{0,1:T(4,128)} %param.18) | copy-start | bytes 12292
  21.9 0.7 %copy-start.11 = (f32[12,4]{0,1:T(4,128)S(1)}, f32[12,4]{0,1:T(4,128)}, u32[]{:S(2)}) copy-start(f32[12,4]{0,1:T(4,128)} %param.24) | copy-start | bytes 580
  22.6 0.7 %copy-start.12 = (f32[4]{0:T(128)S(1)}, f32[4]{0:T(128)}, u32[]{:S(2)}) copy-start(f32[4]{0:T(128)} %shear.1) | copy-start | bytes 52
  23.3 0.7 %copy-start.13 = (f32[4]{0:T(128)S(1)}, f32[4]{0:T(128)}, u32[]{:S(2)}) copy-start(f32[4]{0:T(128)} %bulk.1) | copy-start | bytes 52
  23.9 0.7 %copy-start.14 = (f32[12]{0:T(128)S(1)}, f32[12]{0:T(128)}, u32[]{:S(2)}) copy-start(f32[12]{0:T(128)} %tau.1) | copy-start | bytes 148
  28.6 1.1 %copy-start.1 = (f32[12,6,2048]{2,1,0:T(8,128)S(1)}, f32[12,6,2048]{2,1,0:T(8,128)}, u32[]{:S(2)}) copy-start(f32[12,6,2048]{2,1,0:T(8,128)} %memory_in.1) | copy-start | bytes 1769476
  29.8 0.7 %copy-start.5 = (f32[32,16]{1,0:T(8,128)S(1)}, f32[32,16]{1,0:T(8,128)}, u32[]{:S(2)}) copy-start(f32[32,16]{1,0:T(8,128)} %constant.5.clone.spread) | copy-start | bytes 6148
  30.5 0.7 %copy-start.6 = (s32[2048]{0:T(1024)S(1)}, s32[2048]{0:T(1024)}, u32[]{:S(2)}) copy-start(s32[2048]{0:T(1024)} %param.21) | copy-start | bytes 24580
  31.2 0.7 %copy-start.7 = (f32[2048]{0:T(1024)S(1)}, f32[2048]{0:T(1024)}, u32[]{:S(2)}) copy-start(f32[2048]{0:T(1024)} %param.27) | copy-start | bytes 24580
  31.9 0.7 %copy-start.8 = (f32[16,32]{1,0:T(8,128)S(1)}, f32[16,32]{1,0:T(8,128)}, u32[]{:S(2)}) copy-start(f32[16,32]{1,0:T(8,128)} %constant.4.clone.strain) | copy-start | bytes 6148
  47.0 9.8 %collective-permute-start.3 = (f32[3,34,128]{2,1,0:T(8,128)S(1)}, f32[3,34,128]{2,1,0:T(8,128)S(1)}, u32[]{:S(2)}, u32[]{:S(2)}) collective-permute-start(f32[3,34,128]{2,1,0:T(8,128)S(1)} %get-tuple-element.19.sent), channel_id=1, source_target_pairs={{1,2},{2,1},{3,4},{4,3},{5,6},{6,5},{7,8},{8,7},{9,10},{10,9},{11,... | collective-permute-start | bytes 156680 | tf_op jit(solution)/shard_map/ppermute | solution.py:382
  48.9 8.7 %collective-permute-start.2 = (f32[3,34,128]{2,1,0:T(8,128)S(1)}, f32[3,34,128]{2,1,0:T(8,128)S(1)}, u32[]{:S(2)}, u32[]{:S(2)}) collective-permute-start(f32[3,34,128]{2,1,0:T(8,128)S(1)} %get-tuple-element.19.sent), channel_id=1, source_target_pairs={{0,1},{1,0},{2,3},{3,2},{4,5},{5,4},{6,7},{7,6},{8,9},{9,8},{10,11... | collective-permute-start | bytes 156680 | tf_op jit(solution)/shard_map/ppermute | solution.py:382

commit v3 on v2

--- a/solution.py
+++ b/solution.py
@@ -14,8 +14,8 @@
 EDGE = 128
 DEEP = 24
 GROUP = 8
-LO = 256
-HI = 16
+LO = 128
+HI = 32
 
 
 def strain_rows():
@@ -177,36 +177,11 @@
             send[c, 0:columns, :] = part if step == 0 else send[c, 0:columns, :] + part
 
 
-def prepare_kernel(vel, conn, src, weight, shear, bulk, prony, tau, out, place, share, gains, lows):
-    elems = conn.shape[1]
-    regions, terms = prony.shape
+def corners_kernel(vel, conn, src, weight, out, place, share):
     normed = weight[...] / jnp.sum(weight[...], 0, keepdims=True)
     for half in range(2):
         place[half * 4 : half * 4 + 4, :] = src[:, half * 128 : half * 128 + 128]
         share[half * 4 : half * 4 + 4, :] = normed[:, half * 128 : half * 128 + 128]
-
-    def put(index, value):
-        gains[index * 8 : index * 8 + 8, :] = jnp.broadcast_to(value, (8, 128))
-
-    for r in range(regions):
-        put(terms * regions + r, 2.0 * shear[r])
-        put((terms + 1) * regions + r, bulk[r])
-    for t in range(terms):
-        span = jnp.full((8, 128), tau[t], jnp.float32)
-        decay = jnp.exp(-STEP_BRAIN / span)
-        put((terms + 2) * regions + t, decay)
-        factor = (1.0 - decay) * span / STEP_BRAIN
-        for r in range(regions):
-            put(t * regions + r, (2.0 * shear[r] * prony[r, t]) * factor)
-
-    low_rows = lax.broadcasted_iota(jnp.int32, (LO, elems), 0)
-
-    def corner(q, carry):
-        node = conn[pl.ds(q, 1), :]
-        lows[q] = (low_rows == (node & (LO - 1))).astype(jnp.float32).astype(jnp.bfloat16)
-        return carry
-
-    lax.fori_loop(0, 8, corner, 0)
     blocks = conn.shape[1] // 128
     tables = vel.shape[1] // 128
 
@@ -238,13 +213,13 @@
 
 
 def hexes_kernel(
-    got_a, got_b, corners, conn, region, strain, spread, vel, mass, memory_in, gains, lows,
+    got_a, got_b, corners, conn, region, strain, spread, vel, mass, shear, bulk, weight, tau, memory_in,
     memory, base, shared, scale,
-    work, rate,
+    work, rate, gains,
 ):
     elems = conn.shape[1]
     terms = memory_in.shape[0]
-    regions = (gains.shape[0] // 8 - terms) // (terms + 2)
+    regions = shear.shape[0]
     blocks = elems // 128
     lanes = got_b.shape[2] - EDGE
     ghost = from_next(got_b[0:3, :, lanes:], got_a[0:3, :, lanes:])
@@ -269,6 +244,20 @@
         jnp.dot(table, part, preferred_element_type=jnp.float32) for part in in_parts(work[...], 3)
     )
 
+    def put(index, value):
+        gains[index * 8 : index * 8 + 8, :] = jnp.broadcast_to(value, (8, 128))
+
+    for r in range(regions):
+        put(terms * regions + r, 2.0 * shear[r])
+        put((terms + 1) * regions + r, bulk[r])
+    for t in range(terms):
+        span = jnp.full((8, 128), tau[t], jnp.float32)
+        decay = jnp.exp(-STEP_BRAIN / span)
+        put((terms + 2) * regions + t, decay)
+        factor = (1.0 - decay) * span / STEP_BRAIN
+        for r in range(regions):
+            put(t * regions + r, (2.0 * shear[r] * weight[r, t]) * factor)
+
     def gain(index):
         return gains[index * 8 : index * 8 + 6, :]
 
@@ -289,10 +278,13 @@
             return chosen
 
         stress = pick(terms) * dev + jnp.where(normal, pick(terms + 1) * trace, 0.0)
+        ready = []
         for t in range(terms):
             new = gain((terms + 2) * regions + t) * memory_in[t, :, here] + pick(t) * dev
-            memory[t, :, here] = new
+            ready.append(new)
             stress = stress + new
+        for t in range(terms):
+            memory[t, :, here] = ready[t]
         rate[0:6, here] = jnp.where(label < regions, stress, 0.0)
         return carry
 
@@ -301,27 +293,31 @@
     table = spread[...].astype(jnp.bfloat16)
     work[...] = sum(jnp.dot(table, part, preferred_element_type=jnp.float32) for part in in_parts(rate[...], 2))
 
+    low_rows = lax.broadcasted_iota(jnp.int32, (LO, elems), 0)
     high_rows = lax.broadcasted_iota(jnp.int32, (HI, elems), 0)
 
     def corner(q, sums):
         node = conn[pl.ds(q, 1), :]
-        mine = high_rows == (node >> 8)
+        low = (low_rows == (node & (LO - 1))).astype(jnp.float32).astype(jnp.bfloat16)
+        mine = high_rows == (node >> 7)
         parts = []
         for c in range(3):
             parts += in_parts(jnp.where(mine, work[pl.ds(c * 8 + q, 1), :], 0.0), 2)
         return sums + lax.dot_general(
-            jnp.concatenate(parts, 0), lows[q], (((1,), (1,)), ((), ())), preferred_element_type=jnp.float32
+            jnp.concatenate(parts, 0), low, (((1,), (1,)), ((), ())), preferred_element_type=jnp.float32
         )
 
     sums = lax.fori_loop(0, 8, corner, jnp.zeros((6 * HI, LO), jnp.float32))
     for c in range(3):
         at = c * 2 * HI
         whole = sums[at : at + HI] + sums[at + HI : at + 2 * HI]
-        for h in range(8):
+        for h in range(first):
             here = slice(h * LO, h * LO + LO)
             old = vel[c : c + 1, here]
-            base[c : c + 1, here] = old * (1.0 - COUPLING if h == 7 else 1.0) + STEP_BRAIN * whole[h : h + 1] / mass[:, here]
-        shared[c : c + 1, :] = whole[8:9]
+            kept = 1.0 if h < first - SHARED // LO else 1.0 - COUPLING
+            base[c : c + 1, here] = kept * old + STEP_BRAIN * whole[h : h + 1] / mass[:, here]
+        for half in range(SHARED // LO):
+            shared[c : c + 1, half * LO : half * LO + LO] = whole[first + half : first + half + 1]
     scale[...] = STEP_BRAIN / mass[:, 0:SHARED]
 
 
@@ -390,31 +386,21 @@
         [scratch(3, SHARED), scratch(7, 8, lanes + EDGE), pltpu.SemaphoreType.DMA((15,))], vmem_mib=60,
     )(skull_state, stiffness, brain_vel)
     got_b, got_a = swap(package)
-    gain_rows = ((terms + 2) * regions + terms) * 8
-    corners, place, share, gains, lows = kernel(
-        prepare_kernel,
-        (
-            shape(32, elems),
-            jax.ShapeDtypeStruct((8, 128), jnp.int32),
-            shape(8, 128),
-            shape(gain_rows, 128),
-            jax.ShapeDtypeStruct((8, LO, elems), jnp.bfloat16),
-        ),
-        [vmem] * 4 + [smem] * 4,
-        [vmem] * 5,
-    )(
-        brain_vel, connectivity, intersection_src.T, intersection_weight.T,
-        shear_table, bulk_table, prony_weight.T, prony_tau,
-    )
+    corners, place, share = kernel(
+        corners_kernel,
+        (shape(32, elems), jax.ShapeDtypeStruct((8, 128), jnp.int32), shape(8, 128)),
+        [vmem] * 4,
+        [vmem] * 3,
+    )(brain_vel, connectivity, intersection_src.T, intersection_weight.T)
     memory, base, shared, scale = kernel(
         hexes_kernel,
         (shape(*prony_state.shape), shape(3, nodes), shape(3, SHARED), shape(1, SHARED)),
-        [vmem] * 12,
+        [vmem] * 9 + [smem] * 4 + [vmem],
         [vmem] * 4,
-        [scratch(32, elems), scratch(16, elems)],
+        [scratch(32, elems), scratch(16, elems), scratch(((terms + 2) * regions + terms) * 8, 128)],
     )(
         got_a, got_b, corners, connectivity, region.reshape(1, elems), jnp.asarray(table), jnp.asarray(-table.T),
-        brain_vel, node_mass.reshape(1, nodes), prony_state, gains, lows,
+        brain_vel, node_mass.reshape(1, nodes), shear_table, bulk_table, prony_weight.T, prony_tau, prony_state,
     )
     skull_out, sent = kernel(
         skull_kernel,

time: 59.3 us -> 55.9 us (0.943)
  local copies, waits for them, and re-layouts: 9.55 us -> 0.71 us
  starting transfers between devices: 25.9 us -> 33.2 us
  Pallas kernels: 21.6 us -> 19.8 us
    unnamed x30, local copies, waits for them, and re-layouts: 9.55 us -> 0.71 us
    ppermute x2, starting transfers between devices: 20.2 us -> 27.6 us  [swap(): lax.ppermute(value, 'slab', swap_a)]
    pallas_call x1, Pallas kernels: 4.03 us -> 2 us  [on_device(): kernel(corners_kernel, (shape(32, elems), jax.ShapeDtypeStruct((8, 128),...]
  transfers between devices with their start and end apart: 4 -> 4, of which waited for: 1 -> 2; matrix products, arithmetic and copies ran while one was open for 0% -> 0% of each run, Pallas kernels for 7% -> 4%
where the time goes in v3:
time: 55.9 us; the launch traced here: 55.7 us
  starting transfers between devices  33.2 us (59%)
  Pallas kernels  19.8 us (35%)
  waiting for transfers between devices  1.09 us (2%)
  between operations  0.84 us (2%)
  local copies, waits for them, and re-layouts  0.71 us (1%)
    ppermute x2, starting transfers between devices, swap(): lax.ppermute(value, 'slab', swap_a)  27.6 us
    pallas_call x1, Pallas kernels, on_device(): kernel(skull_kernel, (shape(*skull_state.shape), shape(3, columns + 2, 12...  8.25 us
    pallas_call x1, Pallas kernels, on_device(): kernel(hexes_kernel, (shape(*prony_state.shape), shape(3, nodes), shape(3...  6.42 us
    ppermute x2, starting transfers between devices, swap(): lax.ppermute(value, 'slab', swap_b)  5.67 us
    pallas_call x1, Pallas kernels, on_device(): kernel(pack_kernel, shape(7, 8, lanes + EDGE), [hbm, hbm, hbm], hbm, [scr...  2.14 us
    pallas_call x1, Pallas kernels, on_device(): kernel(corners_kernel, (shape(32, elems), jax.ShapeDtypeStruct((8, 128),...  2 us
  transfers between devices with their start and end apart: 4, of which 2 were waited for; matrix products, arithmetic and copies ran while one was open for 0% of the time, Pallas kernels for 4%

profile of v3, /device:TPU:7, one launch (start us, length us, event | category | flops | bytes accessed | tf_op | source)
XLA Modules:
  0.0 55.7 jit_solution(3452092880072938865)
XLA Ops:
  0.6 0.0 copy-start.3
  0.6 0.0 copy-start.4
  0.7 0.0 copy-start.1
  0.7 0.0 copy-start.9
  0.7 0.0 copy-start.10
  0.7 2.1 %pack.1 = f32[7,8,4224]{2,1,0:T(8,128)} custom-call(f32[6,8,4096]{2,1,0:T(8,128)} %state.3, f32[8,4096]{1,0:T(8,128)} %stiff.3, f32[3,2048]{1,0:T(4,128)} %vel.5), custom_call_target="tpu_custom_call" | custom-call | flops 1000000 | bytes 4000000 | tf_op jit(solution)/shard_map/pack/pallas_call | solution.py:384
  2.8 3.8 %collective-permute-start.1 = (f32[7,8,4224]{2,1,0:T(8,128)}, f32[7,8,4224]{2,1,0:T(8,128)S(1)}, u32[]{:S(2)}, u32[]{:S(2)}) collective-permute-start(f32[7,8,4224]{2,1,0:T(8,128)} %pack.1), channel_id=1, source_target_pairs={{1,2},{2,1},{3,4},{4,3},{5,6},{6,5},{7,8},{8,7},{9,10},{10,9},{11,... | collective-permute-start | bytes 2838536 | tf_op jit(solution)/shard_map/ppermute | solution.py:378
  6.6 12.4 %collective-permute-start = (f32[7,8,4224]{2,1,0:T(8,128)}, f32[7,8,4224]{2,1,0:T(8,128)S(1)}, u32[]{:S(2)}, u32[]{:S(2)}) collective-permute-start(f32[7,8,4224]{2,1,0:T(8,128)} %pack.1), channel_id=1, source_target_pairs={{0,1},{1,0},{2,3},{3,2},{4,5},{5,4},{6,7},{7,6},{8,9},{9,8},{10,11... | collective-permute-start | bytes 2838536 | tf_op jit(solution)/shard_map/ppermute | solution.py:378
  19.0 0.0 copy-done.3
  19.0 0.0 copy-done.4
  19.0 0.0 copy-done.9
  19.0 0.0 copy-done.10
  19.0 0.0 copy-start.5
  19.0 0.0 copy-start.6
  19.1 0.0 copy-start.7
  19.1 0.0 copy-start.8
  19.1 2.0 %corners.1 = (f32[32,2048]{1,0:T(8,128)S(1)}, s32[8,128]{1,0:T(8,128)S(1)}, f32[8,128]{1,0:T(8,128)S(1)}) custom-call(f32[3,2048]{1,0:T(4,128)S(1)} %copy-done.3, s32[8,2048]{1,0:T(8,128)S(1)} %copy-done.4, s32[4,256]{1,0:T(4,128)S(1)} %bitcast.7, f32[4,256]{1,0:T(4,128)S(1)} %bitcast.8), custom_call_target="tpu_custom_call" | custom-call | flops 1000000 | bytes 4000000 | tf_op jit(solution)/shard_map/corners/pallas_call | solution.py:389
  21.1 0.0 collective-permute-done.1.got_b
  21.1 0.2 collective-permute-done.got_a
  21.3 0.0 copy-start.11
  21.3 0.0 copy-start.12
  21.3 0.0 copy-start.13
  21.3 0.0 copy-start.14
  21.3 0.0 copy-done.1
  21.3 0.0 copy-done.5
  21.3 0.0 copy-done.6
  21.4 0.0 copy-done.7
  21.4 0.0 copy-done.8
  21.4 0.6 %copy-done.11 = f32[12,4]{0,1:T(4,128)S(1)} copy-done((f32[12,4]{0,1:T(4,128)S(1)}, f32[12,4]{0,1:T(4,128)}, u32[]{:S(2)}) %copy-start.11) | copy-done | bytes 216
  22.0 0.0 copy-done.12
  22.0 0.0 copy-done.13
  22.0 0.0 copy-done.14
  22.0 0.0 copy-start
  22.0 0.0 copy-start.2
  22.0 6.4 %hexes.1 = (f32[12,6,2048]{2,1,0:T(8,128)}, f32[3,2048]{1,0:T(4,128)S(1)}, f32[3,256]{1,0:T(4,128)S(1)}, f32[1,256]{1,0:T(1,128)S(1)}) custom-call(f32[7,8,4224]{2,1,0:T(8,128)S(1)} %collective-permute-done.got_a, f32[7,8,4224]{2,1,0:T(8,128)S(1)} %collective-permute-done.1.got_b, f32[32,2048]{1,0:T(8,128)S(1)} %get-tuple-element.12.corners, ...), custom_call_target="tpu_custom_call" | custom-call | flops 1000000 | bytes 4000000 | tf_op jit(solution)/shard_map/hexes/pallas_call | solution.py:395
  28.4 0.0 copy-done
  28.4 0.0 copy-done.2
  28.4 8.2 %skull.1 = (f32[6,8,4096]{2,1,0:T(8,128)}, f32[3,34,128]{2,1,0:T(8,128)S(1)}) custom-call(f32[6,8,4096]{2,1,0:T(8,128)S(1)} %copy-done, f32[8,4096]{1,0:T(8,128)S(1)} %copy-done.2, f32[7,8,4224]{2,1,0:T(8,128)S(1)} %collective-permute-done.got_a, f32[7,8,4224]{2,1,0:T(8,128)S(1)} %collective-permute-done.1.got_b, f32[3,256]{1,0:T(4,128)S(1)} %get-tuple-element.13.shared), custom_call_target="tpu_custom_call" | custom-call | flops 1000000 | bytes 4000000 | tf_op jit(solution)/shard_map/skull/pallas_call | solution.py:405
  36.7 1.9 %collective-permute-start.3 = (f32[3,34,128]{2,1,0:T(8,128)S(1)}, f32[3,34,128]{2,1,0:T(8,128)S(1)}, u32[]{:S(2)}, u32[]{:S(2)}) collective-permute-start(f32[3,34,128]{2,1,0:T(8,128)S(1)} %get-tuple-element.15.sent), channel_id=1, source_target_pairs={{1,2},{2,1},{3,4},{4,3},{5,6},{6,5},{7,8},{8,7},{9,10},{10,9},{11,... | collective-permute-start | bytes 156680 | tf_op jit(solution)/shard_map/ppermute | solution.py:378
  38.6 15.2 %collective-permute-start.2 = (f32[3,34,128]{2,1,0:T(8,128)S(1)}, f32[3,34,128]{2,1,0:T(8,128)S(1)}, u32[]{:S(2)}, u32[]{:S(2)}) collective-permute-start(f32[3,34,128]{2,1,0:T(8,128)S(1)} %get-tuple-element.15.sent), channel_id=1, source_target_pairs={{0,1},{1,0},{2,3},{3,2},{4,5},{5,4},{6,7},{7,6},{8,9},{9,8},{10,11... | collective-permute-start | bytes 156680 | tf_op jit(solution)/shard_map/ppermute | solution.py:378
  53.8 0.0 collective-permute-done.3.got_b
  53.8 0.9 %collective-permute-done.2.got_a = f32[3,34,128]{2,1,0:T(8,128)S(1)} collective-permute-done((f32[3,34,128]{2,1,0:T(8,128)S(1)}, f32[3,34,128]{2,1,0:T(8,128)S(1)}, u32[]{:S(2)}, u32[]{:S(2)}) %collective-permute-start.2) | collective-permute-done | bytes 52256 | tf_op jit(solution)/shard_map/ppermute | solution.py:378
  54.7 1.0 %finish.1 = f32[3,2048]{1,0:T(4,128)} custom-call(f32[3,34,128]{2,1,0:T(8,128)S(1)} %get-tuple-element.15.sent, f32[3,34,128]{2,1,0:T(8,128)S(1)} %collective-permute-done.2.got_a, f32[3,34,128]{2,1,0:T(8,128)S(1)} %collective-permute-done.3.got_b, f32[3,2048]{1,0:T(4,128)S(1)} %get-tuple-element.16.base, f32[1,256]{1,0:T(1,128)S(1)} %get-tuple-element.17.scale, ...), custom_call_target="tpu_custom_call" | custom-call | flops 1000000 | bytes 4000000 | tf_op jit(solution)/shard_map/finish/pallas_call | solution.py:413
Async XLA Ops:
  0.6 18.4 %copy-start.3 = (f32[3,2048]{1,0:T(4,128)S(1)}, f32[3,2048]{1,0:T(4,128)}, u32[]{:S(2)}) copy-start(f32[3,2048]{1,0:T(4,128)} %vel.5) | copy-start | bytes 73732
  0.6 18.4 %copy-start.4 = (s32[8,2048]{1,0:T(8,128)S(1)}, s32[8,2048]{1,0:T(8,128)}, u32[]{:S(2)}) copy-start(s32[8,2048]{1,0:T(8,128)} %conn.3) | copy-start | bytes 196612
  0.7 20.7 %copy-start.1 = (f32[12,6,2048]{2,1,0:T(8,128)S(1)}, f32[12,6,2048]{2,1,0:T(8,128)}, u32[]{:S(2)}) copy-start(f32[12,6,2048]{2,1,0:T(8,128)} %memory_in.1) | copy-start | bytes 1769476
  0.7 18.3 %copy-start.9 = (s32[256,4]{0,1:T(4,128)S(1)}, s32[256,4]{0,1:T(4,128)}, u32[]{:S(2)}) copy-start(s32[256,4]{0,1:T(4,128)} %param.17) | copy-start | bytes 12292
  0.7 18.3 %copy-start.10 = (f32[256,4]{0,1:T(4,128)S(1)}, f32[256,4]{0,1:T(4,128)}, u32[]{:S(2)}) copy-start(f32[256,4]{0,1:T(4,128)} %param.18) | copy-start | bytes 12292
  2.8 18.3 %collective-permute-start.1 = (f32[7,8,4224]{2,1,0:T(8,128)}, f32[7,8,4224]{2,1,0:T(8,128)S(1)}, u32[]{:S(2)}, u32[]{:S(2)}) collective-permute-start(f32[7,8,4224]{2,1,0:T(8,128)} %pack.1), channel_id=1, source_target_pairs={{1,2},{2,1},{3,4},{4,3},{5,6},{6,5},{7,8},{8,7},{9,10},{10,9},{11,... | collective-permute-start | bytes 2838536 | tf_op jit(solution)/shard_map/ppermute | solution.py:378
  6.6 14.7 %collective-permute-start = (f32[7,8,4224]{2,1,0:T(8,128)}, f32[7,8,4224]{2,1,0:T(8,128)S(1)}, u32[]{:S(2)}, u32[]{:S(2)}) collective-permute-start(f32[7,8,4224]{2,1,0:T(8,128)} %pack.1), channel_id=1, source_target_pairs={{0,1},{1,0},{2,3},{3,2},{4,5},{5,4},{6,7},{7,6},{8,9},{9,8},{10,11... | collective-permute-start | bytes 2838536 | tf_op jit(solution)/shard_map/ppermute | solution.py:378
  19.0 2.3 %copy-start.5 = (f32[32,16]{1,0:T(8,128)S(1)}, f32[32,16]{1,0:T(8,128)}, u32[]{:S(2)}) copy-start(f32[32,16]{1,0:T(8,128)} %constant.5.clone.spread) | copy-start | bytes 6148
  19.0 2.3 %copy-start.6 = (s32[2048]{0:T(1024)S(1)}, s32[2048]{0:T(1024)}, u32[]{:S(2)}) copy-start(s32[2048]{0:T(1024)} %param.21) | copy-start | bytes 24580
  19.1 2.3 %copy-start.7 = (f32[2048]{0:T(1024)S(1)}, f32[2048]{0:T(1024)}, u32[]{:S(2)}) copy-start(f32[2048]{0:T(1024)} %param.27) | copy-start | bytes 24580
  19.1 2.3 %copy-start.8 = (f32[16,32]{1,0:T(8,128)S(1)}, f32[16,32]{1,0:T(8,128)}, u32[]{:S(2)}) copy-start(f32[16,32]{1,0:T(8,128)} %constant.4.clone.strain) | copy-start | bytes 6148
  21.3 0.7 %copy-start.11 = (f32[12,4]{0,1:T(4,128)S(1)}, f32[12,4]{0,1:T(4,128)}, u32[]{:S(2)}) copy-start(f32[12,4]{0,1:T(4,128)} %param.24) | copy-start | bytes 580
  21.3 0.7 %copy-start.12 = (f32[4]{0:T(128)S(1)}, f32[4]{0:T(128)}, u32[]{:S(2)}) copy-start(f32[4]{0:T(128)} %shear.1) | copy-start | bytes 52
  21.3 0.7 %copy-start.13 = (f32[4]{0:T(128)S(1)}, f32[4]{0:T(128)}, u32[]{:S(2)}) copy-start(f32[4]{0:T(128)} %bulk.1) | copy-start | bytes 52
  21.3 0.7 %copy-start.14 = (f32[12]{0:T(128)S(1)}, f32[12]{0:T(128)}, u32[]{:S(2)}) copy-start(f32[12]{0:T(128)} %tau.1) | copy-start | bytes 148
  22.0 6.4 %copy-start = (f32[6,8,4096]{2,1,0:T(8,128)S(1)}, f32[6,8,4096]{2,1,0:T(8,128)}, u32[]{:S(2)}) copy-start(f32[6,8,4096]{2,1,0:T(8,128)} %state.3) | copy-start | bytes 2359300
  22.0 6.4 %copy-start.2 = (f32[8,4096]{1,0:T(8,128)S(1)}, f32[8,4096]{1,0:T(8,128)}, u32[]{:S(2)}) copy-start(f32[8,4096]{1,0:T(8,128)} %stiff.3) | copy-start | bytes 393220
  36.7 17.1 %collective-permute-start.3 = (f32[3,34,128]{2,1,0:T(8,128)S(1)}, f32[3,34,128]{2,1,0:T(8,128)S(1)}, u32[]{:S(2)}, u32[]{:S(2)}) collective-permute-start(f32[3,34,128]{2,1,0:T(8,128)S(1)} %get-tuple-element.15.sent), channel_id=1, source_target_pairs={{1,2},{2,1},{3,4},{4,3},{5,6},{6,5},{7,8},{8,7},{9,10},{10,9},{11,... | collective-permute-start | bytes 156680 | tf_op jit(solution)/shard_map/ppermute | solution.py:378
  38.6 16.1 %collective-permute-start.2 = (f32[3,34,128]{2,1,0:T(8,128)S(1)}, f32[3,34,128]{2,1,0:T(8,128)S(1)}, u32[]{:S(2)}, u32[]{:S(2)}) collective-permute-start(f32[3,34,128]{2,1,0:T(8,128)S(1)} %get-tuple-element.15.sent), channel_id=1, source_target_pairs={{0,1},{1,0},{2,3},{3,2},{4,5},{5,4},{6,7},{7,6},{8,9},{9,8},{10,11... | collective-permute-start | bytes 156680 | tf_op jit(solution)/shard_map/ppermute | solution.py:378

commit v4 on v2

--- a/solution.py
+++ b/solution.py
@@ -1,6 +1,5 @@
 import jax
 import jax.numpy as jnp
-import numpy as np
 from jax import lax
 from jax.experimental import pallas as pl
 from jax.experimental.pallas import tpu as pltpu
@@ -14,24 +13,8 @@
 EDGE = 128
 DEEP = 24
 GROUP = 8
-LO = 256
-HI = 16
-
-
-def strain_rows():
-    table = np.zeros((16, 32), np.float32)
-    for corner in range(8):
-        slopes = [0.25 * ((corner >> direction & 1) * 2 - 1) for direction in range(3)]
-        table[0, corner] = slopes[0]
-        table[1, 8 + corner] = slopes[1]
-        table[2, 16 + corner] = slopes[2]
-        table[3, corner] = slopes[1]
-        table[3, 8 + corner] = slopes[0]
-        table[4, 8 + corner] = slopes[2]
-        table[4, 16 + corner] = slopes[1]
-        table[5, corner] = slopes[2]
-        table[5, 16 + corner] = slopes[0]
-    return table
+LO = 128
+HI = 32
 
 
 def lookup(row, lane):
@@ -177,9 +160,10 @@
             send[c, 0:columns, :] = part if step == 0 else send[c, 0:columns, :] + part
 
 
-def prepare_kernel(vel, conn, src, weight, shear, bulk, prony, tau, out, place, share, gains, lows):
-    elems = conn.shape[1]
+def prepare_kernel(vel, conn, src, weight, shear, bulk, prony, tau, corners, nodes, place, share, gains):
     regions, terms = prony.shape
+    blocks = conn.shape[1] // 128
+    tables = vel.shape[1] // 128
     normed = weight[...] / jnp.sum(weight[...], 0, keepdims=True)
     for half in range(2):
         place[half * 4 : half * 4 + 4, :] = src[:, half * 128 : half * 128 + 128]
@@ -198,21 +182,12 @@
         factor = (1.0 - decay) * span / STEP_BRAIN
         for r in range(regions):
             put(t * regions + r, (2.0 * shear[r] * prony[r, t]) * factor)
-
-    low_rows = lax.broadcasted_iota(jnp.int32, (LO, elems), 0)
-
-    def corner(q, carry):
-        node = conn[pl.ds(q, 1), :]
-        lows[q] = (low_rows == (node & (LO - 1))).astype(jnp.float32).astype(jnp.bfloat16)
-        return carry
-
-    lax.fori_loop(0, 8, corner, 0)
-    blocks = conn.shape[1] // 128
-    tables = vel.shape[1] // 128
-
-    def block(b, carry):
-        here = pl.ds(pl.multiple_of(b * 128, 128), 128)
-        node = conn[:, here]
+    for b in range(blocks):
+        nodes[pl.ds(b, 8, stride=blocks), :] = conn[:, b * 128 : b * 128 + 128]
+
+    def block(i, carry):
+        here = pl.ds(pl.multiple_of(i * 8, 8), 8)
+        node = nodes[here, :]
         lane, row = node & 127, node >> 7
         found = [jnp.zeros((8, 128), jnp.float32) for _ in range(3)]
         for r in range(tables):
@@ -221,8 +196,7 @@
                 value = lookup(vel[c : c + 1, r * 128 : r * 128 + 128], lane)
                 found[c] = jnp.where(mine, value, found[c])
         for c in range(3):
-            out[c * 8 : c * 8 + 8, here] = found[c]
-        out[24:32, here] = jnp.zeros((8, 128), jnp.float32)
+            corners[pl.ds(pl.multiple_of(c * 8 * blocks + i * 8, 8), 8), :] = found[c]
         return carry
 
     lax.fori_loop(0, blocks, block, 0)
@@ -238,11 +212,11 @@
 
 
 def hexes_kernel(
-    got_a, got_b, corners, conn, region, strain, spread, vel, mass, memory_in, gains, lows,
+    got_a, got_b, corners, nodes, region, vel, mass, memory_in, gains,
     memory, base, shared, scale,
     work, rate,
 ):
-    elems = conn.shape[1]
+    elems = memory_in.shape[2]
     terms = memory_in.shape[0]
     regions = (gains.shape[0] // 8 - terms) // (terms + 2)
     blocks = elems // 128
@@ -250,24 +224,40 @@
     ghost = from_next(got_b[0:3, :, lanes:], got_a[0:3, :, lanes:])
     first = base.shape[1] // 128
 
-    def add_shared(b, carry):
-        here = pl.ds(pl.multiple_of(b * 128, 128), 128)
-        node = conn[:, here]
+    def add_shared(i, carry):
+        node = nodes[pl.ds(pl.multiple_of(i * 8, 8), 8), :]
         lane, row = node & 127, node >> 7
         for c in range(3):
-            found = corners[c * 8 : c * 8 + 8, here]
+            here = pl.ds(pl.multiple_of(c * 8 * blocks + i * 8, 8), 8)
+            found = corners[here, :]
             for half in range(2):
-                value = lookup(ghost[c, half : half + 1], lane)
-                found = jnp.where(row == first + half, value, found)
-            work[c * 8 : c * 8 + 8, here] = found
-        work[24:32, here] = jnp.zeros((8, 128), jnp.float32)
+                found = jnp.where(row == first + half, lookup(ghost[c, half : half + 1], lane), found)
+            work[here, :] = found
         return carry
 
-    lax.fori_loop(0, blocks, add_shared, 0, unroll=2)
-    table = strain[...].astype(jnp.bfloat16)
-    rate[...] = STEP_BRAIN * sum(
-        jnp.dot(table, part, preferred_element_type=jnp.float32) for part in in_parts(work[...], 3)
-    )
+    lax.fori_loop(0, blocks, add_shared, 0, unroll=4)
+
+    def dense(c, q):
+        return slice((c * 8 + q) * blocks, (c * 8 + q + 1) * blocks)
+
+    slopes = []
+    for c in range(3):
+        v = [(0.25 * STEP_BRAIN) * work[dense(c, q), :] for q in range(8)]
+        low = [v[q] + v[q + 1] for q in range(0, 8, 2)]
+        along = [v[q + 1] - v[q] for q in range(0, 8, 2)]
+        slopes.append(
+            [
+                (along[0] + along[1]) + (along[2] + along[3]),
+                (low[1] - low[0]) + (low[3] - low[2]),
+                (low[2] + low[3]) - (low[0] + low[1]),
+            ]
+        )
+    strains = [slopes[c][c] for c in range(3)]
+    trace = strains[0] + strains[1] + strains[2]
+    devs = [strain - trace / 3.0 for strain in strains]
+    devs += [0.5 * (slopes[a][b] + slopes[b][a]) for a, b in ((0, 1), (1, 2), (0, 2))]
+    for i, value in enumerate(devs + [trace]):
+        rate[pl.ds(i, blocks, stride=8), :] = value
 
     def gain(index):
         return gains[index * 8 : index * 8 + 6, :]
@@ -276,9 +266,9 @@
 
     def block(b, carry):
         here = pl.ds(pl.multiple_of(b * 128, 128), 128)
-        strains = rate[0:6, here]
-        trace = rate[0:1, here] + rate[1:2, here] + rate[2:3, here]
-        dev = jnp.where(normal, strains - trace / 3.0, 0.5 * strains)
+        mine = pl.multiple_of(b * 8, 8)
+        dev = rate[pl.ds(mine, 6), :]
+        trace = rate[pl.ds(mine + 6, 1), :]
         label = jnp.broadcast_to(region[:, here], (6, 128))
         masks = [label == r for r in range(regions)]
 
@@ -289,39 +279,53 @@
             return chosen
 
         stress = pick(terms) * dev + jnp.where(normal, pick(terms + 1) * trace, 0.0)
+        ready = []
         for t in range(terms):
             new = gain((terms + 2) * regions + t) * memory_in[t, :, here] + pick(t) * dev
-            memory[t, :, here] = new
+            ready.append(new)
             stress = stress + new
-        rate[0:6, here] = jnp.where(label < regions, stress, 0.0)
+        for t in range(terms):
+            memory[t, :, here] = ready[t]
+        rate[pl.ds(mine, 6), :] = jnp.where(label < regions, stress, 0.0)
         return carry
 
     lax.fori_loop(0, blocks, block, 0, unroll=2)
-    rate[6:16, :] = jnp.zeros((10, elems), jnp.float32)
-    table = spread[...].astype(jnp.bfloat16)
-    work[...] = sum(jnp.dot(table, part, preferred_element_type=jnp.float32) for part in in_parts(rate[...], 2))
-
-    high_rows = lax.broadcasted_iota(jnp.int32, (HI, elems), 0)
+    stress = [0.25 * rate[pl.ds(i, blocks, stride=8), :] for i in range(6)]
+    for c, (a, b, d) in enumerate(((0, 3, 5), (3, 1, 4), (5, 4, 2))):
+        plus, minus = stress[a] + stress[b], stress[a] - stress[b]
+        for q, value in ((7, plus + stress[d]), (3, plus - stress[d]), (5, minus + stress[d]), (1, minus - stress[d])):
+            work[dense(c, q), :] = -value
+            work[dense(c, 7 - q), :] = value
+
+    low_rows = lax.broadcasted_iota(jnp.int32, (LO, 128), 0)
+    high_rows = lax.broadcasted_iota(jnp.int32, (HI, 128), 0)
 
     def corner(q, sums):
-        node = conn[pl.ds(q, 1), :]
-        mine = high_rows == (node >> 8)
-        parts = []
-        for c in range(3):
-            parts += in_parts(jnp.where(mine, work[pl.ds(c * 8 + q, 1), :], 0.0), 2)
+        lows, parts = [], [[] for _ in range(6)]
+        for b in range(blocks):
+            node = nodes[pl.ds(q * blocks + b, 1), :]
+            lows.append((low_rows == (node & (LO - 1))).astype(jnp.float32).astype(jnp.bfloat16))
+            mine = high_rows == (node >> 7)
+            for c in range(3):
+                force = jnp.where(mine, work[pl.ds((c * 8 + q) * blocks + b, 1), :], 0.0)
+                for p, part in enumerate(in_parts(force, 2)):
+                    parts[c * 2 + p].append(part)
+        left = jnp.concatenate([jnp.concatenate(row, 1) for row in parts], 0)
         return sums + lax.dot_general(
-            jnp.concatenate(parts, 0), lows[q], (((1,), (1,)), ((), ())), preferred_element_type=jnp.float32
+            left, jnp.concatenate(lows, 1), (((1,), (1,)), ((), ())), preferred_element_type=jnp.float32
         )
 
-    sums = lax.fori_loop(0, 8, corner, jnp.zeros((6 * HI, LO), jnp.float32))
+    sums = lax.fori_loop(0, 8, corner, jnp.zeros((6 * HI, LO), jnp.float32), unroll=2)
     for c in range(3):
         at = c * 2 * HI
         whole = sums[at : at + HI] + sums[at + HI : at + 2 * HI]
-        for h in range(8):
+        for h in range(first):
             here = slice(h * LO, h * LO + LO)
             old = vel[c : c + 1, here]
-            base[c : c + 1, here] = old * (1.0 - COUPLING if h == 7 else 1.0) + STEP_BRAIN * whole[h : h + 1] / mass[:, here]
-        shared[c : c + 1, :] = whole[8:9]
+            kept = 1.0 if h < first - SHARED // LO else 1.0 - COUPLING
+            base[c : c + 1, here] = kept * old + STEP_BRAIN * whole[h : h + 1] / mass[:, here]
+        for half in range(SHARED // LO):
+            shared[c : c + 1, half * LO : half * LO + LO] = whole[first + half : first + half + 1]
     scale[...] = STEP_BRAIN / mass[:, 0:SHARED]
 
 
@@ -383,7 +387,6 @@
 
     field = [scratch(3 * (columns + 2) * DEEP, 128), scratch(3 * columns * DEEP, 128)]
     slabs = field + field + [scratch(columns * DEEP, 128)]
-    table = strain_rows()
 
     package = kernel(
         pack_kernel, shape(7, 8, lanes + EDGE), [hbm, hbm, hbm], hbm,
@@ -391,15 +394,11 @@
     )(skull_state, stiffness, brain_vel)
     got_b, got_a = swap(package)
     gain_rows = ((terms + 2) * regions + terms) * 8
-    corners, place, share, gains, lows = kernel(
+    index = lambda *dims: jax.ShapeDtypeStruct(dims, jnp.int32)
+    blocks = elems // 128
+    corners, dense_nodes, place, share, gains = kernel(
         prepare_kernel,
-        (
-            shape(32, elems),
-            jax.ShapeDtypeStruct((8, 128), jnp.int32),
-            shape(8, 128),
-            shape(gain_rows, 128),
-            jax.ShapeDtypeStruct((8, LO, elems), jnp.bfloat16),
-        ),
+        (shape(24 * blocks, 128), index(8 * blocks, 128), index(8, 128), shape(8, 128), shape(gain_rows, 128)),
         [vmem] * 4 + [smem] * 4,
         [vmem] * 5,
     )(
@@ -409,12 +408,12 @@
     memory, base, shared, scale = kernel(
         hexes_kernel,
         (shape(*prony_state.shape), shape(3, nodes), shape(3, SHARED), shape(1, SHARED)),
-        [vmem] * 12,
+        [vmem] * 9,
         [vmem] * 4,
-        [scratch(32, elems), scratch(16, elems)],
+        [scratch(24 * blocks, 128), scratch(8 * blocks, 128)],
     )(
-        got_a, got_b, corners, connectivity, region.reshape(1, elems), jnp.asarray(table), jnp.asarray(-table.T),
-        brain_vel, node_mass.reshape(1, nodes), prony_state, gains, lows,
+        got_a, got_b, corners, dense_nodes, region.reshape(1, elems),
+        brain_vel, node_mass.reshape(1, nodes), prony_state, gains,
     )
     skull_out, sent = kernel(
         skull_kernel,

time: 59.3 us -> 52.8 us (0.89)
  local copies, waits for them, and re-layouts: 9.55 us -> 1.3 us
  starting transfers between devices: 25.9 us -> 31.6 us
  Pallas kernels: 21.6 us -> 17.9 us
    unnamed x30 -> x26, local copies, waits for them, and re-layouts: 9.55 us -> 1.3 us
    ppermute x2, starting transfers between devices: 20.2 us -> 26 us  [swap(): lax.ppermute(value, 'slab', swap_a)]
    pallas_call x1, Pallas kernels: 6.19 us -> 3.9 us  [on_device(): kernel(hexes_kernel, (shape(*prony_state.shape), shape(3, nodes), shape(3...]
    pallas_call x1, Pallas kernels: 4.03 us -> 2.59 us  [on_device(): kernel(prepare_kernel, (shape(24 * blocks, 128), index(8 * blocks, 128),...]
  transfers between devices with their start and end apart: 4 -> 4, of which waited for: 1 -> 1; matrix products, arithmetic and copies ran while one was open for 0% -> 0% of each run, Pallas kernels for 7% -> 5%
where the time goes in v4:
time: 52.8 us; the launch traced here: 52.5 us
  starting transfers between devices  31.6 us (60%)
  Pallas kernels  17.9 us (34%)
  local copies, waits for them, and re-layouts  1.3 us (2%)
  waiting for transfers between devices  0.87 us (2%)
  between operations  0.84 us (2%)
    ppermute x2, starting transfers between devices, swap(): lax.ppermute(value, 'slab', swap_a)  26 us
    pallas_call x1, Pallas kernels, on_device(): kernel(skull_kernel, (shape(*skull_state.shape), shape(3, columns + 2, 12...  8.25 us
    ppermute x2, starting transfers between devices, swap(): lax.ppermute(value, 'slab', swap_b)  5.67 us
    pallas_call x1, Pallas kernels, on_device(): kernel(hexes_kernel, (shape(*prony_state.shape), shape(3, nodes), shape(3...  3.9 us
    pallas_call x1, Pallas kernels, on_device(): kernel(prepare_kernel, (shape(24 * blocks, 128), index(8 * blocks, 128),...  2.59 us
    pallas_call x1, Pallas kernels, on_device(): kernel(pack_kernel, shape(7, 8, lanes + EDGE), [hbm, hbm, hbm], hbm, [scr...  2.14 us
    unnamed x26, local copies, waits for them, and re-layouts  1.3 us
  transfers between devices with their start and end apart: 4, of which 1 were waited for; matrix products, arithmetic and copies ran while one was open for 0% of the time, Pallas kernels for 5%

profile of v4, /device:TPU:7, one launch (start us, length us, event | category | flops | bytes accessed | tf_op | source)
XLA Modules:
  0.0 52.5 jit_solution(1605009586893776435)
XLA Ops:
  0.6 0.0 copy-start.3
  0.6 0.0 copy-start.4
  0.7 0.0 copy-start.1
  0.7 0.0 copy-start.8
  0.7 0.0 copy-start.9
  0.7 2.1 %pack.1 = f32[7,8,4224]{2,1,0:T(8,128)} custom-call(f32[6,8,4096]{2,1,0:T(8,128)} %state.3, f32[8,4096]{1,0:T(8,128)} %stiff.3, f32[3,2048]{1,0:T(4,128)} %vel.5), custom_call_target="tpu_custom_call" | custom-call | flops 1000000 | bytes 4000000 | tf_op jit(solution)/shard_map/pack/pallas_call | solution.py:391
  2.8 0.0 copy-start.7
  2.8 3.8 %collective-permute-start.1 = (f32[7,8,4224]{2,1,0:T(8,128)}, f32[7,8,4224]{2,1,0:T(8,128)S(1)}, u32[]{:S(2)}, u32[]{:S(2)}) collective-permute-start(f32[7,8,4224]{2,1,0:T(8,128)} %pack.1), channel_id=1, source_target_pairs={{1,2},{2,1},{3,4},{4,3},{5,6},{6,5},{7,8},{8,7},{9,10},{10,9},{11,... | collective-permute-start | bytes 2838536 | tf_op jit(solution)/shard_map/ppermute | solution.py:386
  6.6 12.4 %collective-permute-start = (f32[7,8,4224]{2,1,0:T(8,128)}, f32[7,8,4224]{2,1,0:T(8,128)S(1)}, u32[]{:S(2)}, u32[]{:S(2)}) collective-permute-start(f32[7,8,4224]{2,1,0:T(8,128)} %pack.1), channel_id=1, source_target_pairs={{0,1},{1,0},{2,3},{3,2},{4,5},{5,4},{6,7},{7,6},{8,9},{9,8},{10,11... | collective-permute-start | bytes 2838536 | tf_op jit(solution)/shard_map/ppermute | solution.py:386
  19.0 0.0 copy-start.10
  19.0 0.0 copy-start.11
  19.0 0.0 copy-start.12
  19.0 0.0 copy-done.3
  19.0 0.0 copy-done.4
  19.1 0.0 copy-done.8
  19.1 0.0 copy-done.9
  19.1 0.0 copy-done.7
  19.1 0.6 %copy-done.10 = f32[4]{0:T(128)S(1)} copy-done((f32[4]{0:T(128)S(1)}, f32[4]{0:T(128)}, u32[]{:S(2)}) %copy-start.10) | copy-done | bytes 40
  19.7 0.0 copy-done.11
  19.7 0.0 copy-done.12
  19.7 0.0 copy-start.6
  19.7 2.6 %prepare.1 = (f32[384,128]{1,0:T(8,128)S(1)}, s32[128,128]{1,0:T(8,128)S(1)}, s32[8,128]{1,0:T(8,128)S(1)}, f32[8,128]{1,0:T(8,128)S(1)}, f32[544,128]{1,0:T(8,128)S(1)}) custom-call(f32[3,2048]{1,0:T(4,128)S(1)} %copy-done.3, s32[8,2048]{1,0:T(8,128)S(1)} %copy-done.4, s32[4,256]{1,0:T(4,128)S(1)} %bitcast.7, f32[4,256]{1,0:T(4,128)S(1)} %bitcast.8, ...), custom_call_target="tpu_custom_call" | custom-call | flops 1000000 | bytes 4000000 | tf_op jit(solution)/shard_map/prepare/pallas_call | solution.py:399
  22.3 0.0 copy-start.5
  22.3 0.0 collective-permute-done.1.got_b
  22.3 0.0 collective-permute-done.got_a
  22.3 0.0 copy-done.1
  22.3 0.0 copy-done.6
  22.3 0.6 %copy-done.5 = s32[2048]{0:T(1024)S(1)} copy-done((s32[2048]{0:T(1024)S(1)}, s32[2048]{0:T(1024)}, u32[]{:S(2)}) %copy-start.5) | copy-done | bytes 8216
  23.0 0.0 copy-start
  23.0 0.0 copy-start.2
  23.0 3.9 %hexes.1 = (f32[12,6,2048]{2,1,0:T(8,128)}, f32[3,2048]{1,0:T(4,128)S(1)}, f32[3,256]{1,0:T(4,128)S(1)}, f32[1,256]{1,0:T(1,128)S(1)}) custom-call(f32[7,8,4224]{2,1,0:T(8,128)S(1)} %collective-permute-done.got_a, f32[7,8,4224]{2,1,0:T(8,128)S(1)} %collective-permute-done.1.got_b, f32[384,128]{1,0:T(8,128)S(1)} %get-tuple-element.14.corners, ...), custom_call_target="tpu_custom_call" | custom-call | flops 1000000 | bytes 4000000 | tf_op jit(solution)/shard_map/hexes/pallas_call | solution.py:408
  26.9 0.0 copy-done
  26.9 0.0 copy-done.2
  26.9 8.2 %skull.1 = (f32[6,8,4096]{2,1,0:T(8,128)}, f32[3,34,128]{2,1,0:T(8,128)S(1)}) custom-call(f32[6,8,4096]{2,1,0:T(8,128)S(1)} %copy-done, f32[8,4096]{1,0:T(8,128)S(1)} %copy-done.2, f32[7,8,4224]{2,1,0:T(8,128)S(1)} %collective-permute-done.got_a, f32[7,8,4224]{2,1,0:T(8,128)S(1)} %collective-permute-done.1.got_b, f32[3,256]{1,0:T(4,128)S(1)} %get-tuple-element.17.shared), custom_call_target="tpu_custom_call" | custom-call | flops 1000000 | bytes 4000000 | tf_op jit(solution)/shard_map/skull/pallas_call | solution.py:418
  35.2 1.9 %collective-permute-start.3 = (f32[3,34,128]{2,1,0:T(8,128)S(1)}, f32[3,34,128]{2,1,0:T(8,128)S(1)}, u32[]{:S(2)}, u32[]{:S(2)}) collective-permute-start(f32[3,34,128]{2,1,0:T(8,128)S(1)} %get-tuple-element.19.sent), channel_id=1, source_target_pairs={{1,2},{2,1},{3,4},{4,3},{5,6},{6,5},{7,8},{8,7},{9,10},{10,9},{11,... | collective-permute-start | bytes 156680 | tf_op jit(solution)/shard_map/ppermute | solution.py:386
  37.1 13.6 %collective-permute-start.2 = (f32[3,34,128]{2,1,0:T(8,128)S(1)}, f32[3,34,128]{2,1,0:T(8,128)S(1)}, u32[]{:S(2)}, u32[]{:S(2)}) collective-permute-start(f32[3,34,128]{2,1,0:T(8,128)S(1)} %get-tuple-element.19.sent), channel_id=1, source_target_pairs={{0,1},{1,0},{2,3},{3,2},{4,5},{5,4},{6,7},{7,6},{8,9},{9,8},{10,11... | collective-permute-start | bytes 156680 | tf_op jit(solution)/shard_map/ppermute | solution.py:386
  50.7 0.0 collective-permute-done.3.got_b
  50.7 0.9 %collective-permute-done.2.got_a = f32[3,34,128]{2,1,0:T(8,128)S(1)} collective-permute-done((f32[3,34,128]{2,1,0:T(8,128)S(1)}, f32[3,34,128]{2,1,0:T(8,128)S(1)}, u32[]{:S(2)}, u32[]{:S(2)}) %collective-permute-start.2) | collective-permute-done | bytes 52256 | tf_op jit(solution)/shard_map/ppermute | solution.py:386
  51.5 1.0 %finish.1 = f32[3,2048]{1,0:T(4,128)} custom-call(f32[3,34,128]{2,1,0:T(8,128)S(1)} %get-tuple-element.19.sent, f32[3,34,128]{2,1,0:T(8,128)S(1)} %collective-permute-done.2.got_a, f32[3,34,128]{2,1,0:T(8,128)S(1)} %collective-permute-done.3.got_b, f32[3,2048]{1,0:T(4,128)S(1)} %get-tuple-element.20.base, f32[1,256]{1,0:T(1,128)S(1)} %get-tuple-element.21.scale, ...), custom_call_target="tpu_custom_call" | custom-call | flops 1000000 | bytes 4000000 | tf_op jit(solution)/shard_map/finish/pallas_call | solution.py:426
Async XLA Ops:
  0.6 18.4 %copy-start.3 = (f32[3,2048]{1,0:T(4,128)S(1)}, f32[3,2048]{1,0:T(4,128)}, u32[]{:S(2)}) copy-start(f32[3,2048]{1,0:T(4,128)} %vel.5) | copy-start | bytes 73732
  0.6 18.4 %copy-start.4 = (s32[8,2048]{1,0:T(8,128)S(1)}, s32[8,2048]{1,0:T(8,128)}, u32[]{:S(2)}) copy-start(s32[8,2048]{1,0:T(8,128)} %conn.1) | copy-start | bytes 196612
  0.7 21.7 %copy-start.1 = (f32[12,6,2048]{2,1,0:T(8,128)S(1)}, f32[12,6,2048]{2,1,0:T(8,128)}, u32[]{:S(2)}) copy-start(f32[12,6,2048]{2,1,0:T(8,128)} %memory_in.1) | copy-start | bytes 1769476
  0.7 18.4 %copy-start.8 = (f32[256,4]{0,1:T(4,128)S(1)}, f32[256,4]{0,1:T(4,128)}, u32[]{:S(2)}) copy-start(f32[256,4]{0,1:T(4,128)} %param.16) | copy-start | bytes 12292
  0.7 18.4 %copy-start.9 = (f32[12,4]{0,1:T(4,128)S(1)}, f32[12,4]{0,1:T(4,128)}, u32[]{:S(2)}) copy-start(f32[12,4]{0,1:T(4,128)} %param.22) | copy-start | bytes 580
  2.8 16.2 %copy-start.7 = (s32[256,4]{0,1:T(4,128)S(1)}, s32[256,4]{0,1:T(4,128)}, u32[]{:S(2)}) copy-start(s32[256,4]{0,1:T(4,128)} %param.15) | copy-start | bytes 12292
  2.8 19.5 %collective-permute-start.1 = (f32[7,8,4224]{2,1,0:T(8,128)}, f32[7,8,4224]{2,1,0:T(8,128)S(1)}, u32[]{:S(2)}, u32[]{:S(2)}) collective-permute-start(f32[7,8,4224]{2,1,0:T(8,128)} %pack.1), channel_id=1, source_target_pairs={{1,2},{2,1},{3,4},{4,3},{5,6},{6,5},{7,8},{8,7},{9,10},{10,9},{11,... | collective-permute-start | bytes 2838536 | tf_op jit(solution)/shard_map/ppermute | solution.py:386
  6.6 15.7 %collective-permute-start = (f32[7,8,4224]{2,1,0:T(8,128)}, f32[7,8,4224]{2,1,0:T(8,128)S(1)}, u32[]{:S(2)}, u32[]{:S(2)}) collective-permute-start(f32[7,8,4224]{2,1,0:T(8,128)} %pack.1), channel_id=1, source_target_pairs={{0,1},{1,0},{2,3},{3,2},{4,5},{5,4},{6,7},{7,6},{8,9},{9,8},{10,11... | collective-permute-start | bytes 2838536 | tf_op jit(solution)/shard_map/ppermute | solution.py:386
  19.0 0.7 %copy-start.10 = (f32[4]{0:T(128)S(1)}, f32[4]{0:T(128)}, u32[]{:S(2)}) copy-start(f32[4]{0:T(128)} %shear.1) | copy-start | bytes 52
  19.0 0.7 %copy-start.11 = (f32[4]{0:T(128)S(1)}, f32[4]{0:T(128)}, u32[]{:S(2)}) copy-start(f32[4]{0:T(128)} %bulk.1) | copy-start | bytes 52
  19.0 0.7 %copy-start.12 = (f32[12]{0:T(128)S(1)}, f32[12]{0:T(128)}, u32[]{:S(2)}) copy-start(f32[12]{0:T(128)} %tau.1) | copy-start | bytes 148
  19.7 2.6 %copy-start.6 = (f32[2048]{0:T(1024)S(1)}, f32[2048]{0:T(1024)}, u32[]{:S(2)}) copy-start(f32[2048]{0:T(1024)} %param.25) | copy-start | bytes 24580
  22.3 0.7 %copy-start.5 = (s32[2048]{0:T(1024)S(1)}, s32[2048]{0:T(1024)}, u32[]{:S(2)}) copy-start(s32[2048]{0:T(1024)} %param.19) | copy-start | bytes 24580
  23.0 3.9 %copy-start = (f32[6,8,4096]{2,1,0:T(8,128)S(1)}, f32[6,8,4096]{2,1,0:T(8,128)}, u32[]{:S(2)}) copy-start(f32[6,8,4096]{2,1,0:T(8,128)} %state.3) | copy-start | bytes 2359300
  23.0 3.9 %copy-start.2 = (f32[8,4096]{1,0:T(8,128)S(1)}, f32[8,4096]{1,0:T(8,128)}, u32[]{:S(2)}) copy-start(f32[8,4096]{1,0:T(8,128)} %stiff.3) | copy-start | bytes 393220
  35.2 15.5 %collective-permute-start.3 = (f32[3,34,128]{2,1,0:T(8,128)S(1)}, f32[3,34,128]{2,1,0:T(8,128)S(1)}, u32[]{:S(2)}, u32[]{:S(2)}) collective-permute-start(f32[3,34,128]{2,1,0:T(8,128)S(1)} %get-tuple-element.19.sent), channel_id=1, source_target_pairs={{1,2},{2,1},{3,4},{4,3},{5,6},{6,5},{7,8},{8,7},{9,10},{10,9},{11,... | collective-permute-start | bytes 156680 | tf_op jit(solution)/shard_map/ppermute | solution.py:386
  37.1 14.5 %collective-permute-start.2 = (f32[3,34,128]{2,1,0:T(8,128)S(1)}, f32[3,34,128]{2,1,0:T(8,128)S(1)}, u32[]{:S(2)}, u32[]{:S(2)}) collective-permute-start(f32[3,34,128]{2,1,0:T(8,128)S(1)} %get-tuple-element.19.sent), channel_id=1, source_target_pairs={{0,1},{1,0},{2,3},{3,2},{4,5},{5,4},{6,7},{7,6},{8,9},{9,8},{10,11... | collective-permute-start | bytes 156680 | tf_op jit(solution)/shard_map/ppermute | solution.py:386

commit v5 on v4

--- a/solution.py
+++ b/solution.py
@@ -62,10 +62,13 @@
 
     def column(j, carry):
         here = pl.ds(pl.multiple_of(j * 128, 128), 128)
+        values = []
         for c in range(7):
             own = state[c, :, here] if c < 6 else stiff[:, here]
             b, a = got_b[c, :, here], got_a[c, :, here]
-            for slab, value in enumerate((from_previous(b, a), own, from_next(b, a))):
+            values.append((from_previous(b, a), own, from_next(b, a)))
+        for c in range(7):
+            for slab, value in enumerate(values[c]):
                 at = slab * 8
                 if c < 3:
                     d[pl.ds(pl.multiple_of((c * (columns + 2) + 1 + j) * DEEP + at, 8), 8), :] = value
@@ -96,9 +99,9 @@
             start = pl.multiple_of(g * (GROUP * DEEP), 8) + (column * DEEP + row)
             return ref[pl.ds(start, 8), :]
 
+        ready = []
         for w in windows:
             stiffs = [at(k, i, w) for i in range(GROUP)]
-            ready = []
             for c in range(3):
                 base = c * (columns + 2)
                 middles = [at(d, base + i, w) for i in range(GROUP + 2)]
@@ -114,8 +117,8 @@
                     old = at(v, c * columns + i, w)
                     new = old + (stiffs[i] * laplace - DAMPING * old)
                     ready.append((w, c, g, i, middle + new, new))
-            for item in ready:
-                emit(*item)
+        for item in ready:
+            emit(*item)
         return carry
 
     lax.fori_loop(0, columns // GROUP, group, 0)

time: 52.8 us -> 52.8 us (level)
  no operation moved by 1% of the time
where the time goes in v5:
time: 52.8 us; the launch traced here: 52.5 us
  starting transfers between devices  31.6 us (60%)
  Pallas kernels  17.9 us (34%)
  local copies, waits for them, and re-layouts  1.3 us (2%)
  waiting for transfers between devices  0.87 us (2%)
  between operations  0.84 us (2%)
    ppermute x2, starting transfers between devices, swap(): lax.ppermute(value, 'slab', swap_a)  26 us
    pallas_call x1, Pallas kernels, on_device(): kernel(skull_kernel, (shape(*skull_state.shape), shape(3, columns + 2, 12...  8.25 us
    ppermute x2, starting transfers between devices, swap(): lax.ppermute(value, 'slab', swap_b)  5.67 us
    pallas_call x1, Pallas kernels, on_device(): kernel(hexes_kernel, (shape(*prony_state.shape), shape(3, nodes), shape(3...  3.9 us
    pallas_call x1, Pallas kernels, on_device(): kernel(prepare_kernel, (shape(24 * blocks, 128), index(8 * blocks, 128),...  2.59 us
    pallas_call x1, Pallas kernels, on_device(): kernel(pack_kernel, shape(7, 8, lanes + EDGE), [hbm, hbm, hbm], hbm, [scr...  2.14 us
    unnamed x26, local copies, waits for them, and re-layouts  1.3 us
  transfers between devices with their start and end apart: 4, of which 1 were waited for; matrix products, arithmetic and copies ran while one was open for 0% of the time, Pallas kernels for 5%

profile of v5, /device:TPU:7, one launch (start us, length us, event | category | flops | bytes accessed | tf_op | source)
XLA Modules:
  0.0 52.5 jit_solution(12578906105280823693)
XLA Ops:
  0.6 0.0 copy-start.3
  0.6 0.0 copy-start.4
  0.7 0.0 copy-start.1
  0.7 0.0 copy-start.8
  0.7 0.0 copy-start.9
  0.7 2.1 %pack.1 = f32[7,8,4224]{2,1,0:T(8,128)} custom-call(f32[6,8,4096]{2,1,0:T(8,128)} %state.3, f32[8,4096]{1,0:T(8,128)} %stiff.3, f32[3,2048]{1,0:T(4,128)} %vel.5), custom_call_target="tpu_custom_call" | custom-call | flops 1000000 | bytes 4000000 | tf_op jit(solution)/shard_map/pack/pallas_call | solution.py:394
  2.8 0.0 copy-start.7
  2.8 3.8 %collective-permute-start.1 = (f32[7,8,4224]{2,1,0:T(8,128)}, f32[7,8,4224]{2,1,0:T(8,128)S(1)}, u32[]{:S(2)}, u32[]{:S(2)}) collective-permute-start(f32[7,8,4224]{2,1,0:T(8,128)} %pack.1), channel_id=1, source_target_pairs={{1,2},{2,1},{3,4},{4,3},{5,6},{6,5},{7,8},{8,7},{9,10},{10,9},{11,... | collective-permute-start | bytes 2838536 | tf_op jit(solution)/shard_map/ppermute | solution.py:389
  6.6 12.4 %collective-permute-start = (f32[7,8,4224]{2,1,0:T(8,128)}, f32[7,8,4224]{2,1,0:T(8,128)S(1)}, u32[]{:S(2)}, u32[]{:S(2)}) collective-permute-start(f32[7,8,4224]{2,1,0:T(8,128)} %pack.1), channel_id=1, source_target_pairs={{0,1},{1,0},{2,3},{3,2},{4,5},{5,4},{6,7},{7,6},{8,9},{9,8},{10,11... | collective-permute-start | bytes 2838536 | tf_op jit(solution)/shard_map/ppermute | solution.py:389
  19.0 0.0 copy-start.10
  19.0 0.0 copy-start.11
  19.0 0.0 copy-start.12
  19.0 0.0 copy-done.3
  19.0 0.0 copy-done.4
  19.1 0.0 copy-done.8
  19.1 0.0 copy-done.9
  19.1 0.0 copy-done.7
  19.1 0.6 %copy-done.10 = f32[4]{0:T(128)S(1)} copy-done((f32[4]{0:T(128)S(1)}, f32[4]{0:T(128)}, u32[]{:S(2)}) %copy-start.10) | copy-done | bytes 40
  19.7 0.0 copy-done.11
  19.7 0.0 copy-done.12
  19.7 0.0 copy-start.6
  19.7 2.6 %prepare.1 = (f32[384,128]{1,0:T(8,128)S(1)}, s32[128,128]{1,0:T(8,128)S(1)}, s32[8,128]{1,0:T(8,128)S(1)}, f32[8,128]{1,0:T(8,128)S(1)}, f32[544,128]{1,0:T(8,128)S(1)}) custom-call(f32[3,2048]{1,0:T(4,128)S(1)} %copy-done.3, s32[8,2048]{1,0:T(8,128)S(1)} %copy-done.4, s32[4,256]{1,0:T(4,128)S(1)} %bitcast.7, f32[4,256]{1,0:T(4,128)S(1)} %bitcast.8, ...), custom_call_target="tpu_custom_call" | custom-call | flops 1000000 | bytes 4000000 | tf_op jit(solution)/shard_map/prepare/pallas_call | solution.py:402
  22.3 0.0 copy-start.5
  22.3 0.0 collective-permute-done.1.got_b
  22.3 0.0 collective-permute-done.got_a
  22.3 0.0 copy-done.1
  22.3 0.0 copy-done.6
  22.3 0.6 %copy-done.5 = s32[2048]{0:T(1024)S(1)} copy-done((s32[2048]{0:T(1024)S(1)}, s32[2048]{0:T(1024)}, u32[]{:S(2)}) %copy-start.5) | copy-done | bytes 8216
  23.0 0.0 copy-start
  23.0 0.0 copy-start.2
  23.0 3.9 %hexes.1 = (f32[12,6,2048]{2,1,0:T(8,128)}, f32[3,2048]{1,0:T(4,128)S(1)}, f32[3,256]{1,0:T(4,128)S(1)}, f32[1,256]{1,0:T(1,128)S(1)}) custom-call(f32[7,8,4224]{2,1,0:T(8,128)S(1)} %collective-permute-done.got_a, f32[7,8,4224]{2,1,0:T(8,128)S(1)} %collective-permute-done.1.got_b, f32[384,128]{1,0:T(8,128)S(1)} %get-tuple-element.14.corners, ...), custom_call_target="tpu_custom_call" | custom-call | flops 1000000 | bytes 4000000 | tf_op jit(solution)/shard_map/hexes/pallas_call | solution.py:411
  26.9 0.0 copy-done
  26.9 0.0 copy-done.2
  26.9 8.3 %skull.1 = (f32[6,8,4096]{2,1,0:T(8,128)}, f32[3,34,128]{2,1,0:T(8,128)S(1)}) custom-call(f32[6,8,4096]{2,1,0:T(8,128)S(1)} %copy-done, f32[8,4096]{1,0:T(8,128)S(1)} %copy-done.2, f32[7,8,4224]{2,1,0:T(8,128)S(1)} %collective-permute-done.got_a, f32[7,8,4224]{2,1,0:T(8,128)S(1)} %collective-permute-done.1.got_b, f32[3,256]{1,0:T(4,128)S(1)} %get-tuple-element.17.shared), custom_call_target="tpu_custom_call" | custom-call | flops 1000000 | bytes 4000000 | tf_op jit(solution)/shard_map/skull/pallas_call | solution.py:421
  35.2 1.9 %collective-permute-start.3 = (f32[3,34,128]{2,1,0:T(8,128)S(1)}, f32[3,34,128]{2,1,0:T(8,128)S(1)}, u32[]{:S(2)}, u32[]{:S(2)}) collective-permute-start(f32[3,34,128]{2,1,0:T(8,128)S(1)} %get-tuple-element.19.sent), channel_id=1, source_target_pairs={{1,2},{2,1},{3,4},{4,3},{5,6},{6,5},{7,8},{8,7},{9,10},{10,9},{11,... | collective-permute-start | bytes 156680 | tf_op jit(solution)/shard_map/ppermute | solution.py:389
  37.1 13.6 %collective-permute-start.2 = (f32[3,34,128]{2,1,0:T(8,128)S(1)}, f32[3,34,128]{2,1,0:T(8,128)S(1)}, u32[]{:S(2)}, u32[]{:S(2)}) collective-permute-start(f32[3,34,128]{2,1,0:T(8,128)S(1)} %get-tuple-element.19.sent), channel_id=1, source_target_pairs={{0,1},{1,0},{2,3},{3,2},{4,5},{5,4},{6,7},{7,6},{8,9},{9,8},{10,11... | collective-permute-start | bytes 156680 | tf_op jit(solution)/shard_map/ppermute | solution.py:389
  50.7 0.0 collective-permute-done.3.got_b
  50.7 0.9 %collective-permute-done.2.got_a = f32[3,34,128]{2,1,0:T(8,128)S(1)} collective-permute-done((f32[3,34,128]{2,1,0:T(8,128)S(1)}, f32[3,34,128]{2,1,0:T(8,128)S(1)}, u32[]{:S(2)}, u32[]{:S(2)}) %collective-permute-start.2) | collective-permute-done | bytes 52256 | tf_op jit(solution)/shard_map/ppermute | solution.py:389
  51.5 1.0 %finish.1 = f32[3,2048]{1,0:T(4,128)} custom-call(f32[3,34,128]{2,1,0:T(8,128)S(1)} %get-tuple-element.19.sent, f32[3,34,128]{2,1,0:T(8,128)S(1)} %collective-permute-done.2.got_a, f32[3,34,128]{2,1,0:T(8,128)S(1)} %collective-permute-done.3.got_b, f32[3,2048]{1,0:T(4,128)S(1)} %get-tuple-element.20.base, f32[1,256]{1,0:T(1,128)S(1)} %get-tuple-element.21.scale, ...), custom_call_target="tpu_custom_call" | custom-call | flops 1000000 | bytes 4000000 | tf_op jit(solution)/shard_map/finish/pallas_call | solution.py:429
Async XLA Ops:
  0.6 18.4 %copy-start.3 = (f32[3,2048]{1,0:T(4,128)S(1)}, f32[3,2048]{1,0:T(4,128)}, u32[]{:S(2)}) copy-start(f32[3,2048]{1,0:T(4,128)} %vel.5) | copy-start | bytes 73732
  0.6 18.4 %copy-start.4 = (s32[8,2048]{1,0:T(8,128)S(1)}, s32[8,2048]{1,0:T(8,128)}, u32[]{:S(2)}) copy-start(s32[8,2048]{1,0:T(8,128)} %conn.1) | copy-start | bytes 196612
  0.7 21.7 %copy-start.1 = (f32[12,6,2048]{2,1,0:T(8,128)S(1)}, f32[12,6,2048]{2,1,0:T(8,128)}, u32[]{:S(2)}) copy-start(f32[12,6,2048]{2,1,0:T(8,128)} %memory_in.1) | copy-start | bytes 1769476
  0.7 18.4 %copy-start.8 = (f32[256,4]{0,1:T(4,128)S(1)}, f32[256,4]{0,1:T(4,128)}, u32[]{:S(2)}) copy-start(f32[256,4]{0,1:T(4,128)} %param.16) | copy-start | bytes 12292
  0.7 18.4 %copy-start.9 = (f32[12,4]{0,1:T(4,128)S(1)}, f32[12,4]{0,1:T(4,128)}, u32[]{:S(2)}) copy-start(f32[12,4]{0,1:T(4,128)} %param.22) | copy-start | bytes 580
  2.8 16.2 %copy-start.7 = (s32[256,4]{0,1:T(4,128)S(1)}, s32[256,4]{0,1:T(4,128)}, u32[]{:S(2)}) copy-start(s32[256,4]{0,1:T(4,128)} %param.15) | copy-start | bytes 12292
  2.8 19.5 %collective-permute-start.1 = (f32[7,8,4224]{2,1,0:T(8,128)}, f32[7,8,4224]{2,1,0:T(8,128)S(1)}, u32[]{:S(2)}, u32[]{:S(2)}) collective-permute-start(f32[7,8,4224]{2,1,0:T(8,128)} %pack.1), channel_id=1, source_target_pairs={{1,2},{2,1},{3,4},{4,3},{5,6},{6,5},{7,8},{8,7},{9,10},{10,9},{11,... | collective-permute-start | bytes 2838536 | tf_op jit(solution)/shard_map/ppermute | solution.py:389
  6.6 15.7 %collective-permute-start = (f32[7,8,4224]{2,1,0:T(8,128)}, f32[7,8,4224]{2,1,0:T(8,128)S(1)}, u32[]{:S(2)}, u32[]{:S(2)}) collective-permute-start(f32[7,8,4224]{2,1,0:T(8,128)} %pack.1), channel_id=1, source_target_pairs={{0,1},{1,0},{2,3},{3,2},{4,5},{5,4},{6,7},{7,6},{8,9},{9,8},{10,11... | collective-permute-start | bytes 2838536 | tf_op jit(solution)/shard_map/ppermute | solution.py:389
  19.0 0.7 %copy-start.10 = (f32[4]{0:T(128)S(1)}, f32[4]{0:T(128)}, u32[]{:S(2)}) copy-start(f32[4]{0:T(128)} %shear.1) | copy-start | bytes 52
  19.0 0.7 %copy-start.11 = (f32[4]{0:T(128)S(1)}, f32[4]{0:T(128)}, u32[]{:S(2)}) copy-start(f32[4]{0:T(128)} %bulk.1) | copy-start | bytes 52
  19.0 0.7 %copy-start.12 = (f32[12]{0:T(128)S(1)}, f32[12]{0:T(128)}, u32[]{:S(2)}) copy-start(f32[12]{0:T(128)} %tau.1) | copy-start | bytes 148
  19.7 2.6 %copy-start.6 = (f32[2048]{0:T(1024)S(1)}, f32[2048]{0:T(1024)}, u32[]{:S(2)}) copy-start(f32[2048]{0:T(1024)} %param.25) | copy-start | bytes 24580
  22.3 0.7 %copy-start.5 = (s32[2048]{0:T(1024)S(1)}, s32[2048]{0:T(1024)}, u32[]{:S(2)}) copy-start(s32[2048]{0:T(1024)} %param.19) | copy-start | bytes 24580
  23.0 3.9 %copy-start = (f32[6,8,4096]{2,1,0:T(8,128)S(1)}, f32[6,8,4096]{2,1,0:T(8,128)}, u32[]{:S(2)}) copy-start(f32[6,8,4096]{2,1,0:T(8,128)} %state.3) | copy-start | bytes 2359300
  23.0 3.9 %copy-start.2 = (f32[8,4096]{1,0:T(8,128)S(1)}, f32[8,4096]{1,0:T(8,128)}, u32[]{:S(2)}) copy-start(f32[8,4096]{1,0:T(8,128)} %stiff.3) | copy-start | bytes 393220
  35.2 15.5 %collective-permute-start.3 = (f32[3,34,128]{2,1,0:T(8,128)S(1)}, f32[3,34,128]{2,1,0:T(8,128)S(1)}, u32[]{:S(2)}, u32[]{:S(2)}) collective-permute-start(f32[3,34,128]{2,1,0:T(8,128)S(1)} %get-tuple-element.19.sent), channel_id=1, source_target_pairs={{1,2},{2,1},{3,4},{4,3},{5,6},{6,5},{7,8},{8,7},{9,10},{10,9},{11,... | collective-permute-start | bytes 156680 | tf_op jit(solution)/shard_map/ppermute | solution.py:389
  37.1 14.5 %collective-permute-start.2 = (f32[3,34,128]{2,1,0:T(8,128)S(1)}, f32[3,34,128]{2,1,0:T(8,128)S(1)}, u32[]{:S(2)}, u32[]{:S(2)}) collective-permute-start(f32[3,34,128]{2,1,0:T(8,128)S(1)} %get-tuple-element.19.sent), channel_id=1, source_target_pairs={{0,1},{1,0},{2,3},{3,2},{4,5},{5,4},{6,7},{7,6},{8,9},{9,8},{10,11... | collective-permute-start | bytes 156680 | tf_op jit(solution)/shard_map/ppermute | solution.py:389

commit v6 on v5

--- a/solution.py
+++ b/solution.py
@@ -12,7 +12,7 @@
 COUPLING = 0.5
 EDGE = 128
 DEEP = 24
-GROUP = 8
+GROUP = 16
 LO = 128
 HI = 32
 
@@ -99,10 +99,9 @@
             start = pl.multiple_of(g * (GROUP * DEEP), 8) + (column * DEEP + row)
             return ref[pl.ds(start, 8), :]
 
-        ready = []
         for w in windows:
-            stiffs = [at(k, i, w) for i in range(GROUP)]
             for c in range(3):
+                ready = []
                 base = c * (columns + 2)
                 middles = [at(d, base + i, w) for i in range(GROUP + 2)]
                 ahead = [pltpu.roll(m, 1, 1) for m in middles[:-1]]
@@ -115,10 +114,10 @@
                     below = at(d, base + i + 1, w + 1)
                     laplace = (below + above) + (left + right) - 4.0 * middle
                     old = at(v, c * columns + i, w)
-                    new = old + (stiffs[i] * laplace - DAMPING * old)
+                    new = old + (at(k, i, w) * laplace - DAMPING * old)
                     ready.append((w, c, g, i, middle + new, new))
-        for item in ready:
-            emit(*item)
+                for item in ready:
+                    emit(*item)
         return carry
 
     lax.fori_loop(0, columns // GROUP, group, 0)
@@ -292,7 +291,7 @@
         rate[pl.ds(mine, 6), :] = jnp.where(label < regions, stress, 0.0)
         return carry
 
-    lax.fori_loop(0, blocks, block, 0, unroll=2)
+    lax.fori_loop(0, blocks, block, 0, unroll=4)
     stress = [0.25 * rate[pl.ds(i, blocks, stride=8), :] for i in range(6)]
     for c, (a, b, d) in enumerate(((0, 3, 5), (3, 1, 4), (5, 4, 2))):
         plus, minus = stress[a] + stress[b], stress[a] - stress[b]
@@ -318,7 +317,7 @@
             left, jnp.concatenate(lows, 1), (((1,), (1,)), ((), ())), preferred_element_type=jnp.float32
         )
 
-    sums = lax.fori_loop(0, 8, corner, jnp.zeros((6 * HI, LO), jnp.float32), unroll=2)
+    sums = lax.fori_loop(0, 8, corner, jnp.zeros((6 * HI, LO), jnp.float32), unroll=4)
     for c in range(3):
         at = c * 2 * HI
         whole = sums[at : at + HI] + sums[at + HI : at + 2 * HI]

time: 52.8 us -> 51.4 us (0.973)
  Pallas kernels: 17.9 us -> 16.5 us
    pallas_call x1, Pallas kernels: 8.25 us -> 7.54 us  [on_device(): kernel(skull_kernel, (shape(*skull_state.shape), shape(3, columns + 2, 12...]
    pallas_call x1, Pallas kernels: 3.9 us -> 3.2 us  [on_device(): kernel(hexes_kernel, (shape(*prony_state.shape), shape(3, nodes), shape(3...]
where the time goes in v6:
time: 51.4 us; the launch traced here: 51.1 us
  starting transfers between devices  31.6 us (61%)
  Pallas kernels  16.5 us (32%)
  local copies, waits for them, and re-layouts  1.3 us (3%)
  waiting for transfers between devices  0.87 us (2%)
  between operations  0.86 us (2%)
    ppermute x2, starting transfers between devices, swap(): lax.ppermute(value, 'slab', swap_a)  26 us
    pallas_call x1, Pallas kernels, on_device(): kernel(skull_kernel, (shape(*skull_state.shape), shape(3, columns + 2, 12...  7.54 us
    ppermute x2, starting transfers between devices, swap(): lax.ppermute(value, 'slab', swap_b)  5.67 us
    pallas_call x1, Pallas kernels, on_device(): kernel(hexes_kernel, (shape(*prony_state.shape), shape(3, nodes), shape(3...  3.2 us
    pallas_call x1, Pallas kernels, on_device(): kernel(prepare_kernel, (shape(24 * blocks, 128), index(8 * blocks, 128),...  2.59 us
    pallas_call x1, Pallas kernels, on_device(): kernel(pack_kernel, shape(7, 8, lanes + EDGE), [hbm, hbm, hbm], hbm, [scr...  2.14 us
    unnamed x26, local copies, waits for them, and re-layouts  1.3 us
  transfers between devices with their start and end apart: 4, of which 1 were waited for; matrix products, arithmetic and copies ran while one was open for 0% of the time, Pallas kernels for 5%

profile of v6, /device:TPU:7, one launch (start us, length us, event | category | flops | bytes accessed | tf_op | source)
XLA Modules:
  0.0 51.1 jit_solution(14297850509696608743)
XLA Ops:
  0.6 0.0 copy-start.3
  0.6 0.0 copy-start.4
  0.7 0.0 copy-start.1
  0.7 0.0 copy-start.8
  0.7 0.0 copy-start.9
  0.7 2.1 %pack.1 = f32[7,8,4224]{2,1,0:T(8,128)} custom-call(f32[6,8,4096]{2,1,0:T(8,128)} %state.3, f32[8,4096]{1,0:T(8,128)} %stiff.3, f32[3,2048]{1,0:T(4,128)} %vel.5), custom_call_target="tpu_custom_call" | custom-call | flops 1000000 | bytes 4000000 | tf_op jit(solution)/shard_map/pack/pallas_call | solution.py:393
  2.8 0.0 copy-start.7
  2.8 3.8 %collective-permute-start.1 = (f32[7,8,4224]{2,1,0:T(8,128)}, f32[7,8,4224]{2,1,0:T(8,128)S(1)}, u32[]{:S(2)}, u32[]{:S(2)}) collective-permute-start(f32[7,8,4224]{2,1,0:T(8,128)} %pack.1), channel_id=1, source_target_pairs={{1,2},{2,1},{3,4},{4,3},{5,6},{6,5},{7,8},{8,7},{9,10},{10,9},{11,... | collective-permute-start | bytes 2838536 | tf_op jit(solution)/shard_map/ppermute | solution.py:388
  6.6 12.4 %collective-permute-start = (f32[7,8,4224]{2,1,0:T(8,128)}, f32[7,8,4224]{2,1,0:T(8,128)S(1)}, u32[]{:S(2)}, u32[]{:S(2)}) collective-permute-start(f32[7,8,4224]{2,1,0:T(8,128)} %pack.1), channel_id=1, source_target_pairs={{0,1},{1,0},{2,3},{3,2},{4,5},{5,4},{6,7},{7,6},{8,9},{9,8},{10,11... | collective-permute-start | bytes 2838536 | tf_op jit(solution)/shard_map/ppermute | solution.py:388
  19.0 0.0 copy-start.10
  19.0 0.0 copy-start.11
  19.0 0.0 copy-start.12
  19.0 0.0 copy-done.3
  19.0 0.0 copy-done.4
  19.1 0.0 copy-done.8
  19.1 0.0 copy-done.9
  19.1 0.0 copy-done.7
  19.1 0.6 %copy-done.10 = f32[4]{0:T(128)S(1)} copy-done((f32[4]{0:T(128)S(1)}, f32[4]{0:T(128)}, u32[]{:S(2)}) %copy-start.10) | copy-done | bytes 40
  19.7 0.0 copy-done.11
  19.7 0.0 copy-done.12
  19.7 0.0 copy-start.6
  19.7 2.6 %prepare.1 = (f32[384,128]{1,0:T(8,128)S(1)}, s32[128,128]{1,0:T(8,128)S(1)}, s32[8,128]{1,0:T(8,128)S(1)}, f32[8,128]{1,0:T(8,128)S(1)}, f32[544,128]{1,0:T(8,128)S(1)}) custom-call(f32[3,2048]{1,0:T(4,128)S(1)} %copy-done.3, s32[8,2048]{1,0:T(8,128)S(1)} %copy-done.4, s32[4,256]{1,0:T(4,128)S(1)} %bitcast.7, f32[4,256]{1,0:T(4,128)S(1)} %bitcast.8, ...), custom_call_target="tpu_custom_call" | custom-call | flops 1000000 | bytes 4000000 | tf_op jit(solution)/shard_map/prepare/pallas_call | solution.py:401
  22.3 0.0 copy-start.5
  22.3 0.0 collective-permute-done.1.got_b
  22.3 0.0 collective-permute-done.got_a
  22.3 0.0 copy-done.1
  22.3 0.0 copy-done.6
  22.3 0.6 %copy-done.5 = s32[2048]{0:T(1024)S(1)} copy-done((s32[2048]{0:T(1024)S(1)}, s32[2048]{0:T(1024)}, u32[]{:S(2)}) %copy-start.5) | copy-done | bytes 8216
  23.0 0.0 copy-start
  23.0 0.0 copy-start.2
  23.0 3.2 %hexes.1 = (f32[12,6,2048]{2,1,0:T(8,128)}, f32[3,2048]{1,0:T(4,128)S(1)}, f32[3,256]{1,0:T(4,128)S(1)}, f32[1,256]{1,0:T(1,128)S(1)}) custom-call(f32[7,8,4224]{2,1,0:T(8,128)S(1)} %collective-permute-done.got_a, f32[7,8,4224]{2,1,0:T(8,128)S(1)} %collective-permute-done.1.got_b, f32[384,128]{1,0:T(8,128)S(1)} %get-tuple-element.14.corners, ...), custom_call_target="tpu_custom_call" | custom-call | flops 1000000 | bytes 4000000 | tf_op jit(solution)/shard_map/hexes/pallas_call | solution.py:410
  26.2 0.0 copy-done
  26.2 0.0 copy-done.2
  26.2 7.5 %skull.1 = (f32[6,8,4096]{2,1,0:T(8,128)}, f32[3,34,128]{2,1,0:T(8,128)S(1)}) custom-call(f32[6,8,4096]{2,1,0:T(8,128)S(1)} %copy-done, f32[8,4096]{1,0:T(8,128)S(1)} %copy-done.2, f32[7,8,4224]{2,1,0:T(8,128)S(1)} %collective-permute-done.got_a, f32[7,8,4224]{2,1,0:T(8,128)S(1)} %collective-permute-done.1.got_b, f32[3,256]{1,0:T(4,128)S(1)} %get-tuple-element.17.shared), custom_call_target="tpu_custom_call" | custom-call | flops 1000000 | bytes 4000000 | tf_op jit(solution)/shard_map/skull/pallas_call | solution.py:420
  33.8 1.9 %collective-permute-start.3 = (f32[3,34,128]{2,1,0:T(8,128)S(1)}, f32[3,34,128]{2,1,0:T(8,128)S(1)}, u32[]{:S(2)}, u32[]{:S(2)}) collective-permute-start(f32[3,34,128]{2,1,0:T(8,128)S(1)} %get-tuple-element.19.sent), channel_id=1, source_target_pairs={{1,2},{2,1},{3,4},{4,3},{5,6},{6,5},{7,8},{8,7},{9,10},{10,9},{11,... | collective-permute-start | bytes 156680 | tf_op jit(solution)/shard_map/ppermute | solution.py:388
  35.7 13.6 %collective-permute-start.2 = (f32[3,34,128]{2,1,0:T(8,128)S(1)}, f32[3,34,128]{2,1,0:T(8,128)S(1)}, u32[]{:S(2)}, u32[]{:S(2)}) collective-permute-start(f32[3,34,128]{2,1,0:T(8,128)S(1)} %get-tuple-element.19.sent), channel_id=1, source_target_pairs={{0,1},{1,0},{2,3},{3,2},{4,5},{5,4},{6,7},{7,6},{8,9},{9,8},{10,11... | collective-permute-start | bytes 156680 | tf_op jit(solution)/shard_map/ppermute | solution.py:388
  49.3 0.0 collective-permute-done.3.got_b
  49.3 0.9 %collective-permute-done.2.got_a = f32[3,34,128]{2,1,0:T(8,128)S(1)} collective-permute-done((f32[3,34,128]{2,1,0:T(8,128)S(1)}, f32[3,34,128]{2,1,0:T(8,128)S(1)}, u32[]{:S(2)}, u32[]{:S(2)}) %collective-permute-start.2) | collective-permute-done | bytes 52256 | tf_op jit(solution)/shard_map/ppermute | solution.py:388
  50.1 1.0 %finish.1 = f32[3,2048]{1,0:T(4,128)} custom-call(f32[3,34,128]{2,1,0:T(8,128)S(1)} %get-tuple-element.19.sent, f32[3,34,128]{2,1,0:T(8,128)S(1)} %collective-permute-done.2.got_a, f32[3,34,128]{2,1,0:T(8,128)S(1)} %collective-permute-done.3.got_b, f32[3,2048]{1,0:T(4,128)S(1)} %get-tuple-element.20.base, f32[1,256]{1,0:T(1,128)S(1)} %get-tuple-element.21.scale, ...), custom_call_target="tpu_custom_call" | custom-call | flops 1000000 | bytes 4000000 | tf_op jit(solution)/shard_map/finish/pallas_call | solution.py:428
Async XLA Ops:
  0.6 18.4 %copy-start.3 = (f32[3,2048]{1,0:T(4,128)S(1)}, f32[3,2048]{1,0:T(4,128)}, u32[]{:S(2)}) copy-start(f32[3,2048]{1,0:T(4,128)} %vel.5) | copy-start | bytes 73732
  0.6 18.4 %copy-start.4 = (s32[8,2048]{1,0:T(8,128)S(1)}, s32[8,2048]{1,0:T(8,128)}, u32[]{:S(2)}) copy-start(s32[8,2048]{1,0:T(8,128)} %conn.1) | copy-start | bytes 196612
  0.7 21.7 %copy-start.1 = (f32[12,6,2048]{2,1,0:T(8,128)S(1)}, f32[12,6,2048]{2,1,0:T(8,128)}, u32[]{:S(2)}) copy-start(f32[12,6,2048]{2,1,0:T(8,128)} %memory_in.1) | copy-start | bytes 1769476
  0.7 18.4 %copy-start.8 = (f32[256,4]{0,1:T(4,128)S(1)}, f32[256,4]{0,1:T(4,128)}, u32[]{:S(2)}) copy-start(f32[256,4]{0,1:T(4,128)} %param.16) | copy-start | bytes 12292
  0.7 18.4 %copy-start.9 = (f32[12,4]{0,1:T(4,128)S(1)}, f32[12,4]{0,1:T(4,128)}, u32[]{:S(2)}) copy-start(f32[12,4]{0,1:T(4,128)} %param.22) | copy-start | bytes 580
  2.8 16.2 %copy-start.7 = (s32[256,4]{0,1:T(4,128)S(1)}, s32[256,4]{0,1:T(4,128)}, u32[]{:S(2)}) copy-start(s32[256,4]{0,1:T(4,128)} %param.15) | copy-start | bytes 12292
  2.8 19.5 %collective-permute-start.1 = (f32[7,8,4224]{2,1,0:T(8,128)}, f32[7,8,4224]{2,1,0:T(8,128)S(1)}, u32[]{:S(2)}, u32[]{:S(2)}) collective-permute-start(f32[7,8,4224]{2,1,0:T(8,128)} %pack.1), channel_id=1, source_target_pairs={{1,2},{2,1},{3,4},{4,3},{5,6},{6,5},{7,8},{8,7},{9,10},{10,9},{11,... | collective-permute-start | bytes 2838536 | tf_op jit(solution)/shard_map/ppermute | solution.py:388
  6.6 15.7 %collective-permute-start = (f32[7,8,4224]{2,1,0:T(8,128)}, f32[7,8,4224]{2,1,0:T(8,128)S(1)}, u32[]{:S(2)}, u32[]{:S(2)}) collective-permute-start(f32[7,8,4224]{2,1,0:T(8,128)} %pack.1), channel_id=1, source_target_pairs={{0,1},{1,0},{2,3},{3,2},{4,5},{5,4},{6,7},{7,6},{8,9},{9,8},{10,11... | collective-permute-start | bytes 2838536 | tf_op jit(solution)/shard_map/ppermute | solution.py:388
  19.0 0.7 %copy-start.10 = (f32[4]{0:T(128)S(1)}, f32[4]{0:T(128)}, u32[]{:S(2)}) copy-start(f32[4]{0:T(128)} %shear.1) | copy-start | bytes 52
  19.0 0.7 %copy-start.11 = (f32[4]{0:T(128)S(1)}, f32[4]{0:T(128)}, u32[]{:S(2)}) copy-start(f32[4]{0:T(128)} %bulk.1) | copy-start | bytes 52
  19.0 0.7 %copy-start.12 = (f32[12]{0:T(128)S(1)}, f32[12]{0:T(128)}, u32[]{:S(2)}) copy-start(f32[12]{0:T(128)} %tau.1) | copy-start | bytes 148
  19.7 2.6 %copy-start.6 = (f32[2048]{0:T(1024)S(1)}, f32[2048]{0:T(1024)}, u32[]{:S(2)}) copy-start(f32[2048]{0:T(1024)} %param.25) | copy-start | bytes 24580
  22.3 0.7 %copy-start.5 = (s32[2048]{0:T(1024)S(1)}, s32[2048]{0:T(1024)}, u32[]{:S(2)}) copy-start(s32[2048]{0:T(1024)} %param.19) | copy-start | bytes 24580
  23.0 3.2 %copy-start = (f32[6,8,4096]{2,1,0:T(8,128)S(1)}, f32[6,8,4096]{2,1,0:T(8,128)}, u32[]{:S(2)}) copy-start(f32[6,8,4096]{2,1,0:T(8,128)} %state.3) | copy-start | bytes 2359300
  23.0 3.2 %copy-start.2 = (f32[8,4096]{1,0:T(8,128)S(1)}, f32[8,4096]{1,0:T(8,128)}, u32[]{:S(2)}) copy-start(f32[8,4096]{1,0:T(8,128)} %stiff.3) | copy-start | bytes 393220
  33.8 15.5 %collective-permute-start.3 = (f32[3,34,128]{2,1,0:T(8,128)S(1)}, f32[3,34,128]{2,1,0:T(8,128)S(1)}, u32[]{:S(2)}, u32[]{:S(2)}) collective-permute-start(f32[3,34,128]{2,1,0:T(8,128)S(1)} %get-tuple-element.19.sent), channel_id=1, source_target_pairs={{1,2},{2,1},{3,4},{4,3},{5,6},{6,5},{7,8},{8,7},{9,10},{10,9},{11,... | collective-permute-start | bytes 156680 | tf_op jit(solution)/shard_map/ppermute | solution.py:388
  35.7 14.5 %collective-permute-start.2 = (f32[3,34,128]{2,1,0:T(8,128)S(1)}, f32[3,34,128]{2,1,0:T(8,128)S(1)}, u32[]{:S(2)}, u32[]{:S(2)}) collective-permute-start(f32[3,34,128]{2,1,0:T(8,128)S(1)} %get-tuple-element.19.sent), channel_id=1, source_target_pairs={{0,1},{1,0},{2,3},{3,2},{4,5},{5,4},{6,7},{7,6},{8,9},{9,8},{10,11... | collective-permute-start | bytes 156680 | tf_op jit(solution)/shard_map/ppermute | solution.py:388
